TPU v7x, 128 devices: a whole 4x4x4 slice. The times are simulated.
128 devices in a mesh: section: 2 (over core), seq: 16 (over y, x), wshard: 4 (over z).
Axes of the slice: x: 4, y: 4, z: 4, core: 2. Of those that a mesh axis runs over, the one named last changes fastest.
Arguments:
- block_input: bfloat16 [2, 4, 1024, 1024], P(None, 'wshard', 'seq'), may hold values from -6 to 6
- doc_ids: int32 [2, 4, 1024], P(None, 'wshard'), may hold values from 0 to 3, never falling along the last dimension, each value on 1 to 961 neighbouring positions
- out_grad: bfloat16 [2, 4, 1024, 1024], P(None, 'wshard', 'seq'), may hold values from -6 to 6
- in_proj: bfloat16 [2, 1024, 4384], P('section', 'wshard'), may hold values from -0.1875 to 0.1875
- out_proj: bfloat16 [2, 2048, 1024], P('section', 'wshard'), may hold values from -0.125 to 0.125
- conv_weight: float32 [2, 4, 2304], P('section'), may hold values from -3 to 3
- conv_bias: float32 [2, 2304], P('section'), may hold values from -3 to 3
- dt_bias: float32 [2, 32], P('section'), may hold values from -6.9 to -2.3
- a_log: float32 [2, 32], P('section'), may hold values from 0 to 2.77
- skip_scale: float32 [2, 32], P('section'), may hold values from 0.5 to 1.5
- pre_gain: float32 [2, 1024], P('section'), may hold values from 0.5 to 1.5
- norm_gain: float32 [2, 2048], P('section'), may hold values from 0.5 to 1.5
Outputs:
- hidden: float32 [2, 2, 4, 1024, 1024], P('section', None, 'wshard', 'seq')
- input_grads: float32 [2, 2, 4, 1024, 1024], P('section', None, 'wshard', 'seq')
- grad_in_proj: float32 [2, 1024, 4384], P('section', 'wshard')
- grad_out_proj: float32 [2, 2048, 1024], P('section', 'wshard')
- grad_conv_weight: float32 [2, 4, 2304], P('section')
- grad_conv_bias: float32 [2, 2304], P('section')
- grad_dt_bias: float32 [2, 32], P('section')
- grad_a_log: float32 [2, 32], P('section')
- grad_skip_scale: float32 [2, 32], P('section')
- grad_pre_gain: float32 [2, 1024], P('section')
- grad_norm_gain: float32 [2, 2048], P('section')
Inputs may be any that keep to these rules, and one draw needn't show every extreme that they name: `doc_ids`: within a sequence the document numbers never fall, and one document covers all positions but fewer than 64.
All inputs are finite; a program needn't handle non-finite values.
Results may differ from a plain program's by a relative error of at most 0.02.
Values may be sent and summed in bfloat16 or wider, within the bound.
A program may use at most 256 MiB of HBM per device.

v0:
```python
from functools import partial

import jax
import jax.numpy as jnp
from jax import lax
from jax.sharding import PartitionSpec as P

SPAN = 256


epsilon = 1e-05
exact_matmul_accuracy = lax.Precision.HIGHEST


def gather_turned(arrays, axis, dims):
    turned = [jnp.moveaxis(a, dim, 0) for a, dim in zip(arrays, dims)]
    widths = [t[0].size for t in turned]
    both = jnp.concatenate([t.reshape(-1, w) for t, w in zip(turned, widths)], axis=1)
    whole = lax.all_gather(both, axis, axis=0, tiled=True)
    blocks = jnp.split(whole, [sum(widths[:k]) for k in range(1, len(widths))], axis=1)
    return tuple(
        (
            jnp.moveaxis(b.reshape(-1, *t.shape[1:]), 0, dim)
            for b, t, dim in zip(blocks, turned, dims)
        )
    )


def in_blocks(x, dim, devices):
    before, after = (x.shape[:dim], x.shape[dim + 1 :])
    return jnp.moveaxis(x.reshape(*before, devices, -1, *after), dim, 0)


def sent_and_summed(x, axis, dim):
    blocks = in_blocks(x, dim, lax.axis_size(axis))
    arrived = lax.all_to_all(blocks, axis, split_axis=0, concat_axis=0, tiled=True)
    return arrived.astype(jnp.float32).sum(axis=0)


def shifted(block, axis, distance):
    devices = range(lax.axis_size(axis))
    route = [(i - distance, i) for i in devices if i - distance in devices]
    return lax.ppermute(block, axis, route)


def in_one(arrays, axis):
    ends = [0]
    for a in arrays:
        ends.append(ends[-1] + a.size)
    so_far = lax.psum(jnp.concatenate([a.ravel() for a in arrays]), axis)
    return tuple((so_far[b:e].reshape(a.shape) for a, b, e in zip(arrays, ends, ends[1:])))


def copy_for_each(x, axis):
    copies = jnp.broadcast_to(x, (lax.axis_size(axis), *x.shape))
    return lax.all_to_all(copies, axis, split_axis=0, concat_axis=0, tiled=True)


def of_everyone(x, axis):
    return copy_for_each(x, axis).sum(axis=0)


def together(arrays, axis):
    flat, at, gathered = (jnp.concatenate([a.reshape(-1) for a in arrays]), 0, [])
    so_far = of_everyone(flat, axis)
    for a in arrays:
        gathered.append(so_far[at : at + a.size].reshape(a.shape))
        at += a.size
    return tuple(gathered)


def rms_scale(values, gain):
    return values * lax.rsqrt(jnp.mean(values * values, axis=-1, keepdims=True) + epsilon) * gain


def gate_norm(mixed, gate_part, norm_scale):
    return rms_scale(mixed * jax.nn.silu(gate_part), norm_scale)


def conv_segment(signal, doc_row, kernel, offset):
    tap_count = kernel.shape[0]
    length = signal.shape[0]
    padded = jnp.pad(signal, ((tap_count - 1, 0), (0, 0)))
    doc_padded = jnp.pad(doc_row, (tap_count - 1, 0), constant_values=-1)
    summed = jnp.zeros_like(signal) + offset
    for tap_index in range(tap_count):
        matching_document_mask = (doc_padded[tap_index : tap_index + length] == doc_row)[:, None]
        summed = summed + jnp.where(
            matching_document_mask, padded[tap_index : tap_index + length] * kernel[tap_index], 0.0
        )
    return jax.nn.silu(summed)


def span_update(carried, block_data):
    scaled_x, b_rows, c_rows, log_decay, doc_block, prev_doc = block_data
    block_len = doc_block.shape[0]
    running = jnp.cumsum(log_decay, axis=0)
    positions = jnp.arange(block_len)
    causal = (positions[:, None] >= positions[None, :]) & (doc_block[:, None] == doc_block[None, :])
    gaps = running.T[:, :, None] - running.T[:, None, :]
    decay_matrix = jnp.exp(jnp.where(causal[None], gaps, -1e30))
    scores = jnp.dot(c_rows, b_rows.T, precision=exact_matmul_accuracy)
    within = jnp.einsum(
        "hij,jhp->ihp", scores[None] * decay_matrix, scaled_x, precision=exact_matmul_accuracy
    )
    keep_row = (doc_block == prev_doc).astype(jnp.float32)
    reach_row = jnp.exp(running) * keep_row[:, None]
    across = (
        jnp.einsum("in,hnp->ihp", c_rows, carried, precision=exact_matmul_accuracy)
        * reach_row[:, :, None]
    )
    block_total = running[-1]
    tail_weight = (
        jnp.exp(block_total[None, :] - running)
        * (doc_block == doc_block[-1]).astype(jnp.float32)[:, None]
    )
    carry_factor = jnp.exp(block_total) * (doc_block[-1] == prev_doc).astype(jnp.float32)
    updated = carried * carry_factor[:, None, None] + jnp.einsum(
        "jn,jhp->hnp", b_rows, scaled_x * tail_weight[:, :, None], precision=exact_matmul_accuracy
    )
    return (updated, within + across)


def mixing(
    x_head,
    bc_rows,
    dt_raw,
    doc_row,
    conv_x,
    bias_x,
    conv_bc,
    bias_bc,
    dt_shift,
    decay_log,
    skip_part,
):
    length, channels = x_head.shape
    head_count = dt_raw.shape[1]
    attention_head_breadth = channels // head_count
    state_size = bc_rows.shape[1] // 2
    conv_out = conv_segment(x_head, doc_row, conv_x, bias_x)
    bc_conv = conv_segment(bc_rows, doc_row, conv_bc, bias_bc)
    step_size = jax.nn.softplus(dt_raw + dt_shift)
    log_decay = -step_size * jnp.exp(decay_log)
    heads_x = conv_out.reshape(length, head_count, attention_head_breadth)
    scaled_x = heads_x * step_size[:, :, None]
    block_count = length // SPAN
    doc_blocks = doc_row.reshape(block_count, SPAN)
    prev_docs = jnp.concatenate([doc_row[:1], doc_blocks[:-1, -1]])
    inputs = (
        scaled_x.reshape(block_count, SPAN, head_count, attention_head_breadth),
        bc_conv[:, :state_size].reshape(block_count, SPAN, state_size),
        bc_conv[:, state_size:].reshape(block_count, SPAN, state_size),
        log_decay.reshape(block_count, SPAN, head_count),
        doc_blocks,
        prev_docs,
    )
    start_state = jnp.zeros((head_count, state_size, attention_head_breadth), jnp.float32)
    unused, outputs = lax.scan(jax.checkpoint(span_update), start_state, inputs)
    mixed = (
        outputs.reshape(length, head_count, attention_head_breadth)
        + heads_x * skip_part[None, :, None]
    )
    return mixed.reshape(length, channels)


def head_part(
    x_head,
    bc_rows,
    dt_rows,
    conv_weight,
    conv_bias,
    dt_bias,
    a_log,
    skip_scale,
    doc_row,
    first_head,
):
    channels = x_head.shape[1]
    head_total = dt_rows.shape[0]
    inner_width = conv_weight.shape[1] - bc_rows.shape[1]
    attention_head_breadth = inner_width // head_total
    head_count = channels // attention_head_breadth
    first_channel = first_head * attention_head_breadth
    conv_x = lax.dynamic_slice_in_dim(conv_weight, first_channel, channels, 1)
    bias_x = lax.dynamic_slice_in_dim(conv_bias, first_channel, channels, 0)
    own_dt = lax.dynamic_slice_in_dim(dt_rows, first_head, head_count, 0).T
    own_shift = lax.dynamic_slice_in_dim(dt_bias, first_head, head_count, 0)
    own_decay = lax.dynamic_slice_in_dim(a_log, first_head, head_count, 0)
    own_skip = lax.dynamic_slice_in_dim(skip_scale, first_head, head_count, 0)
    return mixing(
        x_head,
        bc_rows,
        own_dt,
        doc_row,
        conv_x,
        bias_x,
        conv_weight[:, inner_width:],
        conv_bias[inner_width:],
        own_shift,
        own_decay,
        own_skip,
    )


def store_slot(buffer, value, micro_slot, is_active):
    return jnp.where(
        is_active, lax.dynamic_update_index_in_dim(buffer, value, micro_slot, 0), buffer
    )


def body(
    block_input,
    doc_ids,
    out_grad,
    in_proj,
    out_proj,
    conv_weight,
    conv_bias,
    dt_bias,
    a_log,
    skip_scale,
    pre_gain,
    norm_gain,
):
    section_index = lax.axis_index("section")
    section_count = lax.axis_size("section")
    seq_index = lax.axis_index("seq")
    micro_count = block_input.shape[0]
    token_rows = block_input.shape[2]
    model_width = block_input.shape[3]
    in_full, out_full = (
        lax.all_gather(in_proj[0], "wshard", axis=0, tiled=True),
        lax.all_gather(out_proj[0], "wshard", axis=0, tiled=True),
    )
    inner_width = out_full.shape[0]
    head_total = dt_bias.shape[1]
    heads_here = head_total // lax.axis_size("seq")
    first_head = seq_index * heads_here
    bc_width = in_full.shape[1] - 2 * inner_width - head_total
    layer_params = (conv_weight[0], conv_bias[0], dt_bias[0], a_log[0], skip_scale[0])
    pre_scale = pre_gain[0]
    norm_scale = norm_gain[0]
    step_total = micro_count + section_count - 1
    hidden_buffer = jnp.zeros((micro_count, token_rows, model_width), jnp.float32)
    input_buffer = jnp.zeros((micro_count, token_rows, model_width), jnp.float32)
    kept_buffer = ()
    arriving = jnp.zeros((token_rows, model_width), jnp.float32)
    for clock_step in range(step_total):
        offset_micro = clock_step - section_index
        is_active = (offset_micro >= 0) & (offset_micro < micro_count)
        micro_slot = jnp.clip(offset_micro, 0, micro_count - 1)
        fresh_input = block_input[min(clock_step, micro_count - 1), 0].astype(jnp.float32)
        layer_in = jnp.where(section_index == 0, fresh_input, arriving)
        doc_row = lax.dynamic_index_in_dim(doc_ids[:, 0], micro_slot, 0, keepdims=False)
        forward_normalized_rows = rms_scale(layer_in, pre_scale).astype(jnp.bfloat16)
        projected_rows = jnp.dot(
            forward_normalized_rows, in_full, preferred_element_type=jnp.float32
        )
        forward_gate_part = projected_rows[:, :inner_width]
        x_tokens = projected_rows[:, inner_width : 2 * inner_width].astype(jnp.bfloat16)
        bc_tokens = projected_rows[:, 2 * inner_width : 2 * inner_width + bc_width].astype(
            jnp.bfloat16
        )
        dt_tokens = projected_rows[:, 2 * inner_width + bc_width :].T.astype(jnp.bfloat16)
        forward_x_heads = lax.all_to_all(x_tokens, "seq", split_axis=1, concat_axis=0, tiled=True)
        forward_bc_rows, forward_dt_rows = gather_turned((bc_tokens, dt_tokens), "seq", (0, 1))
        mixed = head_part(
            forward_x_heads.astype(jnp.float32),
            forward_bc_rows.astype(jnp.float32),
            forward_dt_rows.astype(jnp.float32),
            layer_params[0],
            layer_params[1],
            layer_params[2],
            layer_params[3],
            layer_params[4],
            doc_row,
            first_head,
        )
        forward_mixed_tokens = lax.all_to_all(
            mixed.astype(jnp.bfloat16), "seq", split_axis=0, concat_axis=1, tiled=True
        )
        forward_rescaled_result_vector = gate_norm(
            forward_mixed_tokens.astype(jnp.float32), forward_gate_part, norm_scale
        ).astype(jnp.bfloat16)
        auxiliary_residual_path = jnp.dot(
            forward_rescaled_result_vector, out_full, preferred_element_type=jnp.float32
        )
        layer_out = layer_in + auxiliary_residual_path
        kept = (
            forward_gate_part,
            forward_x_heads,
            forward_bc_rows,
            forward_dt_rows,
            forward_mixed_tokens,
        )
        if clock_step == 0:
            kept_buffer = tuple(
                (
                    jnp.zeros((micro_count,) + kept_piece.shape, kept_piece.dtype)
                    for kept_piece in kept
                )
            )
        kept_buffer = tuple(
            (
                store_slot(buffer, kept_piece, micro_slot, is_active)
                for buffer, kept_piece in zip(kept_buffer, kept)
            )
        )
        hidden_buffer = store_slot(hidden_buffer, layer_out, micro_slot, is_active)
        input_buffer = store_slot(input_buffer, layer_in, micro_slot, is_active)
        arriving = shifted(layer_out, "section", 1)
    grad_buffer = jnp.zeros((micro_count, token_rows, model_width), jnp.float32)
    returning = jnp.zeros((token_rows, model_width), jnp.float32)
    totals = ()
    for clock_step in range(step_total):
        offset_micro = clock_step - (section_count - 1 - section_index)
        is_active = (offset_micro >= 0) & (offset_micro < micro_count)
        micro_slot = jnp.clip(offset_micro, 0, micro_count - 1)
        own_grad = out_grad[min(clock_step, micro_count - 1), 0].astype(jnp.float32)
        grad_here = jnp.where(section_index == section_count - 1, own_grad, returning)
        doc_row = lax.dynamic_index_in_dim(doc_ids[:, 0], micro_slot, 0, keepdims=False)
        layer_in = lax.dynamic_index_in_dim(input_buffer, micro_slot, 0, keepdims=False)
        kept = tuple(
            (
                lax.dynamic_index_in_dim(buffer, micro_slot, 0, keepdims=False)
                for buffer in kept_buffer
            )
        )
        gate_part, x_heads, bc_rows, dt_rows, mixed_tokens = kept
        normalized_rows, pre_pull = jax.vjp(rms_scale, layer_in, pre_scale)
        normed_low = normalized_rows.astype(jnp.bfloat16)
        rescaled_result_vector, norm_pull = jax.vjp(
            gate_norm, mixed_tokens.astype(jnp.float32), gate_part, norm_scale
        )
        grad_low = grad_here.astype(jnp.bfloat16)
        grad_outproj = jnp.einsum(
            "tk,td->kd",
            rescaled_result_vector.astype(jnp.bfloat16),
            grad_low,
            preferred_element_type=jnp.float32,
        )
        grad_normed_out = jnp.einsum(
            "td,kd->tk", grad_low, out_full, preferred_element_type=jnp.float32
        )
        grad_mixed, grad_gate, grad_norm_gain = norm_pull(grad_normed_out)
        grad_heads = lax.all_to_all(
            grad_mixed.astype(jnp.bfloat16), "seq", split_axis=1, concat_axis=0, tiled=True
        )
        local_part = partial(head_part, doc_row=doc_row, first_head=first_head)
        unused, head_pull = jax.vjp(
            local_part,
            x_heads.astype(jnp.float32),
            bc_rows.astype(jnp.float32),
            dt_rows.astype(jnp.float32),
            layer_params[0],
            layer_params[1],
            layer_params[2],
            layer_params[3],
            layer_params[4],
        )
        (
            grad_x,
            grad_bc,
            grad_dt,
            grad_conv_w,
            grad_conv_b,
            grad_shift,
            grad_decay,
            derivative_of_bypass_scale,
        ) = head_pull(grad_heads.astype(jnp.float32))
        grad_x_tokens = lax.all_to_all(
            grad_x.astype(jnp.bfloat16), "seq", split_axis=0, concat_axis=1, tiled=True
        )
        grad_bc_own = sent_and_summed(grad_bc.astype(jnp.bfloat16), "seq", 0)
        grad_dt_own = sent_and_summed(grad_dt.astype(jnp.bfloat16), "seq", 1)
        grad_proj = jnp.concatenate(
            [
                grad_gate.astype(jnp.bfloat16),
                grad_x_tokens,
                grad_bc_own.astype(jnp.bfloat16),
                grad_dt_own.T.astype(jnp.bfloat16),
            ],
            axis=1,
        )
        grad_inproj = jnp.einsum(
            "tk,tp->kp", normed_low, grad_proj, preferred_element_type=jnp.float32
        )
        grad_normed = jnp.einsum(
            "tp,kp->tk", grad_proj, in_full, preferred_element_type=jnp.float32
        )
        grad_path, grad_pre_gain = pre_pull(grad_normed)
        grad_in = grad_here + grad_path
        grads = (
            grad_inproj,
            grad_outproj,
            grad_conv_w,
            grad_conv_b,
            grad_shift,
            grad_decay,
            derivative_of_bypass_scale,
            grad_pre_gain,
            grad_norm_gain,
        )
        active_weight = is_active.astype(jnp.float32)
        masked = tuple((grad_piece * active_weight for grad_piece in grads))
        if clock_step == 0:
            totals = masked
        else:
            totals = tuple(
                (total_piece + grad_piece for total_piece, grad_piece in zip(totals, masked))
            )
        grad_buffer = store_slot(grad_buffer, grad_in, micro_slot, is_active)
        returning = shifted(grad_in.astype(jnp.bfloat16), "section", -1).astype(grad_in.dtype)
    rows_in, rows_out = (
        lax.psum_scatter(
            totals[0].astype(jnp.bfloat16), "wshard", scatter_dimension=0, tiled=True
        ).astype(jnp.float32),
        lax.psum_scatter(
            totals[1].astype(jnp.bfloat16), "wshard", scatter_dimension=0, tiled=True
        ).astype(jnp.float32),
    )
    shard_in, shard_out = tuple(
        (
            part.astype(jnp.float32)
            for part in in_one((rows_in.astype(jnp.bfloat16), rows_out.astype(jnp.bfloat16)), "seq")
        )
    )
    small_sums = together(
        (totals[2], totals[3], totals[4], totals[5], totals[6], totals[7], totals[8]),
        ("seq", "wshard"),
    )
    return (
        hidden_buffer[None, :, None],
        grad_buffer[None, :, None],
        shard_in[None],
        shard_out[None],
        small_sums[0][None],
        small_sums[1][None],
        small_sums[2][None],
        small_sums[3][None],
        small_sums[4][None],
        small_sums[5][None],
        small_sums[6][None],
    )


def solution(mesh):
    return jax.shard_map(
        body,
        mesh=mesh,
        in_specs=(
            P(None, "wshard", "seq", None),
            P(None, "wshard", None),
            P(None, "wshard", "seq", None),
            P("section", "wshard", None),
            P("section", "wshard", None),
            P("section", None, None),
            P("section", None),
            P("section", None),
            P("section", None),
            P("section", None),
            P("section", None),
            P("section", None),
        ),
        out_specs=(
            P("section", None, "wshard", "seq", None),
            P("section", None, "wshard", "seq", None),
            P("section", "wshard", None),
            P("section", "wshard", None),
            P("section", None, None),
            P("section", None),
            P("section", None),
            P("section", None),
            P("section", None),
            P("section", None),
            P("section", None),
        ),
        check_vma=False,
    )
```

profile of v0, /device:TPU:0, one launch (start us, length us, event | category | flops | bytes accessed | tf_op | source)
XLA Modules:
  0.0 1614.1 jit_solution(2404904498810294411)
XLA Ops:
  30.7 74.2 %all-gather.5.cloned.1.call-done = bf16[1,1024,4384]{1,2,0:T(8,128)(2,1)} async-done(((bf16[1,256,4384]{1,2,0:T(8,128)(2,1)}), bf16[1,1024,4384]{1,2,0:T(8,128)(2,1)}) %all-gather.5.cloned.1.call-update) | async-done | bytes 8978448 | tf_op jit(solution)/shard_map/all_gather | solution.py:233
  104.9 7.4 fusion.548
  113.1 24.4 %all_gather.16 = bf16[1024,288]{1,0:T(8,128)(2,1)S(1)} all-gather(bf16[64,288]{1,0:T(8,128)(2,1)S(1)} %slice.920), channel_id=1, replica_groups=mesh['section'=2,'seq'=16,'wshard'=4] {'seq'}, dimensions={0}, use_global_device_ids=true | all-gather | bytes 626688 | tf_op jit(solution)/shard_map/all_gather | solution.py:19
  138.4 4.9 all-to-all-start
  146.8 5.2 all-to-all-done
  163.1 42.9 %while.147 = (s32[]{:T(128)}, f32[2,128,64]{1,2,0:T(8,128)}, f32[4,256,2,64]{1,3,2,0:T(8,128)}, f32[4,256,2]{1,2,0:T(2,128)}, s32[4,256]{1,0:T(4,128)S(1)}, /*in...) while((s32[]{:T(128)}, f32[2,128,64]{1,2,0:T(8,128)}, ...), condition=%wide.region_4.5_spmd.clone, body=%wide.region_1.4_spmd.clone.sunk | while | flops 302795264 | bytes 2469741 | solution.py:159
  217.1 7.4 all-to-all-done.1
  241.8 7.4 fusion.549
  250.1 23.2 %all_gather.18 = bf16[1024,288]{1,0:T(8,128)(2,1)S(1)} all-gather(bf16[64,288]{1,0:T(8,128)(2,1)S(1)} %slice.930), channel_id=1, replica_groups=mesh['section'=2,'seq'=16,'wshard'=4] {'seq'}, dimensions={0}, use_global_device_ids=true | all-gather | bytes 626688 | tf_op jit(solution)/shard_map/all_gather | solution.py:19
  298.7 62.1 %while.148 = (s32[]{:T(128)}, f32[2,128,64]{1,2,0:T(8,128)}, f32[4,256,2,64]{1,3,2,0:T(8,128)}, f32[4,256,2]{1,2,0:T(2,128)}, s32[4,256]{1,0:T(4,128)}, /*index=...) while((s32[]{:T(128)}, f32[2,128,64]{1,2,0:T(8,128)}, ...), condition=%wide.region_10.11_spmd.clone, body=%wide.region_7.10_spmd.clone.sunk | while | flops 302795264 | bytes 2469237 | solution.py:159
  369.2 6.6 all-to-all-start.3
  377.7 6.9 all-to-all-done.3
  397.8 7.4 fusion.550
  406.0 22.3 %all_gather.19 = bf16[1024,288]{1,0:T(8,128)(2,1)S(1)} all-gather(bf16[64,288]{1,0:T(8,128)(2,1)S(1)} %slice.936), channel_id=1, replica_groups=mesh['section'=2,'seq'=16,'wshard'=4] {'seq'}, dimensions={0}, use_global_device_ids=true | all-gather | bytes 626688 | tf_op jit(solution)/shard_map/all_gather | solution.py:19
  471.6 56.7 %while.149 = (s32[]{:T(128)}, f32[2,128,64]{1,2,0:T(8,128)S(1)}, f32[4,256,2,64]{1,3,2,0:T(8,128)}, f32[4,256,2]{1,2,0:T(2,128)}, s32[4,256]{1,0:T(4,128)}, /*in...) while((s32[]{:T(128)}, f32[2,128,64]{1,2,0:T(8,128)S(1)}, ...), condition=%wide.region_16.17_spmd.clone, body=%wide.region_13.16_spmd.clone.sunk | while | flops 302795264 | bytes 2469237 | solution.py:159
  536.4 7.4 all-to-all-start.5
  558.1 5.7 multiply_reduce_fusion.41
  570.6 5.7 fusion.368
  595.5 35.9 %while.150 = (s32[]{:T(128)}, f32[2,128,64]{1,2,0:T(8,128)S(1)}, f32[4,2,128,64]{2,3,1,0:T(8,128)}, f32[4,256,2]{1,2,0:T(2,128)}, s32[4,256]{1,0:T(4,128)}, /*in...) while((s32[]{:T(128)}, f32[2,128,64]{1,2,0:T(8,128)S(1)}, ...), condition=%wide.region_23.25_spmd.clone, body=%wide.region_20.24_spmd.clone.sunk | while | flops 50497036 | bytes 555869 | solution.py:159
  634.5 124.9 %while.151 = (s32[]{:T(128)}, f32[2,128,64]{1,2,0:T(8,128)}, f32[4,256,2,64]{1,3,2,0:T(8,128)}, f32[4,256,128]{2,1,0:T(8,128)}, f32[4,256,128]{2,1,0:T(8,128)}, ...) while((s32[]{:T(128)}, f32[2,128,64]{1,2,0:T(8,128)}, ...), condition=%wide.region_36.38_spmd.clone, body=%wide.region_24.37_spmd.clone.sunk | while | flops 757258240 | bytes 7914241 | solution.py:159
  782.4 7.3 all-to-all-start.7
  792.8 5.6 all-to-all-done.7
  803.5 9.3 all-to-all-done.8
  814.0 6.2 multiply_reduce_fusion.53
  833.0 9.7 fusion.401
  859.7 36.0 %while.152 = (s32[]{:T(128)}, f32[2,128,64]{1,2,0:T(8,128)S(1)}, f32[4,2,128,64]{2,3,1,0:T(8,128)}, f32[4,256,2]{1,2,0:T(2,128)}, s32[4,256]{1,0:T(4,128)}, /*in...) while((s32[]{:T(128)}, f32[2,128,64]{1,2,0:T(8,128)S(1)}, ...), condition=%wide.region_47.49_spmd.clone, body=%wide.region_44.48_spmd.clone.sunk | while | flops 50497036 | bytes 555869 | solution.py:159
  898.8 123.1 %while.153 = (s32[]{:T(128)}, f32[2,128,64]{1,2,0:T(8,128)}, f32[4,256,2,64]{1,3,2,0:T(8,128)}, f32[4,256,128]{2,1,0:T(8,128)}, f32[4,256,128]{2,1,0:T(8,128)}, ...) while((s32[]{:T(128)}, f32[2,128,64]{1,2,0:T(8,128)}, ...), condition=%wide.region_60.62_spmd.clone, body=%wide.region_48.61_spmd.clone.sunk | while | flops 757258240 | bytes 7914241 | solution.py:159
  1029.0 7.7 all-to-all-start.13
  1048.1 7.3 all-to-all-start.11
  1058.5 5.6 all-to-all-done.11
  1069.4 9.0 all-to-all-done.12
  1079.6 6.1 multiply_reduce_fusion.52
  1088.1 4.6 fusion.367
  1101.4 9.1 add_convert_fusion.1
  1125.8 36.0 %while.154 = (s32[]{:T(128)}, f32[2,128,64]{1,2,0:T(8,128)S(1)}, f32[4,2,128,64]{2,3,1,0:T(8,128)}, f32[4,256,2]{1,2,0:T(2,128)}, s32[4,256]{1,0:T(4,128)}, /*in...) while((s32[]{:T(128)}, f32[2,128,64]{1,2,0:T(8,128)S(1)}, ...), condition=%wide.region_71.73_spmd.clone, body=%wide.region_68.72_spmd.clone.sunk | while | flops 50497036 | bytes 556373 | solution.py:159
  1164.9 114.6 %while.155 = (s32[]{:T(128)}, f32[2,128,64]{1,2,0:T(8,128)}, f32[4,256,2,64]{1,3,2,0:T(8,128)}, f32[4,256,128]{2,1,0:T(8,128)}, f32[4,256,128]{2,1,0:T(8,128)}, ...) while((s32[]{:T(128)}, f32[2,128,64]{1,2,0:T(8,128)}, ...), condition=%wide.region_84.86_spmd.clone, body=%wide.region_72.85_spmd.clone.sunk | while | flops 757258240 | bytes 6865637 | solution.py:159
  1286.7 7.1 all-to-all-start.17
  1304.1 7.4 all-to-all-start.15
  1313.7 6.9 all-to-all-done.15
  1324.3 8.7 fusion.402
  1335.3 17.1 %add_convert_fusion = bf16[1024,4384]{0,1:T(8,128)(2,1)} fusion(f32[1024,4384]{0,1:T(8,128)} %fusion.402, f32[1024,4384]{0,1:T(8,128)} %fusion.401, f32[]{:T(128)S(6)} %convert_element_type.674, f32[]{:T(128)S(6)} %convert_element_type.672, f32[]{:T(128)S(6)} %convert_element_type.670, f32[2,64,1024]{2,1,0:T(8,128)S(1)} %fusion.377, s32[]{:T(128)S(6)} %min.24, ...), kind=kOutput, calls=%fused_computation.435 | convolution fusion | flops 603996160 | bytes 45732368 | tf_op jit(solution)/shard_map/tk,tp->kp/dot_general | solution.py:386
  1356.6 5.4 multiply_reduce_fusion.51
  1366.0 9.2 all-to-all-start.18
  1377.8 101.0 %reduce-scatter.3.cloned.1.call-done = bf16[256,4384]{0,1:T(8,128)(2,1)} async-done(((bf16[1024,4384]{0,1:T(8,128)(2,1)}), bf16[256,4384]{0,1:T(8,128)(2,1)}) %reduce-scatter.3.cloned.1.call-update) | async-done | bytes 2244624 | tf_op jit(solution)/shard_map/reduce_scatter | solution.py:416
  1481.8 5.1 reshape.1921
  1505.2 83.7 %all-reduce.83.cloned.1.call-done = bf16[1646592]{0:T(1024)(128)(2,1)} async-done(((bf16[1646592]{0:T(1024)(128)(2,1)}), bf16[1646592]{0:T(1024)(128)(2,1)}) %all-reduce.83.cloned.1.call-update) | async-done | bytes 3293200 | tf_op jit(solution)/shard_map/psum | solution.py:50
  1595.3 6.2 reshape.1974
  1601.5 5.9 copy.1065
  (1970 shorter events, 980.4 us)
Async XLA Ops:
  7.2 97.7 %copy-start.52 = (f32[1,1024]{1,0:T(1,128)S(1)}, f32[1,1024]{1,0:T(1,128)}, u32[]{:S(2)}) copy-start(f32[1,1024]{1,0:T(1,128)} %param.41) | copy-start | bytes 12292
  7.2 97.6 %all-gather.5.cloned.1.call-start = ((), (), s32[]{:S(2)}) async-start(), calls=%async_computation.24 | async-start | bytes 11223040 | tf_op jit(solution)/shard_map/all_gather | solution.py:233
  8.0 219.5 %all-gather.7.cloned.1.call-start = ((), (), s32[]{:S(2)}) async-start(), calls=%async_computation.25 | async-start | bytes 5242880 | tf_op jit(solution)/shard_map/all_gather | solution.py:234
  9.6 135.9 %copy-start.211 = (f32[1,256]{1,0:T(1,128)}, f32[1,256]{1,0:T(1,128)S(1)}, u32[]{:S(2)}) copy-start(f32[1,256]{1,0:T(1,128)S(1)} %slice.753) | copy-start | bytes 3076
  10.2 143.6 %copy-start.197 = (f32[128]{0:T(128)}, f32[128]{0:T(128)S(1)}, u32[]{:S(2)}) copy-start(f32[128]{0:T(128)S(1)} %fusion.495) | copy-start | bytes 1540
  11.9 142.0 %copy-start.105 = (f32[128]{0:T(128)}, f32[128]{0:T(128)S(1)}, u32[]{:S(2)}) copy-start(f32[128]{0:T(128)S(1)} %get-tuple-element.3021) | copy-start | bytes 1540
  11.9 142.0 %copy-start.112 = (f32[128]{0:T(128)}, f32[128]{0:T(128)S(1)}, u32[]{:S(2)}) copy-start(f32[128]{0:T(128)S(1)} %get-tuple-element.3022) | copy-start | bytes 1540
  11.9 142.0 %copy-start.120 = (f32[128]{0:T(128)}, f32[128]{0:T(128)S(1)}, u32[]{:S(2)}) copy-start(f32[128]{0:T(128)S(1)} %get-tuple-element.3023) | copy-start | bytes 1540
  11.9 142.0 %copy-start.128 = (f32[128]{0:T(128)}, f32[128]{0:T(128)S(1)}, u32[]{:S(2)}) copy-start(f32[128]{0:T(128)S(1)} %get-tuple-element.3024) | copy-start | bytes 1540
  12.8 132.7 %copy-start.136 = (f32[1,256]{1,0:T(1,128)}, f32[1,256]{1,0:T(1,128)S(1)}, u32[]{:S(2)}) copy-start(f32[1,256]{1,0:T(1,128)S(1)} %get-tuple-element.2977) | copy-start | bytes 3076
  12.8 132.7 %copy-start.142 = (f32[1,256]{1,0:T(1,128)}, f32[1,256]{1,0:T(1,128)S(1)}, u32[]{:S(2)}) copy-start(f32[1,256]{1,0:T(1,128)S(1)} %get-tuple-element.2978) | copy-start | bytes 3076
  12.8 132.7 %copy-start.148 = (f32[1,256]{1,0:T(1,128)}, f32[1,256]{1,0:T(1,128)S(1)}, u32[]{:S(2)}) copy-start(f32[1,256]{1,0:T(1,128)S(1)} %get-tuple-element.2979) | copy-start | bytes 3076
  12.8 132.7 %copy-start.154 = (f32[1,256]{1,0:T(1,128)}, f32[1,256]{1,0:T(1,128)S(1)}, u32[]{:S(2)}) copy-start(f32[1,256]{1,0:T(1,128)S(1)} %get-tuple-element.2980) | copy-start | bytes 3076
  18.2 135.7 %copy-start.229 = (pred[1024]{0:T(1024)(128)(4,1)}, pred[1024]{0:T(1024)(128)(4,1)S(1)}, u32[]{:S(2)}) copy-start(pred[1024]{0:T(1024)(128)(4,1)S(1)} %get-tuple-element.3018) | copy-start | bytes 3076
  18.2 135.8 %copy-start.230 = (pred[1024]{0:T(1024)(128)(4,1)}, pred[1024]{0:T(1024)(128)(4,1)S(1)}, u32[]{:S(2)}) copy-start(pred[1024]{0:T(1024)(128)(4,1)S(1)} %get-tuple-element.3019) | copy-start | bytes 3076
  18.2 135.8 %copy-start.231 = (pred[1024]{0:T(1024)(128)(4,1)}, pred[1024]{0:T(1024)(128)(4,1)S(1)}, u32[]{:S(2)}) copy-start(pred[1024]{0:T(1024)(128)(4,1)S(1)} %get-tuple-element.3020) | copy-start | bytes 3076
  22.6 120.9 %copy-start.160 = (f32[2]{0:T(128)}, f32[2]{0:T(128)S(1)}, u32[]{:S(2)}) copy-start(f32[2]{0:T(128)S(1)} %get-tuple-element.3048) | copy-start | bytes 28
  22.6 120.9 %copy-start.214 = (f32[2]{0:T(128)}, f32[2]{0:T(128)S(1)}, u32[]{:S(2)}) copy-start(f32[2]{0:T(128)S(1)} %get-tuple-element.3047) | copy-start | bytes 28
  138.4 13.6 all-to-all-start
  212.4 12.2 all-to-all-start.1
  232.4 9.2 collective-permute-start
  241.6 45.9 %copy-start.50 = (f32[64,1024]{1,0:T(8,128)}, f32[64,1024]{1,0:T(8,128)S(1)}, u32[]{:S(2)}) copy-start(f32[64,1024]{1,0:T(8,128)S(1)} %collective-permute-done) | copy-start | bytes 786436
  249.2 32.3 %copy-start.149 = (f32[1,256]{1,0:T(1,128)S(1)}, f32[1,256]{1,0:T(1,128)}, u32[]{:S(2)}) copy-start(f32[1,256]{1,0:T(1,128)} %copy-done.148) | copy-start | bytes 3076
  249.2 32.3 %copy-start.155 = (f32[1,256]{1,0:T(1,128)S(1)}, f32[1,256]{1,0:T(1,128)}, u32[]{:S(2)}) copy-start(f32[1,256]{1,0:T(1,128)} %copy-done.154) | copy-start | bytes 3076
  275.3 13.2 all-to-all-start.2
  369.2 15.4 all-to-all-start.3
  394.4 3.2 collective-permute-start.1
  397.7 32.5 %copy-start.40 = (f32[64,1024]{1,0:T(8,128)}, f32[64,1024]{1,0:T(8,128)S(1)}, u32[]{:S(2)}) copy-start(f32[64,1024]{1,0:T(8,128)S(1)} %collective-permute-done.1) | copy-start | bytes 786436
  430.9 31.2 %all-to-all-start.4 = ((bf16[64,16,128]{2,0,1:T(8,128)(2,1)}), bf16[64,16,128]{2,0,1:T(8,128)(2,1)S(1)}, u32[]{:S(2)}, u32[]{:S(2)}) async-start(bf16[64,16,128]{2,0,1:T(8,128)(2,1)} %copy_bitcast_fusion.12), calls=%async_computation.4 | async-start | bytes 524288 | tf_op jit(solution)/shard_map/all_to_all | solution.py:266
  536.4 16.1 all-to-all-start.5
  566.6 12.6 all-to-all-start.6
  766.6 15.8 all-to-all-start.9
  782.4 16.0 all-to-all-start.7
  798.4 14.4 all-to-all-start.8
  821.0 3.2 collective-permute-start.2
  829.2 14.0 all-to-all-start.10
  1029.0 19.0 %all-to-all-start.13 = ((bf16[16,2,1024]{2,1,0:T(2,128)(2,1)}), bf16[16,2,1024]{2,1,0:T(2,128)(2,1)S(1)}, u32[]{:S(2)}, u32[]{:S(2)}) async-start(bf16[16,2,1024]{2,1,0:T(2,128)(2,1)} %reshape.2120), calls=%async_computation.13 | async-start | bytes 131072 | tf_op jit(solution)/shard_map/all_to_all | solution.py:36
  1048.1 16.0 all-to-all-start.11
  1064.1 14.3 all-to-all-start.12
  1086.6 6.2 collective-permute-start.3
  1097.6 13.4 all-to-all-start.14
  1101.2 274.1 %reduce-scatter.5.cloned.1.call-start = ((), (), s32[]{:S(2)}) async-start(), calls=%async_computation.22 | async-start | bytes 5242880 | tf_op jit(solution)/shard_map/reduce_scatter | solution.py:419
  1286.7 17.5 %all-to-all-start.17 = ((bf16[16,2,1024]{2,1,0:T(2,128)(2,1)}), bf16[16,2,1024]{2,1,0:T(2,128)(2,1)S(1)}, u32[]{:S(2)}, u32[]{:S(2)}) async-start(bf16[16,2,1024]{2,1,0:T(2,128)(2,1)} %reshape.2122), calls=%async_computation.17 | async-start | bytes 131072 | tf_op jit(solution)/shard_map/all_to_all | solution.py:36
  1304.1 16.5 %all-to-all-start.15 = ((bf16[16,64,128]{2,1,0:T(8,128)(2,1)}), bf16[16,64,128]{2,1,0:T(8,128)(2,1)}, u32[]{:S(2)}, u32[]{:S(2)}) async-start(bf16[16,64,128]{2,1,0:T(8,128)(2,1)} %bitcast.161), calls=%async_computation.15 | async-start | bytes 524288 | tf_op jit(solution)/shard_map/all_to_all | solution.py:372
  1320.6 14.6 all-to-all-start.16
  1324.2 154.6 %reduce-scatter.3.cloned.1.call-start = ((), (), s32[]{:S(2)}) async-start(), calls=%async_computation.21 | async-start | bytes 11223040 | tf_op jit(solution)/shard_map/reduce_scatter | solution.py:416
  1366.0 131.6 %all-to-all-start.18 = ((f32[64,1,14688]{2,1,0:T(1,128)}), f32[64,1,14688]{2,1,0:T(1,128)}, u32[]{:S(2)}, u32[]{:S(2)}) async-start(f32[64,1,14688]{2,1,0:T(1,128)} %broadcast_in_dim.992), calls=%async_computation.20 | async-start | bytes 7536640 | tf_op jit(solution)/shard_map/all_to_all | solution.py:56
  1375.2 213.7 %all-reduce.83.cloned.1.call-start = ((), (), s32[]{:S(2)}) async-start(), calls=%async_computation.23 | async-start | bytes 6586368 | tf_op jit(solution)/shard_map/psum | solution.py:50
  (300 other events, 2347.2 us)
Sparse Core Ops, SparseCore 0:
  9.7 95.1 all-gather.4
  106.6 48.6 all-gather.6
  1110.7 48.3 reduce-scatter.4
  1352.9 125.8 reduce-scatter.2
  1491.5 97.3 all-reduce.82
where the time goes:
time: 1640 us; the launch traced here: 1610 us
  local copies, waits for them, and re-layouts  371 us (23%)
  matrix products  334 us (20%)
  other arithmetic  333 us (20%)
  waiting for transfers between devices  328 us (20%)
  starting transfers between devices  111 us (7%)
  blocking collectives  69.9 us (4%)
  loops' own time  48.2 us (3%)
  between operations  18.1 us (1%)
    reduce_scatter x1, waiting for transfers between devices, body(): lax.psum_scatter(totals[0].astype(jnp.bfloat16), 'wshard', scatter_dimens...  101 us
    psum x1, waiting for transfers between devices, in_one(): so_far = lax.psum(jnp.concatenate([a.ravel() for a in arrays]), axis)  83.7 us
    another operation x114, other arithmetic  76.1 us
    all_gather x1, waiting for transfers between devices, body(): lax.all_gather(in_proj[0], 'wshard', axis=0, tiled=True)  74.2 us
    all_gather x3, blocking collectives, gather_turned(): whole = lax.all_gather(both, axis, axis=0, tiled=True)  69.9 us
    dynamic_slice x72, local copies, waits for them, and re-layouts, mixing(): unused, outputs = lax.scan(jax.checkpoint(span_update), start_state, inputs)  69.8 us
    dot_general x36, matrix products, span_update(): jnp.einsum('hij,jhp->ihp', scores[None] * decay_matrix, scaled_x, precisi...  65.7 us
    dot_general x48, matrix products, span_update(): scores = jnp.dot(c_rows, b_rows.T, precision=exact_matmul_accuracy)  51.4 us
  transfers between devices with their start and end apart: 28, of which 17 were waited for; matrix products, arithmetic and copies ran while one was open for 27% of the time, Pallas kernels for 0%

commit v1 on v0

v1 whole, which is shorter than its diff:
```python
import jax
import jax.numpy as jnp
from jax import lax
from jax.experimental import pallas as pl
from jax.experimental.pallas import tpu as pltpu
from jax.sharding import PartitionSpec as P

SPAN = 256
EPS = 1e-05
F32 = jnp.float32
BF16 = jnp.bfloat16
MESH = pl.DeviceIdType.MESH
VMEM_ASK = 48 * 1024 * 1024

HC = 128
NS = 128
PC = 640
AUX = 128
HEAD = 64


def dot_nn(a, b):
    return lax.dot_general(a, b, (((1,), (0,)), ((), ())), preferred_element_type=F32)


def dot_nt(a, b):
    return lax.dot_general(a, b, (((1,), (1,)), ((), ())), preferred_element_type=F32)


def dot_tn(a, b):
    return lax.dot_general(a, b, (((0,), (0,)), ((), ())), preferred_element_type=F32)


def three(x):
    hi = x.astype(BF16)
    rest = x - hi.astype(F32)
    mid = rest.astype(BF16)
    low = (rest - mid.astype(F32)).astype(BF16)
    return hi, mid, low


def exact_left(ones, x):
    hi, mid, low = three(x)
    return dot_nn(ones, hi) + dot_nn(ones, mid) + dot_nn(ones, low)


def exact_right(x, ones):
    hi, mid, low = three(x)
    return dot_nn(hi, ones) + dot_nn(mid, ones) + dot_nn(low, ones)


def iota(shape, dim):
    return lax.broadcasted_iota(jnp.int32, shape, dim)


def sigmoid(x):
    return 1.0 / (1.0 + jnp.exp(-x))


def softplus(x):
    return jnp.maximum(x, 0.0) + jnp.log1p(jnp.exp(-jnp.abs(x)))


def conv_rows(vbuf, cw_ref, mask):
    z = vbuf[pl.ds(8, SPAN), :] * cw_ref[3:4, :] + cw_ref[4:5, :]
    for k in (1, 2, 3):
        z = z + vbuf[pl.ds(8 - k, SPAN), :] * cw_ref[3 - k : 4 - k, :] * mask[:, k - 1 : k]
    return z


def block_terms(dt, vec_ref, mask, docr_ref):
    step = softplus(dt + vec_ref[0:1, :])
    log_decay = -step * vec_ref[1:2, :]
    rows, cols = iota((SPAN, SPAN), 0), iota((SPAN, SPAN), 1)
    lower = rows >= cols
    running = exact_left(lower.astype(F32).astype(BF16), log_decay)
    turned = running.T
    allowed = lower & (mask[:, 8:9] == docr_ref[...])
    decays = []
    for h in (0, 1):
        gaps = running[:, h * HEAD : h * HEAD + 1] - turned[h * HEAD : h * HEAD + 1, :]
        decays.append(jnp.exp(jnp.where(allowed, gaps, -1e30)))
    reach = jnp.exp(running) * mask[:, 6:7]
    total = running[SPAN - 1 :, :]
    tail = jnp.exp(total - running) * mask[:, 7:8]
    carry = jnp.exp(total) * mask[SPAN - 1 :, 6:7]
    return step, log_decay, decays, reach, tail, carry


def fwd_kernel(
    n_ref, w_ref, wo_ref, cw_ref, vec_ref, mask_ref, docr_ref,
    part_ref, vh_ref, gate_ref, dt_ref, mix_ref, scan_ref, st_ref,
    vbuf, state,
):
    @pl.when(pl.program_id(0) == 0)
    def _():
        vbuf[0:8, :] = jnp.zeros((8, 3 * HC), F32)
        state[...] = jnp.zeros_like(state)

    mask = mask_ref[...]
    proj = dot_nn(n_ref[...], w_ref[...])
    gate = proj[:, :HC]
    v = proj[:, HC : 4 * HC].astype(BF16).astype(F32)
    dt = proj[:, 4 * HC :].astype(BF16).astype(F32)
    vbuf[8:, :] = v
    z = conv_rows(vbuf, cw_ref, mask)
    vh_ref[0] = vbuf[...]
    vbuf[0:8, :] = v[SPAN - 8 :, :]
    act = z * sigmoid(z)
    xc = act[:, :HC]
    b16 = act[:, HC : 2 * HC].astype(BF16)
    c16 = act[:, 2 * HC :].astype(BF16)
    step, _, decays, reach, tail, carry = block_terms(dt, vec_ref, mask, docr_ref)
    xs = xc * step
    xs16 = xs.astype(BF16)
    scores = dot_nt(c16, b16)
    within = [dot_nn((scores * d).astype(BF16), xs16) for d in decays]
    first = iota((SPAN, HC), 1) < HEAD
    st = state[...]
    st_ref[0] = st
    scan = jnp.where(first, within[0], within[1]) + dot_nn(c16, st.astype(BF16)) * reach
    state[...] = st * carry + dot_tn(b16, (xs * tail).astype(BF16))
    mixed = (scan + xc * vec_ref[2:3, :]).astype(BF16)
    g = mixed.astype(F32) * (gate * sigmoid(gate))
    part_ref[:, : wo_ref.shape[1]] = dot_nn(
        (g * vec_ref[3:4, :]).astype(BF16), wo_ref[...]
    ).astype(BF16)
    hi, mid, low = three(jnp.sum(g * g, axis=1, keepdims=True))
    lane = iota((SPAN, AUX), 1)
    aux = jnp.where(lane == 0, hi.astype(F32), 0.0)
    aux = jnp.where(lane == 1, mid.astype(F32), aux)
    aux = jnp.where(lane == 2, low.astype(F32), aux)
    part_ref[:, wo_ref.shape[1] :] = aux.astype(BF16)
    gate_ref[...] = gate
    dt_ref[...] = dt
    mix_ref[...] = mixed
    scan_ref[...] = scan


def whole(shape):
    return pl.BlockSpec(shape, lambda i: (0,) * len(shape))


def forward_core(n, w, wo, cw, vec, mask, docr):
    length, width = n.shape
    blocks = length // SPAN

    def rows(cols):
        return pl.BlockSpec((SPAN, cols), lambda i: (i, 0))

    return pl.pallas_call(
        fwd_kernel,
        grid=(blocks,),
        in_specs=[
            rows(width), whole(w.shape), whole(wo.shape), whole(cw.shape), whole(vec.shape),
            rows(mask.shape[1]), pl.BlockSpec((1, SPAN), lambda i: (0, i)),
        ],
        out_specs=[
            rows(width + AUX),
            pl.BlockSpec((1, SPAN + 8, 3 * HC), lambda i: (i, 0, 0)),
            rows(HC), rows(HC), rows(HC), rows(HC),
            pl.BlockSpec((1, NS, HC), lambda i: (i, 0, 0)),
        ],
        out_shape=[
            jax.ShapeDtypeStruct((length, width + AUX), BF16),
            jax.ShapeDtypeStruct((blocks, SPAN + 8, 3 * HC), F32),
            jax.ShapeDtypeStruct((length, HC), F32),
            jax.ShapeDtypeStruct((length, HC), F32),
            jax.ShapeDtypeStruct((length, HC), BF16),
            jax.ShapeDtypeStruct((length, HC), F32),
            jax.ShapeDtypeStruct((blocks, NS, HC), F32),
        ],
        scratch_shapes=[pltpu.VMEM((SPAN + 8, 3 * HC), F32), pltpu.VMEM((NS, HC), F32)],
        compiler_params=pltpu.CompilerParams(vmem_limit_bytes=VMEM_ASK),
        name="forward_core",
    )(n, w, wo, cw, vec, mask, docr)


def bwd_kernel(
    c_ref, n_ref, w_ref, wo_ref, cw_ref, vec_ref, mask_ref, docr_ref,
    vh_ref, gate_ref, dt_ref, mix_ref, scan_ref, st_ref,
    part_ref, gin_ref, gout_ref, small_ref,
    dzbuf, dstate,
):
    @pl.when(pl.program_id(0) == 0)
    def _():
        dzbuf[SPAN:, :] = jnp.zeros((8, 3 * HC), F32)
        dstate[...] = jnp.zeros_like(dstate)
        gin_ref[...] = jnp.zeros_like(gin_ref)
        gout_ref[...] = jnp.zeros_like(gout_ref)
        small_ref[...] = jnp.zeros_like(small_ref)

    width = wo_ref.shape[1]
    mask = mask_ref[...]
    cot = c_ref[:, :width]
    aux = c_ref[:, width:].astype(F32)
    r = aux[:, 0:1] + aux[:, 1:2] + aux[:, 2:3]
    pull = aux[:, 3:4] + aux[:, 4:5]
    gate = gate_ref[...]
    sg = sigmoid(gate)
    silu = gate * sg
    mixed = mix_ref[...].astype(F32)
    g = mixed * silu
    gain = vec_ref[3:4, :]
    dy = dot_nt(cot, wo_ref[...])
    gr = g * r
    gout_ref[...] += dot_tn((gr * gain).astype(BF16), cot)
    d_gain = jnp.sum(dy * gr, axis=0, keepdims=True)
    dg = dy * (r * gain) - g * pull
    dm16 = (dg * silu).astype(BF16)
    dm = dm16.astype(F32)
    dgate = dg * mixed * (sg * (1.0 + gate * (1.0 - sg)))

    vbuf = vh_ref.at[0]
    z = conv_rows(vbuf, cw_ref, mask)
    sz = sigmoid(z)
    act = z * sz
    xc = act[:, :HC]
    b16 = act[:, HC : 2 * HC].astype(BF16)
    c16 = act[:, 2 * HC :].astype(BF16)
    dt = dt_ref[...]
    step, log_decay, decays, reach, tail, carry = block_terms(dt, vec_ref, mask, docr_ref)
    xs16 = (xc * step).astype(BF16)
    xs = xs16.astype(F32)
    scores = dot_nt(c16, b16)
    first = iota((SPAN, HC), 1) < HEAD
    zero16 = jnp.zeros((SPAN, HC), BF16)
    dscores = jnp.zeros((SPAN, SPAN), F32)
    dxs = []
    for h in (0, 1):
        own = jnp.where(first, dm16, zero16) if h == 0 else jnp.where(first, zero16, dm16)
        dp = dot_nt(own, xs16)
        dscores = dscores + dp * decays[h]
        dxs.append(dot_tn((scores * decays[h]).astype(BF16), dm16))
    ds16 = dscores.astype(BF16)
    st = st_ref[0]
    dst = dstate[...]
    dst16 = dst.astype(BF16)
    dcs16 = (dm * reach).astype(BF16)
    dc = dot_nn(ds16, b16) + dot_nt(dcs16, st.astype(BF16))
    db = dot_tn(ds16, c16) + dot_nt((xs * tail).astype(BF16), dst16)
    dxs_tail = dot_nn(b16, dst16) * tail
    dxs_all = jnp.where(first, dxs[0], dxs[1]) + dxs_tail
    dstate[...] = dst * carry + dot_tn(c16, dcs16)

    d_total = jnp.sum(xs * dxs_tail, axis=0, keepdims=True) + carry * jnp.sum(
        dst * st, axis=0, keepdims=True
    )
    flow = dm * scan_ref[...] - xs * dxs_all
    rows, cols = iota((SPAN, SPAN), 0), iota((SPAN, SPAN), 1)
    upper = (cols >= rows).astype(F32).astype(BF16)
    flow = exact_left(upper, flow) + d_total
    same_head = ((iota((HC, HC), 0) < HEAD) == (iota((HC, HC), 1) < HEAD)).astype(F32).astype(BF16)
    d_log = exact_right(flow, same_head)
    d_step = exact_right(dxs_all * xc, same_head) - d_log * vec_ref[1:2, :]
    d_alog = jnp.sum(d_log * log_decay, axis=0, keepdims=True)
    d_dt = d_step * sigmoid(dt + vec_ref[0:1, :])
    d_skip = jnp.sum(dm * xc, axis=0, keepdims=True)
    d_xc = dm * vec_ref[2:3, :] + dxs_all * step

    dact = sz * (1.0 + z * (1.0 - sz))
    dzbuf[:SPAN, 0:HC] = d_xc * dact[:, :HC]
    dzbuf[:SPAN, HC : 2 * HC] = db * dact[:, HC : 2 * HC]
    dzbuf[:SPAN, 2 * HC :] = dc * dact[:, 2 * HC :]
    dz = dzbuf[:SPAN, :]
    dv = dz * cw_ref[3:4, :]
    small_ref[3:4, :] += jnp.sum(dz * vbuf[pl.ds(8, SPAN), :], axis=0, keepdims=True)
    small_ref[4:5, :] += jnp.sum(dz, axis=0, keepdims=True)
    for k in (1, 2, 3):
        dv = dv + dzbuf[pl.ds(k, SPAN), :] * cw_ref[3 - k : 4 - k, :] * mask[:, 2 + k : 3 + k]
        small_ref[3 - k : 4 - k, :] += jnp.sum(
            dz * vbuf[pl.ds(8 - k, SPAN), :] * mask[:, k - 1 : k], axis=0, keepdims=True
        )
    dzbuf[SPAN:, :] = dz[:8, :]
    small_ref[5:6, 0:HC] += d_gain
    small_ref[5:6, HC : 2 * HC] += d_skip
    small_ref[6:7, 0:HC] += jnp.sum(d_dt, axis=0, keepdims=True)
    small_ref[6:7, HC : 2 * HC] += d_alog

    lane = iota((SPAN, HC), 1)
    one_each = jnp.where((lane == 0) | (lane == HEAD), d_dt, 0.0)
    gp = jnp.concatenate(
        [dgate.astype(BF16), dv.astype(BF16), one_each.astype(BF16)], axis=1
    )
    part_ref[...] = dot_nt(gp, w_ref[...]).astype(BF16)
    gin_ref[...] += dot_tn(n_ref[...], gp)


def backward_core(cot, n, w, wo, cw, vec, mask, docr, kept):
    length, width = n.shape
    blocks = length // SPAN
    last = blocks - 1

    def rows(cols):
        return pl.BlockSpec((SPAN, cols), lambda i: (last - i, 0))

    def stack(a):
        return pl.BlockSpec((1,) + a.shape[1:], lambda i: (last - i, 0, 0))

    return pl.pallas_call(
        bwd_kernel,
        grid=(blocks,),
        in_specs=[
            rows(width + AUX), rows(width), whole(w.shape), whole(wo.shape), whole(cw.shape),
            whole(vec.shape), rows(mask.shape[1]), pl.BlockSpec((1, SPAN), lambda i: (0, last - i)),
            stack(kept[0]), rows(HC), rows(HC), rows(HC), rows(HC), stack(kept[5]),
        ],
        out_specs=[rows(width), whole(w.shape), whole(wo.shape), whole((8, 3 * HC))],
        out_shape=[
            jax.ShapeDtypeStruct((length, width), BF16),
            jax.ShapeDtypeStruct(w.shape, F32),
            jax.ShapeDtypeStruct(wo.shape, F32),
            jax.ShapeDtypeStruct((8, 3 * HC), F32),
        ],
        scratch_shapes=[pltpu.VMEM((SPAN + 8, 3 * HC), F32), pltpu.VMEM((NS, HC), F32)],
        compiler_params=pltpu.CompilerParams(vmem_limit_bytes=VMEM_ASK),
        name="backward_core",
    )(cot, n, w, wo, cw, vec, mask, docr, *kept)


def greet_all(axis, count, me):
    barrier = pltpu.get_barrier_semaphore()
    for d in range(1, count):
        pl.semaphore_signal(
            barrier, inc=1, device_id={axis: lax.rem(me + d, count)}, device_id_type=MESH
        )
    pl.semaphore_wait(barrier, count - 1)


def spread_kernel(axis, count, x_ref, o_ref, send, recv, own):
    me = lax.axis_index(axis)
    rows = x_ref.shape[0]
    place = o_ref.at[pl.ds(pl.multiple_of(me * rows, rows), rows)]
    mine = pltpu.make_async_copy(x_ref, place, own)
    mine.start()
    greet_all(axis, count, me)
    copies = []
    for d in range(1, count):
        copy = pltpu.make_async_remote_copy(
            src_ref=x_ref, dst_ref=place, send_sem=send.at[d], recv_sem=recv.at[d],
            device_id={axis: lax.rem(me + d, count)}, device_id_type=MESH,
        )
        copy.start()
        copies.append(copy)
    mine.wait()
    for copy in copies:
        copy.wait()


def spread(x, axis, call_id):
    count = lax.axis_size(axis)
    return pl.pallas_call(
        lambda *refs: spread_kernel(axis, count, *refs),
        in_specs=[pl.BlockSpec(memory_space=pl.ANY)],
        out_specs=pl.BlockSpec(memory_space=pl.ANY),
        out_shape=jax.ShapeDtypeStruct((count * x.shape[0],) + x.shape[1:], x.dtype),
        scratch_shapes=[
            pltpu.SemaphoreType.DMA((count,)), pltpu.SemaphoreType.DMA((count,)),
            pltpu.SemaphoreType.DMA,
        ],
        compiler_params=pltpu.CompilerParams(collective_id=call_id, has_side_effects=True),
        name="spread",
    )(x)


def collect_kernel(axis, count, x_ref, o_ref, landing, send, recv, own):
    me = lax.axis_index(axis)
    rows = o_ref.shape[0]

    def block(j):
        return x_ref.at[pl.ds(pl.multiple_of(j * rows, rows), rows)]

    mine = pltpu.make_async_copy(block(me), landing.at[0], own)
    mine.start()
    greet_all(axis, count, me)
    copies = []
    for d in range(1, count):
        to = lax.rem(me + d, count)
        copy = pltpu.make_async_remote_copy(
            src_ref=block(to), dst_ref=landing.at[d], send_sem=send.at[d], recv_sem=recv.at[d],
            device_id={axis: to}, device_id_type=MESH,
        )
        copy.start()
        copies.append(copy)
    mine.wait()
    for copy in copies:
        copy.wait()
    total = landing[0].astype(F32)
    for d in range(1, count):
        total = total + landing[d].astype(F32)
    o_ref[...] = total


def collect(x, axis, call_id):
    count = lax.axis_size(axis)
    rows = x.shape[0] // count
    return pl.pallas_call(
        lambda *refs: collect_kernel(axis, count, *refs),
        in_specs=[pl.BlockSpec(memory_space=pl.ANY)],
        out_specs=pl.BlockSpec(memory_space=pltpu.VMEM),
        out_shape=jax.ShapeDtypeStruct((rows, x.shape[1]), F32),
        scratch_shapes=[
            pltpu.VMEM((count, rows, x.shape[1]), x.dtype),
            pltpu.SemaphoreType.DMA((count,)), pltpu.SemaphoreType.DMA((count,)),
            pltpu.SemaphoreType.DMA,
        ],
        compiler_params=pltpu.CompilerParams(
            collective_id=call_id, has_side_effects=True, vmem_limit_bytes=VMEM_ASK
        ),
        name="collect",
    )(x)


def rms_scale(values, gain):
    return values * lax.rsqrt(jnp.mean(values * values, axis=-1, keepdims=True) + EPS) * gain


def document_masks(doc):
    length = doc.shape[0]
    cols = []
    for k in (1, 2, 3):
        before = jnp.pad(doc, (k, 0), constant_values=-1)[:length]
        cols.append(before == doc)
    for k in (1, 2, 3):
        after = jnp.pad(doc, (0, k), constant_values=-1)[k:]
        cols.append(after == doc)
    blocks = doc.reshape(-1, SPAN)
    previous = jnp.concatenate([doc[:1], blocks[:-1, -1]])
    cols.append((blocks == previous[:, None]).reshape(-1))
    cols.append((blocks == blocks[:, -1:]).reshape(-1))
    cols.append(doc)
    cols = [c.astype(F32) for c in cols]
    cols += [jnp.zeros_like(cols[0])] * (16 - len(cols))
    return jnp.stack(cols, axis=1), doc.astype(F32)[None, :]


def forward_layer(u, n, layer, mask, docr, inner, reduce_rows):
    w, wo, cw, vec, _ = layer
    out = forward_core(n, w, wo, cw, vec, mask, docr)
    summed = reduce_rows(out[0])
    width = u.shape[1]
    square = summed[:, width] + summed[:, width + 1] + summed[:, width + 2]
    r = lax.rsqrt(square / inner + EPS)[:, None]
    branch = summed[:, :width] * r
    return u + branch, (branch, r, out[1:])


def backward_payload(c, branch, r, inner):
    low = c.astype(BF16)
    pull = r * r * jnp.sum(low.astype(F32) * branch, axis=1, keepdims=True) / inner
    hi, mid, lo = three(r)
    phi, pmid, _ = three(pull)
    pad = jnp.zeros((c.shape[0], AUX - 5), BF16)
    return jnp.concatenate([low, hi, mid, lo, phi, pmid, pad], axis=1)


def layer_weights(in_proj, out_proj, conv_weight, conv_bias, dt_bias, a_log, skip_scale, pre_gain, norm_gain, inner, q):
    heads = dt_bias.shape[0]
    def cols(a, start, size):
        return lax.dynamic_slice_in_dim(a, start, size, a.ndim - 1)
    bc = 2 * inner
    wdt = jnp.repeat(cols(in_proj, bc + 2 * NS + 2 * q, 2), HEAD, axis=1)
    w = jnp.concatenate(
        [cols(in_proj, q * HC, HC), cols(in_proj, inner + q * HC, HC),
         in_proj[:, bc : bc + 2 * NS], wdt], axis=1,
    )
    cw = jnp.concatenate([cols(conv_weight, q * HC, HC), conv_weight[:, inner:]], axis=1)
    cb = jnp.concatenate([cols(conv_bias, q * HC, HC), conv_bias[inner:]])
    def lanes(a):
        return jnp.repeat(cols(a, 2 * q, 2), HEAD)
    vec = jnp.stack(
        [lanes(dt_bias), jnp.exp(lanes(a_log)), lanes(skip_scale), cols(norm_gain, q * HC, HC)]
    )
    return w, cw, cb, vec, pre_gain


def body(
    block_input, doc_ids, out_grad, in_proj, out_proj, conv_weight, conv_bias,
    dt_bias, a_log, skip_scale, pre_gain, norm_gain,
):
    part = lax.axis_index("section")
    q = lax.axis_index("seq")
    n_seq = lax.axis_size("seq")
    n_z = lax.axis_size("wshard")
    inner = norm_gain.shape[1]
    width = block_input.shape[3]
    heads = dt_bias.shape[1]

    w, cw, cb, vec, pre = layer_weights(
        in_proj[0], None, conv_weight[0], conv_bias[0], dt_bias[0], a_log[0], skip_scale[0],
        pre_gain[0], norm_gain[0], inner, q,
    )
    out_rows = out_proj.shape[1]
    per_plane = out_rows // HC
    wo = lax.dynamic_slice_in_dim(out_proj[0], lax.rem(q, per_plane) * HC, HC, 0)
    both = ("section", "wshard")
    w_all = lax.all_gather(w, both, axis=0, tiled=True).reshape(2, width, PC)
    wo_all = lax.all_gather(wo, both, axis=0).reshape(2, n_z, HC, width)
    wo_all = lax.dynamic_index_in_dim(wo_all, q // per_plane, 1, keepdims=False)
    small = jnp.concatenate([cw.ravel(), cb, vec.ravel(), pre])
    small_all = lax.all_gather(small, "section", axis=0)
    layers = []
    for l in (0, 1):
        s = small_all[l]
        cwl = jnp.concatenate([s[: 5 * 3 * HC].reshape(5, 3 * HC), jnp.zeros((3, 3 * HC), F32)])
        at = 5 * 3 * HC
        vecl = jnp.concatenate([s[at : at + 4 * HC].reshape(4, HC), jnp.zeros((4, HC), F32)])
        layers.append((w_all[l], wo_all[l], cwl, vecl, s[at + 4 * HC :]))

    doc = lax.dynamic_index_in_dim(doc_ids[:, 0], part, 0, keepdims=False)
    mask, docr = document_masks(doc)
    u = lax.dynamic_index_in_dim(block_input[:, 0], part, 0, keepdims=False).astype(F32)
    cot = lax.dynamic_index_in_dim(out_grad[:, 0], part, 0, keepdims=False).astype(F32)

    inputs, normed, saved, hidden = [], [], [], []
    for l in (0, 1):
        inputs.append(u)
        n = spread(rms_scale(u, layers[l][4]).astype(BF16), "seq", 1)
        normed.append(n)
        u, s = forward_layer(
            u, n, layers[l], mask, docr, inner, lambda x: collect(x, "seq", 2)
        )
        hidden.append(u)
        saved.append(s)

    grads_in, grads = [None, None], [None, None]
    for l in (1, 0):
        branch, r, kept = saved[l]
        w, wo, cwl, vecl, gain = layers[l]
        payload = spread(backward_payload(cot, branch, r, inner), "seq", 3)
        gpart, gin, gout, gsmall = backward_core(
            payload, normed[l], w, wo, cwl, vecl, mask, docr, kept
        )
        g_normed = collect(gpart, "seq", 4)
        _, pull = jax.vjp(rms_scale, inputs[l], gain)
        path, g_pre = pull(g_normed)
        cot = cot + path
        grads_in[l] = cot
        grads[l] = (gin, gout, gsmall, g_pre)

    def swap(a):
        return lax.ppermute(a, "section", [(0, 1), (1, 0)])

    def by_layer(pair):
        mine = jnp.where(part == 0, pair[0], pair[1])
        other = swap(jnp.where(part == 0, pair[1], pair[0]))
        return jnp.where(part == 0, jnp.stack([mine, other]), jnp.stack([other, mine]))

    hidden_out = by_layer(hidden)
    grads_out = by_layer(grads_in)

    def sent_and_summed(x, axis):
        arrived = lax.all_to_all(x, axis, split_axis=0, concat_axis=0, tiled=True)
        return arrived.astype(F32).sum(axis=0)

    n_rows = width // n_z
    gin = jnp.stack([grads[0][0], grads[1][0]]).astype(BF16).reshape(2 * n_z, n_rows * PC)
    gout = jnp.stack([grads[0][1], grads[1][1]]).astype(BF16).reshape(2 * n_z, -1)
    piece = HC // n_z
    summed = sent_and_summed(jnp.concatenate([gin, gout], axis=1), both)
    gin = summed[: n_rows * PC].reshape(n_rows, PC)
    gout = summed[n_rows * PC :].reshape(piece, width).astype(BF16)
    n_y = n_seq // per_plane
    route = []
    for y in range(n_y):
        for x in range(per_plane):
            for z in range(n_z):
                route.append(((y * per_plane + x) * n_z + z, (z * per_plane + x) * n_z + y))
    gout = lax.ppermute(gout, ("seq", "wshard"), route)
    g_bc = gin[:, 2 * HC : 4 * HC].astype(BF16).reshape(n_seq, -1)
    g_bc = sent_and_summed(g_bc, "seq").astype(BF16)
    g_own = jnp.concatenate([gin[:, : 2 * HC], gin[:, 4 * HC :: HEAD]], axis=1).astype(BF16)
    flat = jnp.concatenate([g_own.ravel(), g_bc, gout.ravel()])
    everyone = lax.all_gather(flat, "seq", axis=0)
    own = everyone[:, : g_own.size].reshape(n_seq, n_rows, -1)
    own = jnp.moveaxis(own, 0, 1).astype(F32)
    shard_in = jnp.concatenate(
        [
            own[:, :, :HC].reshape(n_rows, -1),
            own[:, :, HC : 2 * HC].reshape(n_rows, -1),
            everyone[:, g_own.size : g_own.size + g_bc.size].reshape(n_rows, -1).astype(F32),
            own[:, :, 2 * HC :].reshape(n_rows, -1),
        ],
        axis=1,
    )
    shard_out = everyone[:, g_own.size + g_bc.size :].reshape(n_z, per_plane, piece, width)
    shard_out = jnp.moveaxis(shard_out, 0, 1).reshape(out_rows, width).astype(F32)

    def placed(values, extent, start):
        full = jnp.zeros(values.shape[:-1] + (extent,), F32)
        return lax.dynamic_update_slice_in_dim(full, values, start, values.ndim - 1)

    def small_vector(g):
        _, _, s, g_pre = g
        conv = jnp.concatenate([placed(s[:5, :HC], inner, q * HC), s[:5, HC:]], axis=1)
        per_head = jnp.stack([
            s[6, 0:HC:HEAD],
            s[6, HC : 2 * HC : HEAD],
            s[5, HC : 2 * HC].reshape(-1, HEAD).sum(axis=1),
        ])
        return jnp.concatenate([
            conv.ravel(), placed(per_head, heads, 2 * q).ravel(), g_pre,
            placed(s[5, :HC], inner, q * HC),
        ])

    vectors = [small_vector(g) for g in grads]
    mine = jnp.where(part == 0, vectors[0], vectors[1])
    mine = mine + swap(jnp.where(part == 0, vectors[1], vectors[0]))
    sums = lax.psum(mine, ("seq", "wshard"))
    channels = conv_weight.shape[2]
    at = 0
    pieces = []
    for shape in (
        conv_weight.shape[1:], (channels,), (heads,), (heads,), (heads,), (width,), (inner,)
    ):
        size = 1
        for extent in shape:
            size *= extent
        pieces.append(sums[at : at + size].reshape((1,) + shape))
        at += size
    return (
        hidden_out[None, :, None], grads_out[None, :, None], shard_in[None], shard_out[None],
        *pieces,
    )


def solution(mesh):
    specs = (
        P(None, "wshard", "seq", None),
        P(None, "wshard", None),
        P(None, "wshard", "seq", None),
        P("section", "wshard", None),
        P("section", "wshard", None),
        P("section", None, None),
        P("section", None),
        P("section", None),
        P("section", None),
        P("section", None),
        P("section", None),
        P("section", None),
    )
    outs = (
        P("section", None, "wshard", "seq", None),
        P("section", None, "wshard", "seq", None),
        P("section", "wshard", None),
        P("section", "wshard", None),
        P("section", None, None),
    ) + (P("section", None),) * 6
    return jax.shard_map(body, mesh=mesh, in_specs=specs, out_specs=outs, check_vma=False)
```

time: 1640 us -> 921 us (0.56); the launches traced: 1610 us -> 917 us
  Pallas kernels: 0 us -> 352 us
  matrix products: 334 us -> 0 us
  blocking collectives: 69.9 us -> 389 us
  waiting for transfers between devices: 328 us -> 10.1 us
  other arithmetic: 333 us -> 40.8 us
  local copies, waits for them, and re-layouts: 371 us -> 102 us
  starting transfers between devices: 111 us -> 7.3 us
  loops' own time: 48.2 us -> 0 us
    pallas_call x0 -> x12, Pallas kernels: none -> 352 us  [the longest x4 156 us: collect(): pl.pallas_call(lambda *refs: collect_kernel(axis, count, *refs), in_specs...]
    psum x0 -> x1, blocking collectives: none -> 345 us  [body(): sums = lax.psum(mine, ('seq', 'wshard'))]
    dot_general x174 -> x0, matrix products: 313 us -> none  [the longest x36 65.7 us: span_update(): jnp.einsum('hij,jhp->ihp', scores[None] * decay_matrix, scaled_x, precisi...]
    reduce_scatter x2 -> x0, waiting for transfers between devices: 101 us -> none  [the longest x1 101 us: body(): lax.psum_scatter(totals[0].astype(jnp.bfloat16), 'wshard', scatter_dimens...]
    all_to_all x19 -> x1, starting transfers between devices: 105 us -> 5.87 us  [sent_and_summed(): arrived = lax.all_to_all(x, axis, split_axis=0, concat_axis=0, tiled=True)]
    psum x1 -> x0, waiting for transfers between devices: 83.7 us -> none  [in_one(): so_far = lax.psum(jnp.concatenate([a.ravel() for a in arrays]), axis)]
    another operation x126 -> x10, other arithmetic: 83.8 us -> 0.91 us  [the longest x3 0.55 us: body(): jnp.stack([grads[0][0], grads[1][0]]).astype(BF16)]
    convert_element_type x55 -> x12, other arithmetic: 82.9 us -> 9.63 us  [the longest x1 2.3 us: body(): own = jnp.moveaxis(own, 0, 1).astype(F32)]
  transfers between devices with their start and end apart: 28 -> 8, of which waited for: 17 -> 3; matrix products, arithmetic and copies ran while one was open for 27% -> 3% of each run, Pallas kernels for 0% -> 9%
where the time goes in v1:
time: 921 us; the launch traced here: 917 us
  blocking collectives  389 us (42%)
  Pallas kernels  352 us (38%)
  local copies, waits for them, and re-layouts  102 us (11%)
  other arithmetic  40.8 us (4%)
  between operations  15.2 us (2%)
  waiting for transfers between devices  10.1 us (1%)
    psum x1, blocking collectives, body(): sums = lax.psum(mine, ('seq', 'wshard'))  345 us
    pallas_call x4, Pallas kernels, collect(): pl.pallas_call(lambda *refs: collect_kernel(axis, count, *refs), in_specs...  156 us
    pallas_call x4, Pallas kernels, spread(): pl.pallas_call(lambda *refs: spread_kernel(axis, count, *refs), in_specs=...  145 us
    unnamed x152, local copies, waits for them, and re-layouts  50.7 us
    all_to_all x1, blocking collectives, sent_and_summed(): arrived = lax.all_to_all(x, axis, split_axis=0, concat_axis=0, tiled=True)  41.6 us
    pallas_call x2, Pallas kernels, backward_core(): pl.pallas_call(bwd_kernel, grid=(blocks,), in_specs=[rows(width + AUX), r...  32.9 us
  transfers between devices with their start and end apart: 8, of which 3 were waited for; matrix products, arithmetic and copies ran while one was open for 3% of the time, Pallas kernels for 9%

profile of v1, /device:TPU:0, one launch (start us, length us, event | category | flops | bytes accessed | tf_op | source)
XLA Modules:
  0.0 916.5 jit_solution(6513314313133059814)
XLA Ops:
  9.3 3.0 copy.102
  17.9 1.8 all-gather.2
  21.3 37.6 %spread.4.n_ref = bf16[1024,1024]{1,0:T(8,128)(2,1)} custom-call(bf16[64,1024]{1,0:T(8,128)(2,1)} %fusion.2.refs_0_), custom_call_target="tpu_custom_call" | custom-call | tf_op jit(solution)/shard_map/spread/pallas_call | solution.py:352
  62.5 1.8 dynamic-slice_bitcast_fusion
  64.3 2.9 all-gather.8.cloned.1.call-done
  67.2 1.9 fusion.35
  69.2 9.1 forward_core.2
  81.1 2.1 copy-done.6
  83.2 41.9 %collect.4 = f32[64,1152]{1,0:T(8,128)S(1)} custom-call(bf16[1024,1152]{1,0:T(8,128)(2,1)S(1)} %copy-done.6), custom_call_target="tpu_custom_call" | custom-call | tf_op jit(solution)/shard_map/collect/pallas_call | solution.py:397
  128.5 33.8 %spread.5.n_ref = bf16[1024,1024]{1,0:T(8,128)(2,1)} custom-call(bf16[64,1024]{1,0:T(8,128)(2,1)} %multiply_convert_fusion.refs_0_), custom_call_target="tpu_custom_call" | custom-call | tf_op jit(solution)/shard_map/spread/pallas_call | solution.py:352
  163.3 8.6 forward_core.3
  173.8 2.3 copy-done.7
  176.1 37.2 %collect.5 = f32[64,1152]{1,0:T(8,128)} custom-call(bf16[1024,1152]{1,0:T(8,128)(2,1)S(1)} %copy-done.7), custom_call_target="tpu_custom_call" | custom-call | tf_op jit(solution)/shard_map/collect/pallas_call | solution.py:397
  213.4 1.6 subtract_convert_fusion.3
  215.0 2.1 fusion.4
  219.3 1.7 concatenate.91.refs_0_
  221.0 37.2 %spread.6.c_ref = bf16[1024,1152]{1,0:T(8,128)(2,1)} custom-call(bf16[64,1152]{1,0:T(8,128)(2,1)} %concatenate.91.refs_0_), custom_call_target="tpu_custom_call" | custom-call | tf_op jit(solution)/shard_map/spread/pallas_call | solution.py:352
  264.2 16.4 %backward_core.2 = (bf16[1024,1024]{1,0:T(8,128)(2,1)}, f32[1024,640]{1,0:T(8,128)}, f32[128,1024]{1,0:T(8,128)S(1)}, f32[8,384]{1,0:T(8,128)S(1)}) custom-call(bf16[1024,1152]{1,0:T(8,128)(2,1)} %spread.6.c_ref, bf16[1024,1024]{1,0:T(8,128)(2,1)} %spread.5.n_ref, bf16[1024,640]{1,0:T(8,128)(2,1)S(1)} %get-tuple-element.76.w_ref, ...), custom_call_target="tpu_custom_call" | custom-call | tf_op jit(solution)/shard_map/backward_core/pallas_call | solution.py:300
  280.7 1.8 copy-done.9
  282.4 33.9 %collect.6 = f32[64,1024]{1,0:T(8,128)S(1)} custom-call(bf16[1024,1024]{1,0:T(8,128)(2,1)S(1)} %copy-done.9), custom_call_target="tpu_custom_call" | custom-call | tf_op jit(solution)/shard_map/collect/pallas_call | solution.py:397
  318.3 1.7 concatenate.92.refs_0_
  320.0 36.8 %spread.7.c_ref = bf16[1024,1152]{1,0:T(8,128)(2,1)} custom-call(bf16[64,1152]{1,0:T(8,128)(2,1)} %concatenate.92.refs_0_), custom_call_target="tpu_custom_call" | custom-call | tf_op jit(solution)/shard_map/spread/pallas_call | solution.py:352
  360.8 16.5 %backward_core.3 = (bf16[1024,1024]{1,0:T(8,128)(2,1)}, f32[1024,640]{1,0:T(8,128)}, f32[128,1024]{1,0:T(8,128)S(1)}, f32[8,384]{1,0:T(8,128)S(1)}) custom-call(bf16[1024,1152]{1,0:T(8,128)(2,1)} %spread.7.c_ref, bf16[1024,1024]{1,0:T(8,128)(2,1)} %spread.4.n_ref, bf16[1024,640]{1,0:T(8,128)(2,1)S(1)} %get-tuple-element.77.w_ref, ...), custom_call_target="tpu_custom_call" | custom-call | tf_op jit(solution)/shard_map/backward_core/pallas_call | solution.py:300
  380.8 2.7 convert_element_type.250
  383.5 3.0 maximum_bitcast_fusion.1
  387.0 3.8 reduce.26
  390.7 4.8 reshape.533
  395.5 41.6 %all_to_all.19 = bf16[8,2,98304]{2,1,0:T(2,128)(2,1)} all-to-all(bf16[8,2,98304]{2,1,0:T(2,128)(2,1)S(1)} %reshape.533), channel_id=1, replica_groups=mesh['section'=2,'seq'=16,'wshard'=4] {'section','wshard'}, dimensions={0} | all-to-all | bytes 6291456 | tf_op jit(solution)/shard_map/all_to_all | solution.py:553
  437.1 7.8 reshape.534
  444.9 9.3 %convert_reduce_fusion = bf16[196608]{0:T(1024)(128)(2,1)S(1)} fusion(bf16[8,1,196608]{2,1,0:T(2,128)(2,1)} %reshape.534), kind=kLoop, calls=%fused_computation | loop fusion | flops 2949120 | bytes 3538944 | tf_op jit(solution)/shard_map/reduce_sum | solution.py:554
  454.6 1.5 reduce.27
  456.8 5.9 all-to-all-start.1
  464.2 6.6 all-to-all-done.1
  472.6 43.3 %collect.7 = f32[64,1024]{1,0:T(8,128)S(1)} custom-call(bf16[1024,1024]{1,0:T(8,128)(2,1)S(1)} %copy-done.8), custom_call_target="tpu_custom_call" | custom-call | tf_op jit(solution)/shard_map/collect/pallas_call | solution.py:397
  518.9 345.4 %psum.7 = f32[14688]{0:T(1024)S(1)} all-reduce(f32[14688]{0:T(1024)S(1)} %select_add_fusion), channel_id=1, replica_groups=mesh['section'=2,'seq'=16,'wshard'=4] {'seq','wshard'}, use_global_device_ids=true, to_apply=%region_12.13 | all-reduce | flops 14688 | bytes 117504 | tf_op jit(solution)/shard_map/psum | solution.py:609
  867.5 1.9 maximum_select_fusion
  870.2 3.2 copy.125
  873.4 2.3 slice_convert_fusion
  875.8 9.2 %reshape.496 = f32[16,256,258]{2,1,0:T(8,128)} reshape(f32[16,66048]{1,0:T(8,128)} %slice_convert_fusion) | data formatting | bytes 8454144 | tf_op jit(solution)/shard_map/convert_element_type | solution.py:576
  884.9 3.1 slice.298
  888.1 4.7 fusion.34
  892.8 1.5 slice_convert_fusion.1
  894.3 2.2 copy.114
  897.3 1.9 copy.113
  899.2 2.9 copy.112
  902.2 2.8 copy.122
  905.0 1.5 copy.116
  907.3 2.4 maximum_bitcast_fusion
  (298 shorter events, 52.3 us)
Async XLA Ops:
  7.2 55.3 %all-gather.10.cloned.1.call-start = ((), (), s32[]{:S(2)}) async-start(), calls=%async_computation.3 | async-start | bytes 2359296 | tf_op jit(solution)/shard_map/all_gather | solution.py:498
  9.2 58.1 %all-gather.8.cloned.1.call-start = ((), (), s32[]{:S(2)}) async-start(), calls=%async_computation.2 | async-start | bytes 2949120 | tf_op jit(solution)/shard_map/all_gather | solution.py:497
  9.2 7.3 copy-start.66
  9.2 7.5 copy-start.62
  9.2 7.5 copy-start.63
  9.2 7.9 copy-start.58
  9.3 8.6 slice-start
  9.3 8.6 copy-start.57
  9.3 10.5 %copy-start.39 = (bf16[2,1,64,1024]{3,2,1,0:T(8,128)(2,1)S(1)}, bf16[2,1,64,1024]{3,2,1,0:T(8,128)(2,1)}, u32[]{:S(2)}) copy-start(bf16[2,1,64,1024]{3,2,1,0:T(8,128)(2,1)} %param.12) | copy-start | bytes 786436
  12.3 46.7 %copy-start.59 = (s32[2,1,1024]{2,1,0:T(1,128)S(1)}, s32[2,1,1024]{2,1,0:T(1,128)}, u32[]{:S(2)}) copy-start(s32[2,1,1024]{2,1,0:T(1,128)} %param.13) | copy-start | bytes 24580
  19.9 39.0 %copy-start.60 = (f32[64]{0:T(128)}, f32[64]{0:T(128)S(1)}, u32[]{:S(2)}) copy-start(f32[64]{0:T(128)S(1)} %fusion.7) | copy-start | bytes 772
  19.9 39.0 %copy-start.55 = (f32[64]{0:T(128)}, f32[64]{0:T(128)S(1)}, u32[]{:S(2)}) copy-start(f32[64]{0:T(128)S(1)} %fusion.32) | copy-start | bytes 772
  20.0 107.6 %copy-start.47 = (f32[1,1024]{1,0:T(1,128)}, f32[1,1024]{1,0:T(1,128)S(1)}, u32[]{:S(2)}) copy-start(f32[1,1024]{1,0:T(1,128)S(1)} %get-tuple-element.103) | copy-start | bytes 12292
  64.3 4.9 copy-start.2
  81.0 44.1 %copy-start.14 = (f32[1024,128]{1,0:T(8,128)}, f32[1024,128]{1,0:T(8,128)S(1)}, u32[]{:S(2)}) copy-start(f32[1024,128]{1,0:T(8,128)S(1)} %get-tuple-element.44.dt_ref) | copy-start | bytes 1572868
  81.0 44.8 %copy-start.16 = (f32[1024,128]{1,0:T(8,128)}, f32[1024,128]{1,0:T(8,128)S(1)}, u32[]{:S(2)}) copy-start(f32[1024,128]{1,0:T(8,128)S(1)} %get-tuple-element.46.scan_ref) | copy-start | bytes 1572868
  81.0 44.8 %copy-start.26 = (bf16[1024,128]{1,0:T(8,128)(2,1)}, bf16[1024,128]{1,0:T(8,128)(2,1)S(1)}, u32[]{:S(2)}) copy-start(bf16[1024,128]{1,0:T(8,128)(2,1)S(1)} %get-tuple-element.45.mix_ref) | copy-start | bytes 786436
  125.9 46.0 %copy-start.51 = (f32[64]{0:T(128)}, f32[64]{0:T(128)S(1)}, u32[]{:S(2)}) copy-start(f32[64]{0:T(128)S(1)} %reduce.7) | copy-start | bytes 772
  127.6 44.3 %copy-start.53 = (f32[64]{0:T(128)}, f32[64]{0:T(128)S(1)}, u32[]{:S(2)}) copy-start(f32[64]{0:T(128)S(1)} %fusion.33) | copy-start | bytes 772
  173.8 39.6 %copy-start.18 = (f32[1024,128]{1,0:T(8,128)}, f32[1024,128]{1,0:T(8,128)S(1)}, u32[]{:S(2)}) copy-start(f32[1024,128]{1,0:T(8,128)S(1)} %get-tuple-element.36.gate_ref) | copy-start | bytes 1572868
  173.8 41.1 %copy-start.20 = (f32[1024,128]{1,0:T(8,128)}, f32[1024,128]{1,0:T(8,128)S(1)}, u32[]{:S(2)}) copy-start(f32[1024,128]{1,0:T(8,128)S(1)} %get-tuple-element.37.dt_ref) | copy-start | bytes 1572868
  173.8 41.1 %copy-start.22 = (f32[1024,128]{1,0:T(8,128)}, f32[1024,128]{1,0:T(8,128)S(1)}, u32[]{:S(2)}) copy-start(f32[1024,128]{1,0:T(8,128)S(1)} %get-tuple-element.39.scan_ref) | copy-start | bytes 1572868
  173.8 41.1 %copy-start.32 = (f32[4,128,128]{2,1,0:T(8,128)}, f32[4,128,128]{2,1,0:T(8,128)S(1)}, u32[]{:S(2)}) copy-start(f32[4,128,128]{2,1,0:T(8,128)S(1)} %get-tuple-element.40.st_ref) | copy-start | bytes 786436
  264.2 52.1 %copy-start.36 = (f32[64,1024]{1,0:T(8,128)S(1)}, f32[64,1024]{1,0:T(8,128)}, u32[]{:S(2)}) copy-start(f32[64,1024]{1,0:T(8,128)} %copy-done.35) | copy-start | bytes 786436
  264.2 52.1 %copy-start.48 = (f32[1,1024]{1,0:T(1,128)S(1)}, f32[1,1024]{1,0:T(1,128)}, u32[]{:S(2)}) copy-start(f32[1,1024]{1,0:T(1,128)} %copy-done.47) | copy-start | bytes 12292
  264.2 52.2 %copy-start.54 = (f32[64]{0:T(128)S(1)}, f32[64]{0:T(128)}, u32[]{:S(2)}) copy-start(f32[64]{0:T(128)} %copy-done.53) | copy-start | bytes 772
  280.6 37.5 %copy-start.24 = (f32[128,1024]{1,0:T(8,128)}, f32[128,1024]{1,0:T(8,128)S(1)}, u32[]{:S(2)}) copy-start(f32[128,1024]{1,0:T(8,128)S(1)} %get-tuple-element.52) | copy-start | bytes 1572868
  280.6 36.5 %copy-start.65 = (f32[64]{0:T(128)S(1)}, f32[64]{0:T(128)}, u32[]{:S(2)}) copy-start(f32[64]{0:T(128)} %copy-done.64) | copy-start | bytes 772
  280.6 36.5 %copy-start.52 = (f32[64]{0:T(128)S(1)}, f32[64]{0:T(128)}, u32[]{:S(2)}) copy-start(f32[64]{0:T(128)} %copy-done.51) | copy-start | bytes 772
  282.4 34.7 %copy-start.41 = (bf16[64,1024]{1,0:T(8,128)(2,1)S(1)}, bf16[64,1024]{1,0:T(8,128)(2,1)}, u32[]{:S(2)}) copy-start(bf16[64,1024]{1,0:T(8,128)(2,1)} %get-tuple-element.67) | copy-start | bytes 393220
  282.4 35.8 %copy-start.49 = (bf16[64,1]{1,0:T(8,128)(2,1)S(1)}, bf16[64,1]{1,0:T(8,128)(2,1)}, u32[]{:S(2)}) copy-start(bf16[64,1]{1,0:T(8,128)(2,1)} %get-tuple-element.64) | copy-start | bytes 388
  317.1 39.8 %copy-start.3 = (bf16[128,1024]{1,0:T(8,128)(2,1)S(1)}, bf16[128,1024]{1,0:T(8,128)(2,1)}, u32[]{:S(2)}) copy-start(bf16[128,1024]{1,0:T(8,128)(2,1)} %copy-done.2) | copy-start | bytes 786436
  317.1 39.8 %copy-start.13 = (f32[1024,128]{1,0:T(8,128)S(1)}, f32[1024,128]{1,0:T(8,128)}, u32[]{:S(2)}) copy-start(f32[1024,128]{1,0:T(8,128)} %copy-done.12) | copy-start | bytes 1572868
  318.1 38.7 %copy-start.25 = (f32[128,1024]{1,0:T(8,128)S(1)}, f32[128,1024]{1,0:T(8,128)}, u32[]{:S(2)}) copy-start(f32[128,1024]{1,0:T(8,128)} %copy-done.24) | copy-start | bytes 1572868
  454.5 18.1 %copy-start.8 = (bf16[1024,1024]{1,0:T(8,128)(2,1)S(1)}, bf16[1024,1024]{1,0:T(8,128)(2,1)}, u32[]{:S(2)}) copy-start(bf16[1024,1024]{1,0:T(8,128)(2,1)} %get-tuple-element.48.refs_0_) | copy-start | bytes 6291460
  456.8 14.0 %all-to-all-start.1 = ((bf16[16,2,2048]{2,1,0:T(2,128)(2,1)}), bf16[16,2,2048]{2,1,0:T(2,128)(2,1)S(1)}, u32[]{:S(2)}, u32[]{:S(2)}) async-start(bf16[16,2,2048]{2,1,0:T(2,128)(2,1)} %reshape.535), calls=%async_computation.1 | async-start | bytes 262144 | tf_op jit(solution)/shard_map/all_to_all | solution.py:553
  462.7 407.5 %all-gather.12.cloned.1.call-start = ((), (), s32[]{:S(2)}) async-start(), calls=%async_computation.4 | async-start | bytes 6998016 | tf_op jit(solution)/shard_map/all_gather | solution.py:574
  463.0 1.1 collective-permute-start.2
  464.2 52.9 %copy-start.50 = (f32[1024]{0:T(1024)S(1)}, f32[1024]{0:T(1024)}, u32[]{:S(2)}) copy-start(f32[1024]{0:T(1024)} %get-tuple-element.57) | copy-start | bytes 12292
  464.2 53.0 %copy-start.40 = (bf16[2,1,64,1024]{3,2,1,0:T(8,128)(2,1)S(1)}, bf16[2,1,64,1024]{3,2,1,0:T(8,128)(2,1)}, u32[]{:S(2)}) copy-start(bf16[2,1,64,1024]{3,2,1,0:T(8,128)(2,1)} %param.12) | copy-start | bytes 786436
  464.2 53.0 %copy-start.46 = (f32[1,1024]{1,0:T(1,128)S(1)}, f32[1,1024]{1,0:T(1,128)}, u32[]{:S(2)}) copy-start(f32[1,1024]{1,0:T(1,128)} %copy-done.45) | copy-start | bytes 12292
  464.2 53.0 %copy-start.56 = (f32[64]{0:T(128)S(1)}, f32[64]{0:T(128)}, u32[]{:S(2)}) copy-start(f32[64]{0:T(128)} %copy-done.55) | copy-start | bytes 772
  471.2 46.5 %copy-start.61 = (f32[64]{0:T(128)S(1)}, f32[64]{0:T(128)}, u32[]{:S(2)}) copy-start(f32[64]{0:T(128)} %copy-done.60) | copy-start | bytes 772
  471.2 46.5 %copy-start.43 = (f32[64,1024]{1,0:T(8,128)S(1)}, f32[64,1024]{1,0:T(8,128)}, u32[]{:S(2)}) copy-start(f32[64,1024]{1,0:T(8,128)} %get-tuple-element.63) | copy-start | bytes 786436
  472.6 394.9 %collective-permute-start = (f32[64,1024]{1,0:T(8,128)}, f32[64,1024]{1,0:T(8,128)}, u32[]{:S(2)}, u32[]{:S(2)}) collective-permute-start(f32[64,1024]{1,0:T(8,128)} %get-tuple-element.88), channel_id=1, source_target_pairs={{0,64},{64,0},{1,65},{65,1},{2,66},{66,2},{3,67},{67,3},{4,68},{68... | collective-permute-start | bytes 786440 | tf_op jit(solution)/shard_map/ppermute | solution.py:542
  472.6 394.9 %copy-start.42 = (f32[1,1,1,64,1024]{4,3,2,1,0:T(8,128)S(1)}, f32[1,1,1,64,1024]{4,3,2,1,0:T(8,128)}, u32[]{:S(2)}) copy-start(f32[1,1,1,64,1024]{4,3,2,1,0:T(8,128)} %get-tuple-element.89) | copy-start | bytes 786436
  517.5 1.3 collective-permute-start.3
  517.8 351.5 %collective-permute-start.1 = (f32[64,1024]{1,0:T(8,128)S(1)}, f32[64,1024]{1,0:T(8,128)S(1)}, u32[]{:S(2)}, u32[]{:S(2)}) collective-permute-start(f32[64,1024]{1,0:T(8,128)S(1)} %get-tuple-element.83), channel_id=1, source_target_pairs={{0,64},{64,0},{1,65},{65,1},{2,66},{66,2},{3,67},{67,3},{4,68},{68... | collective-permute-start | bytes 786440 | tf_op jit(solution)/shard_map/ppermute | solution.py:542
  (28 other events, 36.7 us)
Sparse Core Ops, SparseCore 0:
  10.3 27.8 all-gather.9
  40.5 26.7 all-gather.7
  472.3 83.3 all-gather.11

commit v2 on v1

--- a/solution.py
+++ b/solution.py
@@ -17,6 +17,8 @@
 PC = 640
 AUX = 128
 HEAD = 64
+SIDE = 4
+SPREAD_SPACE = pltpu.VMEM
 
 
 def dot_nn(a, b):
@@ -318,97 +320,561 @@
     )(cot, n, w, wo, cw, vec, mask, docr, *kept)
 
 
-def greet_all(axis, count, me):
+def ring_places(axis):
+    me = lax.axis_index(axis)
+    return me % SIDE, me // SIDE
+
+
+def place_of(half, f, s):
+    f, s = lax.rem(f, SIDE), lax.rem(s, SIDE)
+    return s * SIDE + f if half == 0 else f * SIDE + s
+
+
+def greet_neighbours(axis, x, y):
     barrier = pltpu.get_barrier_semaphore()
-    for d in range(1, count):
+    for dx, dy in ((1, 0), (3, 0), (0, 1), (0, 3)):
         pl.semaphore_signal(
-            barrier, inc=1, device_id={axis: lax.rem(me + d, count)}, device_id_type=MESH
+            barrier, inc=1, device_id={axis: place_of(0, x + dx, y + dy)}, device_id_type=MESH
         )
-    pl.semaphore_wait(barrier, count - 1)
-
-
-def spread_kernel(axis, count, x_ref, o_ref, send, recv, own):
-    me = lax.axis_index(axis)
+    pl.semaphore_wait(barrier, 4)
+
+
+def rows_at(ref, start, size):
+    return ref.at[pl.ds(pl.multiple_of(start, 16), size)]
+
+
+def spread_kernel(axis, x_ref, o_ref, send, recv, own):
+    x, y = ring_places(axis)
+    greet_neighbours(axis, x, y)
+    spread_steps(axis, x_ref, o_ref, send, recv, own)
+
+
+def spread_steps(axis, x_ref, o_ref, send, recv, own):
+    x, y = ring_places(axis)
     rows = x_ref.shape[0]
-    place = o_ref.at[pl.ds(pl.multiple_of(me * rows, rows), rows)]
-    mine = pltpu.make_async_copy(x_ref, place, own)
+    half_rows, quarter = rows // 2, rows // 4
+    mine = pltpu.make_async_copy(x_ref, rows_at(o_ref, place_of(0, x, y) * rows, rows), own)
     mine.start()
-    greet_all(axis, count, me)
-    copies = []
-    for d in range(1, count):
+    copies = {}
+
+    def go(name, half, block, offset, size, to, source=None):
+        index = len(copies)
+        place = rows_at(o_ref, block * rows + half * half_rows + offset, size)
         copy = pltpu.make_async_remote_copy(
-            src_ref=x_ref, dst_ref=place, send_sem=send.at[d], recv_sem=recv.at[d],
-            device_id={axis: lax.rem(me + d, count)}, device_id_type=MESH,
+            src_ref=place if source is None else source, dst_ref=place,
+            send_sem=send.at[index], recv_sem=recv.at[index],
+            device_id={axis: to}, device_id_type=MESH,
         )
         copy.start()
-        copies.append(copy)
+        copies[half, name] = copy
+
+    firsts = ((x, y), (y, x))
+
+    def across(half, d):
+        f, s = firsts[half]
+        block = place_of(half, f + d, s)
+        source = None
+        if d == 0:
+            source = x_ref.at[pl.ds(half * half_rows, half_rows)]
+        go(("t1", d), half, block, 0, half_rows, place_of(half, f, s + 1), source)
+        go(("t2", d), half, block, 0, half_rows, place_of(half, f, s + 3), source)
+
+    def onward(half, d):
+        f, s = firsts[half]
+        copies[half, ("t1", d)].wait_recv()
+        go(("u1", d), half, place_of(half, f + d, s + 3), 0, quarter, place_of(half, f, s + 1))
+        copies[half, ("t2", d)].wait_recv()
+        go(("u2", d), half, place_of(half, f + d, s + 1), quarter, quarter, place_of(half, f, s + 3))
+
+    for half in (0, 1):
+        f, s = firsts[half]
+        source = x_ref.at[pl.ds(half * half_rows, half_rows)]
+        block = place_of(half, f, s)
+        go("s1", half, block, 0, half_rows, place_of(half, f + 1, s), source)
+        go("s2", half, block, 0, half_rows, place_of(half, f + 3, s), source)
+    for half in (0, 1):
+        across(half, 0)
+    for half in (0, 1):
+        f, s = firsts[half]
+        copies[half, "s1"].wait_recv()
+        go("s3", half, place_of(half, f + 3, s), 0, quarter, place_of(half, f + 1, s))
+        copies[half, "s2"].wait_recv()
+        go("s4", half, place_of(half, f + 1, s), quarter, quarter, place_of(half, f + 3, s))
+    for half in (0, 1):
+        across(half, 3)
+        across(half, 1)
+    for half in (0, 1):
+        onward(half, 0)
+    for half in (0, 1):
+        copies[half, "s3"].wait_recv()
+        copies[half, "s4"].wait_recv()
+        across(half, 2)
+    for d in (3, 1, 2):
+        for half in (0, 1):
+            onward(half, d)
+    for half in (0, 1):
+        for d in range(SIDE):
+            copies[half, ("u1", d)].wait_recv()
+            copies[half, ("u2", d)].wait_recv()
+    for copy in copies.values():
+        copy.wait_send()
     mine.wait()
-    for copy in copies:
-        copy.wait()
 
 
 def spread(x, axis, call_id):
     count = lax.axis_size(axis)
     return pl.pallas_call(
-        lambda *refs: spread_kernel(axis, count, *refs),
-        in_specs=[pl.BlockSpec(memory_space=pl.ANY)],
-        out_specs=pl.BlockSpec(memory_space=pl.ANY),
+        lambda *refs: spread_kernel(axis, *refs),
+        in_specs=[pl.BlockSpec(memory_space=SPREAD_SPACE)],
+        out_specs=pl.BlockSpec(memory_space=SPREAD_SPACE),
         out_shape=jax.ShapeDtypeStruct((count * x.shape[0],) + x.shape[1:], x.dtype),
         scratch_shapes=[
-            pltpu.SemaphoreType.DMA((count,)), pltpu.SemaphoreType.DMA((count,)),
+            pltpu.SemaphoreType.DMA((40,)), pltpu.SemaphoreType.DMA((40,)),
             pltpu.SemaphoreType.DMA,
         ],
-        compiler_params=pltpu.CompilerParams(collective_id=call_id, has_side_effects=True),
+        compiler_params=pltpu.CompilerParams(
+            collective_id=call_id, has_side_effects=True, vmem_limit_bytes=VMEM_ASK
+        ),
         name="spread",
     )(x)
 
 
-def collect_kernel(axis, count, x_ref, o_ref, landing, send, recv, own):
-    me = lax.axis_index(axis)
+def collect_kernel(axis, x_ref, o_ref, far, near, stage, reduced, far2, near2, stage2, send, recv):
+    x, y = ring_places(axis)
     rows = o_ref.shape[0]
-
-    def block(j):
-        return x_ref.at[pl.ds(pl.multiple_of(j * rows, rows), rows)]
-
-    mine = pltpu.make_async_copy(block(me), landing.at[0], own)
-    mine.start()
-    greet_all(axis, count, me)
-    copies = []
-    for d in range(1, count):
-        to = lax.rem(me + d, count)
+    half_rows, quarter = rows // 2, rows // 4
+    greet_neighbours(axis, x, y)
+    copies = {}
+    firsts = ((x, y), (y, x))
+    order = (2, 1, 3, 0)
+
+    def go(name, half, source, target, to):
+        index = len(copies)
         copy = pltpu.make_async_remote_copy(
-            src_ref=block(to), dst_ref=landing.at[d], send_sem=send.at[d], recv_sem=recv.at[d],
+            src_ref=source, dst_ref=target, send_sem=send.at[index], recv_sem=recv.at[index],
             device_id={axis: to}, device_id_type=MESH,
         )
         copy.start()
-        copies.append(copy)
-    mine.wait()
-    for copy in copies:
-        copy.wait()
-    total = landing[0].astype(F32)
-    for d in range(1, count):
-        total = total + landing[d].astype(F32)
-    o_ref[...] = total
+        copies[half, name] = copy
+
+    def start_of(half, f, s):
+        return pl.multiple_of(place_of(half, f, s) * rows + half * half_rows, 16)
+
+    for d in order:
+        for half in (0, 1):
+            f, s = firsts[half]
+            start = start_of(half, f + d, s + 2)
+            go(("a1", d), half, rows_at(x_ref, start, quarter), far.at[half, d, 0],
+               place_of(half, f, s + 1))
+            go(("a2", d), half, rows_at(x_ref, start + quarter, quarter), far.at[half, d, 1],
+               place_of(half, f, s + 3))
+    for d in order:
+        for half in (0, 1):
+            f, s = firsts[half]
+            for side, (step, other) in enumerate(((1, 0), (3, 1))):
+                start = start_of(half, f + d, s + step)
+                plain = quarter * (1 - side)
+                through = quarter * side
+                stage[half, d, side, pl.ds(plain, quarter)] = x_ref[
+                    pl.ds(pl.multiple_of(start + plain, 16), quarter), :
+                ]
+                copies[half, (("a1", "a2")[side], d)].wait_recv()
+                stage[half, d, side, pl.ds(through, quarter)] = (
+                    x_ref[pl.ds(pl.multiple_of(start + through, 16), quarter), :].astype(F32)
+                    + far[half, d, side].astype(F32)
+                ).astype(BF16)
+                go((("b1", "b2")[side], d), half, stage.at[half, d, side], near.at[half, d, side],
+                   place_of(half, f, s + step))
+
+    def reduce_second(half, d):
+        f, s = firsts[half]
+        copies[half, ("b1", d)].wait_recv()
+        copies[half, ("b2", d)].wait_recv()
+        reduced[half, d] = (
+            x_ref[pl.ds(start_of(half, f + d, s), half_rows), :].astype(F32)
+            + near[half, d, 0].astype(F32) + near[half, d, 1].astype(F32)
+        )
+
+    for half in (0, 1):
+        f, s = firsts[half]
+        reduce_second(half, 2)
+        stage2[half, 2] = reduced[half, 2].astype(BF16)
+        go("c1", half, stage2.at[half, 2, pl.ds(0, quarter)], far2.at[half, 0],
+           place_of(half, f + 1, s))
+        go("c2", half, stage2.at[half, 2, pl.ds(quarter, quarter)], far2.at[half, 1],
+           place_of(half, f + 3, s))
+    for d, side in ((1, 0), (3, 1)):
+        for half in (0, 1):
+            f, s = firsts[half]
+            reduce_second(half, d)
+            plain, through = quarter * (1 - side), quarter * side
+            copies[half, ("c1", "c2")[side]].wait_recv()
+            stage2[half, side, pl.ds(plain, quarter)] = reduced[
+                half, d, pl.ds(plain, quarter)
+            ].astype(BF16)
+            stage2[half, side, pl.ds(through, quarter)] = (
+                reduced[half, d, pl.ds(through, quarter)] + far2[half, side].astype(F32)
+            ).astype(BF16)
+            go(("d1", "d2")[side], half, stage2.at[half, side], near2.at[half, side],
+               place_of(half, f + d, s))
+    for half in (0, 1):
+        reduce_second(half, 0)
+        copies[half, "d1"].wait_recv()
+        copies[half, "d2"].wait_recv()
+        o_ref[pl.ds(half * half_rows, half_rows), :] = (
+            reduced[half, 0] + near2[half, 0].astype(F32) + near2[half, 1].astype(F32)
+        )
+    for copy in copies.values():
+        copy.wait_send()
 
 
 def collect(x, axis, call_id):
     count = lax.axis_size(axis)
-    rows = x.shape[0] // count
+    rows, cols = x.shape[0] // count, x.shape[1]
+    half_rows, quarter = rows // 2, rows // 4
     return pl.pallas_call(
-        lambda *refs: collect_kernel(axis, count, *refs),
-        in_specs=[pl.BlockSpec(memory_space=pl.ANY)],
+        lambda *refs: collect_kernel(axis, *refs),
+        in_specs=[pl.BlockSpec(memory_space=pltpu.VMEM)],
         out_specs=pl.BlockSpec(memory_space=pltpu.VMEM),
-        out_shape=jax.ShapeDtypeStruct((rows, x.shape[1]), F32),
+        out_shape=jax.ShapeDtypeStruct((rows, cols), F32),
         scratch_shapes=[
-            pltpu.VMEM((count, rows, x.shape[1]), x.dtype),
-            pltpu.SemaphoreType.DMA((count,)), pltpu.SemaphoreType.DMA((count,)),
-            pltpu.SemaphoreType.DMA,
+            pltpu.VMEM((2, SIDE, 2, quarter, cols), x.dtype),
+            pltpu.VMEM((2, SIDE, 2, half_rows, cols), x.dtype),
+            pltpu.VMEM((2, SIDE, 2, half_rows, cols), x.dtype),
+            pltpu.VMEM((2, SIDE, half_rows, cols), F32),
+            pltpu.VMEM((2, 2, quarter, cols), x.dtype),
+            pltpu.VMEM((2, 2, half_rows, cols), x.dtype),
+            pltpu.VMEM((2, 3, half_rows, cols), x.dtype),
+            pltpu.SemaphoreType.DMA((40,)), pltpu.SemaphoreType.DMA((40,)),
         ],
         compiler_params=pltpu.CompilerParams(
             collective_id=call_id, has_side_effects=True, vmem_limit_bytes=VMEM_ASK
         ),
         name="collect",
     )(x)
+
+
+def greet(axis_steps):
+    barrier = pltpu.get_barrier_semaphore()
+    for target in axis_steps:
+        pl.semaphore_signal(barrier, inc=1, device_id=target, device_id_type=MESH)
+    pl.semaphore_wait(barrier, len(axis_steps))
+
+
+def ring_neighbours(axis, x, y):
+    steps = ((1, 0), (3, 0), (0, 1), (0, 3))
+    return [{axis: place_of(0, x + dx, y + dy)} for dx, dy in steps]
+
+
+def plane_neighbours():
+    z = lax.axis_index("wshard")
+    return [{"wshard": lax.rem(z + 1, SIDE)}, {"wshard": lax.rem(z + 3, SIDE)}]
+
+
+def other_core():
+    return {"section": 1 - lax.axis_index("section")}
+
+
+class Sender:
+    def __init__(self, send, recv):
+        self.send, self.recv, self.used, self.copies = send, recv, 0, {}
+
+    def make(self, name, source, target, to):
+        copy = pltpu.make_async_remote_copy(
+            src_ref=source, dst_ref=target, send_sem=self.send.at[self.used],
+            recv_sem=self.recv.at[self.used], device_id=to, device_id_type=MESH,
+        )
+        self.used += 1
+        self.copies[name] = copy
+        return copy
+
+    def go(self, name, source, target, to):
+        self.make(name, source, target, to).start()
+
+    def arrived(self, name):
+        self.copies[name].wait_recv()
+
+    def sent(self):
+        for copy in self.copies.values():
+            copy.wait_send()
+
+
+def opening_kernel(
+    axis, x_ref, w_ref, wo_ref, o_ref, wall_ref, woall_ref,
+    send, recv, own, send2, recv2, own2,
+):
+    x, y = ring_places(axis)
+    part, z = lax.axis_index("section"), lax.axis_index("wshard")
+    up, down = plane_neighbours()
+    greet(ring_neighbours(axis, x, y) + [up, down, other_core()])
+    rows = w_ref.shape[0]
+    half = rows // 2
+    half_wo = wo_ref.shape[0] // 2
+    planes = Sender(send2, recv2)
+
+    def held(at, offset=0, size=rows):
+        return wall_ref.at[part, pl.ds(pl.multiple_of(lax.rem(at, SIDE) * rows + offset, 16), size)]
+
+    mine = pltpu.make_async_copy(w_ref, held(z), own2.at[0])
+    mine.start()
+    planes.go("up", w_ref, held(z), up)
+    planes.go("down", w_ref, held(z), down)
+    role = lax.rem(z - y + SIDE, SIDE)
+    woown = woall_ref.at[part]
+    first, second = woown.at[pl.ds(0, half_wo)], woown.at[pl.ds(half_wo, half_wo)]
+    rows_mine = pltpu.make_async_copy(wo_ref, woown, own2.at[1])
+    rows_up = planes.make("wo_up", wo_ref, woown, up)
+    rows_down = planes.make("wo_down", wo_ref, woown, down)
+    on_up = planes.make("wo_on_up", first, first, up)
+    on_down = planes.make("wo_on_down", second, second, down)
+    swap_wo = planes.make("swap_wo", woown, woown, other_core())
+
+    @pl.when(role == 0)
+    def _():
+        rows_mine.start()
+        rows_up.start()
+        rows_down.start()
+
+    spread_steps(axis, x_ref, o_ref, send, recv, own)
+
+    planes.arrived("up")
+    planes.go("on_up", held(z + 3, 0, half), held(z + 3, 0, half), up)
+    planes.arrived("down")
+    planes.go("on_down", held(z + 1, half, half), held(z + 1, half, half), down)
+
+    @pl.when(role == 1)
+    def _():
+        rows_up.wait_recv()
+        on_up.start()
+
+    @pl.when(role == 3)
+    def _():
+        rows_down.wait_recv()
+        on_down.start()
+
+    mine.wait()
+    for k, at in enumerate((z, z + 3, z + 1)):
+        planes.go(("swap", k), held(at), held(at), other_core())
+
+    @pl.when(role == 0)
+    def _():
+        rows_mine.wait()
+
+    @pl.when(role == 2)
+    def _():
+        on_up.wait_recv()
+        on_down.wait_recv()
+
+    swap_wo.start()
+    planes.arrived("on_up")
+    planes.arrived("on_down")
+    planes.go(("swap", 3), held(z + 2), held(z + 2), other_core())
+    for k in range(SIDE):
+        planes.arrived(("swap", k))
+    swap_wo.wait_recv()
+
+    @pl.when(role == 0)
+    def _():
+        rows_up.wait_send()
+        rows_down.wait_send()
+
+    @pl.when(role == 1)
+    def _():
+        on_up.wait_send()
+
+    @pl.when(role == 3)
+    def _():
+        on_down.wait_send()
+
+    for name, copy in planes.copies.items():
+        if name not in ("wo_up", "wo_down", "wo_on_up", "wo_on_down"):
+            copy.wait_send()
+
+
+def opening(x, w, wo, axis, call_id):
+    count = lax.axis_size(axis)
+    vmem = pl.BlockSpec(memory_space=pltpu.VMEM)
+    return pl.pallas_call(
+        lambda *refs: opening_kernel(axis, *refs),
+        in_specs=[vmem] * 3,
+        out_specs=[vmem] * 3,
+        out_shape=[
+            jax.ShapeDtypeStruct((count * x.shape[0], x.shape[1]), x.dtype),
+            jax.ShapeDtypeStruct((2, SIDE * w.shape[0], w.shape[1]), w.dtype),
+            jax.ShapeDtypeStruct((2,) + wo.shape, wo.dtype),
+        ],
+        scratch_shapes=[
+            pltpu.SemaphoreType.DMA((40,)), pltpu.SemaphoreType.DMA((40,)),
+            pltpu.SemaphoreType.DMA,
+            pltpu.SemaphoreType.DMA((16,)), pltpu.SemaphoreType.DMA((16,)),
+            pltpu.SemaphoreType.DMA((2,)),
+        ],
+        compiler_params=pltpu.CompilerParams(
+            collective_id=call_id, has_side_effects=True, vmem_limit_bytes=VMEM_ASK
+        ),
+        name="opening",
+    )(x, w, wo)
+
+
+def fold_kernel(
+    gin_ref, gout_ref, small_ref, gin2_ref, gout2_ref, small2_ref,
+    fin_ref, fout_ref, fsmall_ref,
+    land_in, land_out, land_small, sum_in, sum_out, sum_small,
+    far_in, far_out, near_in, near_out, all_small, send, recv,
+):
+    z = lax.axis_index("wshard")
+    up, down = plane_neighbours()
+    across = {"wshard": lax.rem(z + 2, SIDE)}
+    greet([up, down, across, other_core()])
+    out = Sender(send, recv)
+    arrays = (
+        (gin_ref, gin2_ref, land_in, sum_in, far_in, near_in, fin_ref),
+        (gout_ref, gout2_ref, land_out, sum_out, far_out, near_out, fout_ref),
+    )
+
+    def block(ref, d, offset=0, size=None):
+        rows = ref.shape[0] // SIDE
+        start = lax.rem(z + d, SIDE) * rows + offset
+        return pl.ds(pl.multiple_of(start, 16), rows if size is None else size)
+
+    for d in (2, 1, 3, 0):
+        for k, (_, theirs, land, *_) in enumerate(arrays):
+            out.go(("swap", k, d), theirs.at[block(theirs, d)], land.at[block(theirs, d)], other_core())
+    out.go("small", small2_ref, land_small, other_core())
+
+    def add_cores(d):
+        for k, (ours, _, land, total, *_) in enumerate(arrays):
+            out.arrived(("swap", k, d))
+            at = block(ours, d)
+            total[at, :] = (ours[at, :].astype(F32) + land[at, :].astype(F32)).astype(BF16)
+
+    add_cores(2)
+    for k, (_, _, _, total, far, _, _) in enumerate(arrays):
+        half = total.shape[0] // SIDE // 2
+        out.go(("far1", k), total.at[block(total, 2, 0, half)], far.at[0], up)
+        out.go(("far2", k), total.at[block(total, 2, half, half)], far.at[1], down)
+    out.arrived("small")
+    sum_small[...] = small_ref[...] + land_small[...]
+    out.go("small1", sum_small, all_small.at[0], up)
+    out.go("small2", sum_small, all_small.at[1], down)
+    out.go("small3", sum_small, all_small.at[2], across)
+    for side, (d, to) in enumerate(((1, up), (3, down))):
+        add_cores(d)
+        for k, (_, _, _, total, far, near, _) in enumerate(arrays):
+            half = total.shape[0] // SIDE // 2
+            out.arrived((("far1", "far2")[side], k))
+            at = block(total, d, half * side, half)
+            total[at, :] = (total[at, :].astype(F32) + far[side].astype(F32)).astype(BF16)
+            out.go((("near1", "near2")[side], k), total.at[block(total, d)], near.at[side], to)
+    add_cores(0)
+    for k, (_, _, _, total, _, near, done) in enumerate(arrays):
+        out.arrived(("near1", k))
+        out.arrived(("near2", k))
+        done[...] = (
+            total[block(total, 0), :].astype(F32) + near[0].astype(F32) + near[1].astype(F32)
+        ).astype(BF16)
+    for name in ("small1", "small2", "small3"):
+        out.arrived(name)
+    fsmall_ref[...] = sum_small[...] + all_small[0] + all_small[1] + all_small[2]
+    out.sent()
+
+
+def fold(gin, gout, small, gin2, gout2, small2, call_id):
+    vmem = pl.BlockSpec(memory_space=pltpu.VMEM)
+    (a, b), (c, d) = gin.shape, gout.shape
+    return pl.pallas_call(
+        fold_kernel,
+        in_specs=[vmem] * 6,
+        out_specs=[vmem] * 3,
+        out_shape=[
+            jax.ShapeDtypeStruct((a // SIDE, b), BF16),
+            jax.ShapeDtypeStruct((c // SIDE, d), BF16),
+            jax.ShapeDtypeStruct(small.shape, F32),
+        ],
+        scratch_shapes=[
+            pltpu.VMEM((a, b), BF16), pltpu.VMEM((c, d), BF16), pltpu.VMEM(small.shape, F32),
+            pltpu.VMEM((a, b), BF16), pltpu.VMEM((c, d), BF16), pltpu.VMEM(small.shape, F32),
+            pltpu.VMEM((2, a // SIDE // 2, b), BF16), pltpu.VMEM((2, c // SIDE // 2, d), BF16),
+            pltpu.VMEM((2, a // SIDE, b), BF16), pltpu.VMEM((2, c // SIDE, d), BF16),
+            pltpu.VMEM((3,) + small.shape, F32),
+            pltpu.SemaphoreType.DMA((24,)), pltpu.SemaphoreType.DMA((24,)),
+        ],
+        compiler_params=pltpu.CompilerParams(
+            collective_id=call_id, has_side_effects=True, vmem_limit_bytes=VMEM_ASK
+        ),
+        name="fold",
+    )(gin, gout, small, gin2, gout2, small2)
+
+
+def exchange_kernel(axis, count, x_ref, o_ref, landing, send, recv):
+    me = lax.axis_index(axis)
+    rows = o_ref.shape[0]
+    greet([{axis: lax.rem(me + d, count)} for d in range(1, count)])
+    out = Sender(send, recv)
+
+    def block(j):
+        return pl.ds(pl.multiple_of(j * rows, 16), rows)
+
+    for d in range(1, count):
+        to = lax.rem(me + d, count)
+        out.go(d, x_ref.at[block(to)], landing.at[d], {axis: to})
+    total = x_ref[block(me), :].astype(F32)
+    for d in range(1, count):
+        out.arrived(d)
+        total = total + landing[d].astype(F32)
+    o_ref[...] = total.astype(BF16)
+    out.sent()
+
+
+def exchange(x, axis, call_id):
+    count = lax.axis_size(axis)
+    rows = x.shape[0] // count
+    vmem = pl.BlockSpec(memory_space=pltpu.VMEM)
+    return pl.pallas_call(
+        lambda *refs: exchange_kernel(axis, count, *refs),
+        in_specs=[vmem],
+        out_specs=vmem,
+        out_shape=jax.ShapeDtypeStruct((rows, x.shape[1]), BF16),
+        scratch_shapes=[
+            pltpu.VMEM((count, rows, x.shape[1]), x.dtype),
+            pltpu.SemaphoreType.DMA((count,)), pltpu.SemaphoreType.DMA((count,)),
+        ],
+        compiler_params=pltpu.CompilerParams(
+            collective_id=call_id, has_side_effects=True, vmem_limit_bytes=VMEM_ASK
+        ),
+        name="exchange",
+    )(x)
+
+
+def assemble_kernel(inner, all_ref, gin_ref, gout_ref, steps):
+    count = all_ref.shape[0]
+    for j in range(count):
+        gin_ref[:, j * HC : (j + 1) * HC] = all_ref[j, 0:256, 0:HC].astype(F32)
+        gin_ref[:, inner + j * HC : inner + (j + 1) * HC] = all_ref[j, 0:256, HC:].astype(F32)
+        gin_ref[j * 16 : (j + 1) * 16, 2 * inner : 2 * inner + 2 * NS] = all_ref[
+            j, 256:272, :
+        ].astype(F32)
+        steps[2 * j : 2 * j + 2, :] = all_ref[j, 272:288, :].astype(F32)[0:2, :]
+        big, small = j % SIDE, j // SIDE
+        for c in range(4):
+            gout_ref[big * HC + small * 32 : big * HC + small * 32 + 32, c * 256 : (c + 1) * 256] = (
+                all_ref[j, 288 + 32 * c : 320 + 32 * c, :].astype(F32)
+            )
+    gin_ref[:, 2 * inner + 2 * NS :] = steps[...].T
+
+
+def assemble(everyone, inner, columns, width):
+    return pl.pallas_call(
+        lambda *refs: assemble_kernel(inner, *refs),
+        in_specs=[pl.BlockSpec(memory_space=pltpu.VMEM)],
+        out_specs=[pl.BlockSpec(memory_space=pltpu.VMEM)] * 2,
+        out_shape=[
+            jax.ShapeDtypeStruct((256, columns), F32), jax.ShapeDtypeStruct((512, width), F32)
+        ],
+        scratch_shapes=[pltpu.VMEM((2 * everyone.shape[0], 256), F32)],
+        compiler_params=pltpu.CompilerParams(vmem_limit_bytes=VMEM_ASK),
+        name="assemble",
+    )(everyone)
 
 
 def rms_scale(values, gain):
@@ -493,12 +959,16 @@
     out_rows = out_proj.shape[1]
     per_plane = out_rows // HC
     wo = lax.dynamic_slice_in_dim(out_proj[0], lax.rem(q, per_plane) * HC, HC, 0)
-    both = ("section", "wshard")
-    w_all = lax.all_gather(w, both, axis=0, tiled=True).reshape(2, width, PC)
-    wo_all = lax.all_gather(wo, both, axis=0).reshape(2, n_z, HC, width)
-    wo_all = lax.dynamic_index_in_dim(wo_all, q // per_plane, 1, keepdims=False)
     small = jnp.concatenate([cw.ravel(), cb, vec.ravel(), pre])
     small_all = lax.all_gather(small, "section", axis=0)
+    doc = lax.dynamic_index_in_dim(doc_ids[:, 0], part, 0, keepdims=False)
+    mask, docr = document_masks(doc)
+    u = lax.dynamic_index_in_dim(block_input[:, 0], part, 0, keepdims=False).astype(F32)
+    cot = lax.dynamic_index_in_dim(out_grad[:, 0], part, 0, keepdims=False).astype(F32)
+
+    n, w_all, wo_all = opening(
+        rms_scale(u, small_all[0][-width:]).astype(BF16), w, wo, "seq", 1
+    )
     layers = []
     for l in (0, 1):
         s = small_all[l]
@@ -507,15 +977,11 @@
         vecl = jnp.concatenate([s[at : at + 4 * HC].reshape(4, HC), jnp.zeros((4, HC), F32)])
         layers.append((w_all[l], wo_all[l], cwl, vecl, s[at + 4 * HC :]))
 
-    doc = lax.dynamic_index_in_dim(doc_ids[:, 0], part, 0, keepdims=False)
-    mask, docr = document_masks(doc)
-    u = lax.dynamic_index_in_dim(block_input[:, 0], part, 0, keepdims=False).astype(F32)
-    cot = lax.dynamic_index_in_dim(out_grad[:, 0], part, 0, keepdims=False).astype(F32)
-
     inputs, normed, saved, hidden = [], [], [], []
     for l in (0, 1):
         inputs.append(u)
-        n = spread(rms_scale(u, layers[l][4]).astype(BF16), "seq", 1)
+        if l == 1:
+            n = spread(rms_scale(u, layers[l][4]).astype(BF16), "seq", 5)
         normed.append(n)
         u, s = forward_layer(
             u, n, layers[l], mask, docr, inner, lambda x: collect(x, "seq", 2)
@@ -549,78 +1015,50 @@
     hidden_out = by_layer(hidden)
     grads_out = by_layer(grads_in)
 
-    def sent_and_summed(x, axis):
-        arrived = lax.all_to_all(x, axis, split_axis=0, concat_axis=0, tiled=True)
-        return arrived.astype(F32).sum(axis=0)
-
+    def packed(g):
+        gin, gout, gsmall, g_pre = g
+        pre_rows = jnp.pad(g_pre, (0, 8 * 3 * HC - width)).reshape(8, 3 * HC)
+        return gin.astype(BF16), gout.astype(BF16), jnp.concatenate([gsmall, pre_rows])
+
+    pair = [packed(g) for g in grads]
+    mine = [jnp.where(part == 0, a, b) for a, b in zip(*pair)]
+    other = [jnp.where(part == 0, b, a) for a, b in zip(*pair)]
+    gin, gout, gsmall = fold(*mine, *other, 6)
     n_rows = width // n_z
-    gin = jnp.stack([grads[0][0], grads[1][0]]).astype(BF16).reshape(2 * n_z, n_rows * PC)
-    gout = jnp.stack([grads[0][1], grads[1][1]]).astype(BF16).reshape(2 * n_z, -1)
-    piece = HC // n_z
-    summed = sent_and_summed(jnp.concatenate([gin, gout], axis=1), both)
-    gin = summed[: n_rows * PC].reshape(n_rows, PC)
-    gout = summed[n_rows * PC :].reshape(piece, width).astype(BF16)
-    n_y = n_seq // per_plane
     route = []
-    for y in range(n_y):
-        for x in range(per_plane):
-            for z in range(n_z):
-                route.append(((y * per_plane + x) * n_z + z, (z * per_plane + x) * n_z + y))
+    for y in range(SIDE):
+        for x in range(SIDE):
+            for z in range(SIDE):
+                route.append(((y * SIDE + x) * n_z + z, (z * SIDE + x) * n_z + y))
     gout = lax.ppermute(gout, ("seq", "wshard"), route)
-    g_bc = gin[:, 2 * HC : 4 * HC].astype(BF16).reshape(n_seq, -1)
-    g_bc = sent_and_summed(g_bc, "seq").astype(BF16)
-    g_own = jnp.concatenate([gin[:, : 2 * HC], gin[:, 4 * HC :: HEAD]], axis=1).astype(BF16)
-    flat = jnp.concatenate([g_own.ravel(), g_bc, gout.ravel()])
-    everyone = lax.all_gather(flat, "seq", axis=0)
-    own = everyone[:, : g_own.size].reshape(n_seq, n_rows, -1)
-    own = jnp.moveaxis(own, 0, 1).astype(F32)
-    shard_in = jnp.concatenate(
-        [
-            own[:, :, :HC].reshape(n_rows, -1),
-            own[:, :, HC : 2 * HC].reshape(n_rows, -1),
-            everyone[:, g_own.size : g_own.size + g_bc.size].reshape(n_rows, -1).astype(F32),
-            own[:, :, 2 * HC :].reshape(n_rows, -1),
-        ],
-        axis=1,
-    )
-    shard_out = everyone[:, g_own.size + g_bc.size :].reshape(n_z, per_plane, piece, width)
-    shard_out = jnp.moveaxis(shard_out, 0, 1).reshape(out_rows, width).astype(F32)
-
-    def placed(values, extent, start):
-        full = jnp.zeros(values.shape[:-1] + (extent,), F32)
-        return lax.dynamic_update_slice_in_dim(full, values, start, values.ndim - 1)
-
-    def small_vector(g):
-        _, _, s, g_pre = g
-        conv = jnp.concatenate([placed(s[:5, :HC], inner, q * HC), s[:5, HC:]], axis=1)
-        per_head = jnp.stack([
-            s[6, 0:HC:HEAD],
-            s[6, HC : 2 * HC : HEAD],
-            s[5, HC : 2 * HC].reshape(-1, HEAD).sum(axis=1),
-        ])
-        return jnp.concatenate([
-            conv.ravel(), placed(per_head, heads, 2 * q).ravel(), g_pre,
-            placed(s[5, :HC], inner, q * HC),
-        ])
-
-    vectors = [small_vector(g) for g in grads]
-    mine = jnp.where(part == 0, vectors[0], vectors[1])
-    mine = mine + swap(jnp.where(part == 0, vectors[1], vectors[0]))
-    sums = lax.psum(mine, ("seq", "wshard"))
-    channels = conv_weight.shape[2]
-    at = 0
-    pieces = []
-    for shape in (
-        conv_weight.shape[1:], (channels,), (heads,), (heads,), (heads,), (width,), (inner,)
-    ):
-        size = 1
-        for extent in shape:
-            size *= extent
-        pieces.append(sums[at : at + size].reshape((1,) + shape))
-        at += size
+    g_bc = exchange(gin[:, 2 * HC : 4 * HC], "seq", 7)
+    g_dt = jnp.pad(gin[:, 4 * HC :: HEAD].T, ((0, 14), (0, 0)))
+    smalls = [t.reshape(-1, 256) for t in three(gsmall)]
+    block = [gin[:, : 2 * HC], g_bc, g_dt] + [gout[:, c : c + 256] for c in range(0, width, 256)]
+    block = jnp.concatenate(block + smalls)
+    used = block.shape[0]
+    size = -(-used // 64) * 64
+    everyone = spread(jnp.pad(block, ((0, size - used), (0, 0))), "seq", 8)
+    everyone = everyone.reshape(n_seq, size, 256)
+    shard_in, shard_out = assemble(everyone, inner, in_proj.shape[2], width)
+
+    third = smalls[0].shape[0]
+    small = sum(
+        everyone[:, used - third * (3 - k) : used - third * (2 - k)].astype(F32) for k in range(3)
+    ).reshape(n_seq, 16, 3 * HC)
+    conv_x = jnp.moveaxis(small[:, :5, :HC], 0, 1).reshape(5, inner)
+    conv = jnp.concatenate([conv_x, small[:, :5, HC:].sum(axis=0)], axis=1)
+    pieces = [
+        conv[:4], conv[4],
+        small[:, 6, 0:HC:HEAD].reshape(heads),
+        small[:, 6, HC : 2 * HC : HEAD].reshape(heads),
+        small[:, 5, HC : 2 * HC].reshape(heads, HEAD).sum(axis=1),
+        small[:, 8:].sum(axis=0).reshape(-1)[:width],
+        small[:, 5, :HC].reshape(inner),
+    ]
     return (
         hidden_out[None, :, None], grads_out[None, :, None], shard_in[None], shard_out[None],
-        *pieces,
+        *[p[None] for p in pieces],
     )
 
 

time: 921 us -> 353 us (0.38)
  blocking collectives: 389 us -> 1.82 us
  Pallas kernels: 352 us -> 274 us
  local copies, waits for them, and re-layouts: 102 us -> 58.3 us
  other arithmetic: 40.8 us -> 15.2 us
  between operations: 15.2 us -> 1.6 us
  waiting for transfers between devices: 10.1 us -> 0.01 us
    psum x1 -> x0, blocking collectives: 345 us -> none  [body(): sums = lax.psum(mine, ('seq', 'wshard'))]
    pallas_call x8 -> x12, Pallas kernels: 302 us -> 223 us  [the longest x4 83.3 us: spread(): pl.pallas_call(lambda *refs: spread_kernel(axis, *refs), in_specs=[pl.Blo...]
    all_to_all x1 -> x0, blocking collectives: 41.6 us -> none  [sent_and_summed(): arrived = lax.all_to_all(x, axis, split_axis=0, concat_axis=0, tiled=True)]
    slice x21 -> x5, local copies, waits for them, and re-layouts: 16.9 us -> 0.83 us  [the longest x1 0.6 us: body(): small[:, 8:].sum(axis=0).reshape(-1)[:width]]
    convert_element_type x8 -> x0, local copies, waits for them, and re-layouts: 14.9 us -> none  [the longest x1 9.19 us: body(): own = jnp.moveaxis(own, 0, 1).astype(F32)]
    unnamed x152 -> x115, local copies, waits for them, and re-layouts: 50.7 us -> 40.6 us
  transfers between devices with their start and end apart: 8 -> 3, of which waited for: 3 -> 0; matrix products, arithmetic and copies ran while one was open for 3% -> 6% of each run, Pallas kernels for 9% -> 48%
where the time goes in v2:
time: 353 us; the launch traced here: 352 us
  Pallas kernels  274 us (78%)
  local copies, waits for them, and re-layouts  58.3 us (17%)
  other arithmetic  15.2 us (4%)
    pallas_call x4, Pallas kernels, spread(): pl.pallas_call(lambda *refs: spread_kernel(axis, *refs), in_specs=[pl.Blo...  83.3 us
    pallas_call x4, Pallas kernels, collect(): pl.pallas_call(lambda *refs: collect_kernel(axis, *refs), in_specs=[pl.Bl...  73.5 us
    unnamed x115, local copies, waits for them, and re-layouts  40.6 us
    pallas_call x2, Pallas kernels, backward_core(): pl.pallas_call(bwd_kernel, grid=(blocks,), in_specs=[rows(width + AUX), r...  33 us
    pallas_call x1, Pallas kernels, opening(): pl.pallas_call(lambda *refs: opening_kernel(axis, *refs), in_specs=[vmem]...  30.2 us
    pallas_call x1, Pallas kernels, fold(): pl.pallas_call(fold_kernel, in_specs=[vmem] * 6, out_specs=[vmem] * 3, ou...  20.2 us
    pallas_call x2, Pallas kernels, forward_core(): pl.pallas_call(fwd_kernel, grid=(blocks,), in_specs=[rows(width), whole(w...  17.3 us
    pallas_call x1, Pallas kernels, exchange(): pl.pallas_call(lambda *refs: exchange_kernel(axis, count, *refs), in_spec...  12.9 us
  transfers between devices with their start and end apart: 3, of which 0 were waited for; matrix products, arithmetic and copies ran while one was open for 6% of the time, Pallas kernels for 48%

profile of v2, /device:TPU:0, one launch (start us, length us, event | category | flops | bytes accessed | tf_op | source)
XLA Modules:
  0.0 352.0 jit_solution(13306635846203044638)
XLA Ops:
  0.7 1.3 constant_dynamic-slice_fusion
  10.3 1.8 all-gather.1
  12.2 1.0 fusion.7
  13.3 4.2 %copy.94 = bf16[1,256,4384]{2,1,0:T(8,128)(2,1)} copy(bf16[1,256,4384]{1,2,0:T(8,128)(2,1)} %param.15) | data formatting | bytes 4489216 | tf_op args[3]
  19.3 0.9 constant_dynamic-slice_fusion.4
  20.8 0.9 slice.226
  21.9 30.2 %opening.1 = (bf16[1024,1024]{1,0:T(8,128)(2,1)S(1)}, bf16[2,1024,640]{2,1,0:T(8,128)(2,1)S(1)}, bf16[2,128,1024]{2,1,0:T(8,128)(2,1)S(1)}) custom-call(bf16[64,1024]{1,0:T(8,128)(2,1)S(1)} %fusion.2.refs_0_, bf16[256,640]{1,0:T(8,128)(2,1)S(1)} %pad_maximum_fusion.refs_1_, bf16[128,1024]{1,0:T(8,128)(2,1)S(1)} %dynamic-slice_bitcast_fusion.refs_2_), custom_call_target="tpu_custom_call" | custom-call | tf_op jit(solution)/shard_map/opening/pallas_call | solution.py:697
  52.2 1.5 slice_bitcast_fusion
  54.0 8.7 %forward_core.2 = (bf16[1024,1152]{1,0:T(8,128)(2,1)}, f32[4,264,384]{2,1,0:T(8,128)S(1)}, f32[1024,128]{1,0:T(8,128)S(1)}, f32[1024,128]{1,0:T(8,128)S(1)}, bf1...) custom-call(bf16[1024,1024]{1,0:T(8,128)(2,1)} %copy-done.9, ...), custom_call_target="tpu_custom_call" | custom-call | tf_op jit(solution)/shard_map/forward_core/pallas_call | solution.py:153
  62.6 1.2 copy-done.14
  65.4 2.1 copy-done.10
  67.5 19.8 %collect.4 = f32[64,1152]{1,0:T(8,128)S(1)} custom-call(bf16[1024,1152]{1,0:T(8,128)(2,1)S(1)} %copy-done.10), custom_call_target="tpu_custom_call" | custom-call | tf_op jit(solution)/shard_map/collect/pallas_call | solution.py:535
  87.8 18.0 %spread.4.n_ref = bf16[1024,1024]{1,0:T(8,128)(2,1)S(1)} custom-call(bf16[64,1024]{1,0:T(8,128)(2,1)S(1)} %multiply_convert_fusion.refs_0_), custom_call_target="tpu_custom_call" | custom-call | tf_op jit(solution)/shard_map/spread/pallas_call | solution.py:426
  105.9 1.3 copy-done.4
  107.2 1.3 copy-done.5
  108.5 8.6 %forward_core.3 = (bf16[1024,1152]{1,0:T(8,128)(2,1)}, f32[4,264,384]{2,1,0:T(8,128)S(1)}, f32[1024,128]{1,0:T(8,128)S(1)}, f32[1024,128]{1,0:T(8,128)S(1)}, bf1...) custom-call(bf16[1024,1024]{1,0:T(8,128)(2,1)} %copy-done.4, ...), custom_call_target="tpu_custom_call" | custom-call | tf_op jit(solution)/shard_map/forward_core/pallas_call | solution.py:153
  117.1 1.2 copy-done.15
  119.8 2.1 copy-done.11
  121.9 18.1 %collect.5 = f32[64,1152]{1,0:T(8,128)S(1)} custom-call(bf16[1024,1152]{1,0:T(8,128)(2,1)S(1)} %copy-done.11), custom_call_target="tpu_custom_call" | custom-call | tf_op jit(solution)/shard_map/collect/pallas_call | solution.py:535
  140.3 1.9 fusion.4
  142.6 1.0 concatenate.78.refs_0_
  143.7 20.4 %spread.5.c_ref = bf16[1024,1152]{1,0:T(8,128)(2,1)S(1)} custom-call(bf16[64,1152]{1,0:T(8,128)(2,1)S(1)} %concatenate.78.refs_0_), custom_call_target="tpu_custom_call" | custom-call | tf_op jit(solution)/shard_map/spread/pallas_call | solution.py:426
  164.1 1.4 copy-done.8
  165.5 1.3 copy-done.6
  166.8 1.0 copy-done.23
  167.9 16.4 %backward_core.2 = (bf16[1024,1024]{1,0:T(8,128)(2,1)}, f32[1024,640]{1,0:T(8,128)}, f32[128,1024]{1,0:T(8,128)S(1)}, f32[8,384]{1,0:T(8,128)S(1)}) custom-call(bf16[1024,1152]{1,0:T(8,128)(2,1)} %copy-done.8, bf16[1024,1024]{1,0:T(8,128)(2,1)} %copy-done.4, bf16[1024,640]{1,0:T(8,128)(2,1)S(1)} %copy-done.6, ...), custom_call_target="tpu_custom_call" | custom-call | tf_op jit(solution)/shard_map/backward_core/pallas_call | solution.py:302
  184.3 1.8 copy-done.13
  186.0 17.9 %collect.6 = f32[64,1024]{1,0:T(8,128)S(1)} custom-call(bf16[1024,1024]{1,0:T(8,128)(2,1)S(1)} %copy-done.13), custom_call_target="tpu_custom_call" | custom-call | tf_op jit(solution)/shard_map/collect/pallas_call | solution.py:535
  204.2 1.0 multiply_reduce_fusion.1
  205.3 1.0 concatenate.79.refs_0_
  206.3 18.1 %spread.6.c_ref = bf16[1024,1152]{1,0:T(8,128)(2,1)S(1)} custom-call(bf16[64,1152]{1,0:T(8,128)(2,1)S(1)} %concatenate.79.refs_0_), custom_call_target="tpu_custom_call" | custom-call | tf_op jit(solution)/shard_map/spread/pallas_call | solution.py:426
  224.4 1.4 copy-done.7
  225.8 1.0 copy-done.19
  226.9 1.0 copy-done.21
  227.9 0.9 copy-done.33
  228.9 0.9 copy-done.35
  229.8 16.6 %backward_core.3 = (bf16[1024,1024]{1,0:T(8,128)(2,1)}, f32[1024,640]{1,0:T(8,128)}, f32[128,1024]{1,0:T(8,128)S(1)}, f32[8,384]{1,0:T(8,128)S(1)}) custom-call(bf16[1024,1152]{1,0:T(8,128)(2,1)} %copy-done.7, bf16[1024,1024]{1,0:T(8,128)(2,1)} %copy-done.9, bf16[1024,640]{1,0:T(8,128)(2,1)S(1)} %get-tuple-element.148.w_ref, ...), custom_call_target="tpu_custom_call" | custom-call | tf_op jit(solution)/shard_map/backward_core/pallas_call | solution.py:302
  246.4 1.8 copy-done.12
  248.2 17.7 %collect.7 = f32[64,1024]{1,0:T(8,128)S(1)} custom-call(bf16[1024,1024]{1,0:T(8,128)(2,1)S(1)} %copy-done.12), custom_call_target="tpu_custom_call" | custom-call | tf_op jit(solution)/shard_map/collect/pallas_call | solution.py:535
  266.2 2.9 broadcast_select_fusion
  269.3 20.2 %fold.1 = (bf16[256,640]{1,0:T(8,128)(2,1)S(1)}, bf16[32,1024]{1,0:T(8,128)(2,1)S(1)}, f32[16,384]{1,0:T(8,128)S(1)}) custom-call(bf16[1024,640]{1,0:T(8,128)(2,1)S(1)} %get-tuple-element.146.gin_ref, bf16[128,1024]{1,0:T(8,128)(2,1)S(1)} %get-tuple-element.152.gout_ref, f32[16,384]{1,0:T(8,128)S(1)} %get-tuple-element.170.small_ref, ...), custom_call_target="tpu_custom_call" | custom-call | tf_op jit(solution)/shard_map/fold/pallas_call | solution.py:785
  291.2 12.9 %exchange.1 = bf16[16,256]{1,0:T(8,128)(2,1)S(1)} custom-call(bf16[256,256]{1,0:T(8,128)(2,1)S(1)} %get-tuple-element.161.refs_0_), custom_call_target="tpu_custom_call" | custom-call | tf_op jit(solution)/shard_map/exchange/pallas_call | solution.py:833
  304.2 26.8 %spread.7 = bf16[8192,256]{1,0:T(8,128)(2,1)S(1)} custom-call(bf16[512,256]{1,0:T(8,128)(2,1)S(1)} %pad.52.refs_0_), custom_call_target="tpu_custom_call" | custom-call | tf_op jit(solution)/shard_map/spread/pallas_call | solution.py:426
  331.2 2.0 copy-done.2
  334.8 2.2 copy-done.3
  337.0 3.2 assemble.1
  343.3 6.0 %copy.106 = f32[1,256,4384]{1,2,0:T(8,128)} copy(f32[1,256,4384]{2,1,0:T(8,128)} %bitcast.112) | data formatting | bytes 8978432
  349.2 1.9 maximum_select_fusion
  (202 shorter events, 23.3 us)
Async XLA Ops:
  0.6 21.2 %copy-start = (bf16[1,512,1024]{2,1,0:T(8,128)(2,1)S(1)}, bf16[1,512,1024]{2,1,0:T(8,128)(2,1)}, u32[]{:S(2)}) copy-start(bf16[1,512,1024]{2,1,0:T(8,128)(2,1)} %param.16) | copy-start | bytes 3145732
  13.2 8.5 %copy-start.42 = (bf16[2,1,64,1024]{3,2,1,0:T(8,128)(2,1)S(1)}, bf16[2,1,64,1024]{3,2,1,0:T(8,128)(2,1)}, u32[]{:S(2)}) copy-start(bf16[2,1,64,1024]{3,2,1,0:T(8,128)(2,1)} %param.12) | copy-start | bytes 786436
  52.2 1.8 copy-start.9
  62.6 1.2 copy-start.14
  63.9 0.8 copy-start.16
  65.4 21.9 %copy-start.18 = (f32[1024,128]{1,0:T(8,128)}, f32[1024,128]{1,0:T(8,128)S(1)}, u32[]{:S(2)}) copy-start(f32[1024,128]{1,0:T(8,128)S(1)} %get-tuple-element.55.dt_ref) | copy-start | bytes 1572868
  65.4 22.0 %copy-start.20 = (f32[1024,128]{1,0:T(8,128)}, f32[1024,128]{1,0:T(8,128)S(1)}, u32[]{:S(2)}) copy-start(f32[1024,128]{1,0:T(8,128)S(1)} %get-tuple-element.57.scan_ref) | copy-start | bytes 1572868
  65.4 22.0 %copy-start.32 = (bf16[1024,128]{1,0:T(8,128)(2,1)}, bf16[1024,128]{1,0:T(8,128)(2,1)S(1)}, u32[]{:S(2)}) copy-start(bf16[1024,128]{1,0:T(8,128)(2,1)S(1)} %get-tuple-element.56.mix_ref) | copy-start | bytes 786436
  65.4 2.1 copy-start.10
  87.7 52.5 %copy-start.40 = (f32[64,1024]{1,0:T(8,128)}, f32[64,1024]{1,0:T(8,128)S(1)}, u32[]{:S(2)}) copy-start(f32[64,1024]{1,0:T(8,128)S(1)} %get-tuple-element.142) | copy-start | bytes 786436
  105.8 1.3 copy-start.4
  107.2 1.3 copy-start.5
  117.1 1.2 copy-start.15
  118.3 0.8 copy-start.22
  119.8 20.2 %copy-start.24 = (f32[1024,128]{1,0:T(8,128)}, f32[1024,128]{1,0:T(8,128)S(1)}, u32[]{:S(2)}) copy-start(f32[1024,128]{1,0:T(8,128)S(1)} %get-tuple-element.48.dt_ref) | copy-start | bytes 1572868
  119.8 20.4 %copy-start.26 = (f32[1024,128]{1,0:T(8,128)}, f32[1024,128]{1,0:T(8,128)S(1)}, u32[]{:S(2)}) copy-start(f32[1024,128]{1,0:T(8,128)S(1)} %get-tuple-element.50.scan_ref) | copy-start | bytes 1572868
  119.8 20.4 %copy-start.38 = (f32[4,128,128]{2,1,0:T(8,128)}, f32[4,128,128]{2,1,0:T(8,128)S(1)}, u32[]{:S(2)}) copy-start(f32[4,128,128]{2,1,0:T(8,128)S(1)} %get-tuple-element.51.st_ref) | copy-start | bytes 786436
  119.8 2.1 copy-start.11
  142.2 23.3 %copy-start.25 = (f32[1024,128]{1,0:T(8,128)S(1)}, f32[1024,128]{1,0:T(8,128)}, u32[]{:S(2)}) copy-start(f32[1024,128]{1,0:T(8,128)} %copy-done.24) | copy-start | bytes 1572868
  142.2 207.0 %collective-permute-start = (f32[64,1024]{1,0:T(8,128)}, f32[64,1024]{1,0:T(8,128)}, u32[]{:S(2)}, u32[]{:S(2)}) collective-permute-start(f32[64,1024]{1,0:T(8,128)} %get-tuple-element.163), channel_id=1, source_target_pairs={{0,64},{64,0},{1,65},{65,1},{2,66},{66,2},{3,67},{67,3},{4,68},{68... | collective-permute-start | bytes 786440 | tf_op jit(solution)/shard_map/ppermute | solution.py:1008
  143.6 21.9 %copy-start.27 = (f32[1024,128]{1,0:T(8,128)S(1)}, f32[1024,128]{1,0:T(8,128)}, u32[]{:S(2)}) copy-start(f32[1024,128]{1,0:T(8,128)} %copy-done.26) | copy-start | bytes 1572868
  143.7 21.9 %copy-start.37 = (bf16[1024,128]{1,0:T(8,128)(2,1)S(1)}, bf16[1024,128]{1,0:T(8,128)(2,1)}, u32[]{:S(2)}) copy-start(bf16[1024,128]{1,0:T(8,128)(2,1)} %copy-done.36) | copy-start | bytes 786436
  143.7 21.9 %copy-start.39 = (f32[4,128,128]{2,1,0:T(8,128)S(1)}, f32[4,128,128]{2,1,0:T(8,128)}, u32[]{:S(2)}) copy-start(f32[4,128,128]{2,1,0:T(8,128)} %copy-done.38) | copy-start | bytes 786436
  164.1 1.4 copy-start.8
  165.5 1.3 copy-start.6
  166.8 1.0 copy-start.23
  184.3 20.9 %copy-start.28 = (f32[128,1024]{1,0:T(8,128)}, f32[128,1024]{1,0:T(8,128)S(1)}, u32[]{:S(2)}) copy-start(f32[128,1024]{1,0:T(8,128)S(1)} %get-tuple-element.63) | copy-start | bytes 1572868
  184.3 1.8 copy-start.13
  186.0 17.9 %copy-start.41 = (f32[64,1024]{1,0:T(8,128)S(1)}, f32[64,1024]{1,0:T(8,128)}, u32[]{:S(2)}) copy-start(f32[64,1024]{1,0:T(8,128)} %copy-done.40) | copy-start | bytes 786436
  186.0 18.1 %copy-start.44 = (bf16[64,1024]{1,0:T(8,128)(2,1)S(1)}, bf16[64,1024]{1,0:T(8,128)(2,1)}, u32[]{:S(2)}) copy-start(bf16[64,1024]{1,0:T(8,128)(2,1)} %get-tuple-element.138) | copy-start | bytes 393220
  204.1 21.7 %copy-start.17 = (f32[1024,128]{1,0:T(8,128)S(1)}, f32[1024,128]{1,0:T(8,128)}, u32[]{:S(2)}) copy-start(f32[1024,128]{1,0:T(8,128)} %copy-done.16) | copy-start | bytes 1572868
  224.4 1.4 copy-start.7
  225.8 1.0 copy-start.19
  226.9 1.0 copy-start.21
  227.9 0.9 copy-start.33
  228.9 0.9 copy-start.35
  246.4 19.5 %copy-start.30 = (f32[128,1024]{1,0:T(8,128)}, f32[128,1024]{1,0:T(8,128)S(1)}, u32[]{:S(2)}) copy-start(f32[128,1024]{1,0:T(8,128)S(1)} %get-tuple-element.62) | copy-start | bytes 1572868
  246.4 1.8 copy-start.12
  248.2 17.8 %copy-start.43 = (bf16[2,1,64,1024]{3,2,1,0:T(8,128)(2,1)S(1)}, bf16[2,1,64,1024]{3,2,1,0:T(8,128)(2,1)}, u32[]{:S(2)}) copy-start(bf16[2,1,64,1024]{3,2,1,0:T(8,128)(2,1)} %param.12) | copy-start | bytes 786436
  266.2 3.0 copy-start.29
  266.2 3.0 copy-start.31
  269.1 21.0 %copy-start.46 = (f32[64,1024]{1,0:T(8,128)S(1)}, f32[64,1024]{1,0:T(8,128)}, u32[]{:S(2)}) copy-start(f32[64,1024]{1,0:T(8,128)} %get-tuple-element.134) | copy-start | bytes 786436
  289.4 14.7 %collective-permute-start.2 = (bf16[32,1024]{1,0:T(8,128)(2,1)S(1)}, bf16[32,1024]{1,0:T(8,128)(2,1)S(1)}, u32[]{:S(2)}, u32[]{:S(2)}) collective-permute-start(bf16[32,1024]{1,0:T(8,128)(2,1)S(1)} %get-tuple-element.67), channel_id=1, source_target_pairs={{0,0},{1,16},{2,32},{3,48},{4,4},{5,20},{6,36},{7,52},{8,8},{9,24}... | collective-permute-start | bytes 196616 | tf_op jit(solution)/shard_map/ppermute | solution.py:1033
  290.3 60.8 %collective-permute-start.1 = (f32[64,1024]{1,0:T(8,128)S(1)}, f32[64,1024]{1,0:T(8,128)S(1)}, u32[]{:S(2)}, u32[]{:S(2)}) collective-permute-start(f32[64,1024]{1,0:T(8,128)S(1)} %get-tuple-element.154), channel_id=1, source_target_pairs={{0,64},{64,0},{1,65},{65,1},{2,66},{66,2},{3,67},{67,3},{4,68},{68... | collective-permute-start | bytes 786440 | tf_op jit(solution)/shard_map/ppermute | solution.py:1008
  331.2 2.0 copy-start.2
  334.8 2.2 copy-start.3
  343.3 6.0 %copy-start.45 = (f32[1,1,1,64,1024]{4,3,2,1,0:T(8,128)S(1)}, f32[1,1,1,64,1024]{4,3,2,1,0:T(8,128)}, u32[]{:S(2)}) copy-start(f32[1,1,1,64,1024]{4,3,2,1,0:T(8,128)} %get-tuple-element.164) | copy-start | bytes 786436
  343.3 8.7 %copy-start.1 = (bf16[1,512,1024]{2,1,0:T(8,128)(2,1)S(1)}, bf16[1,512,1024]{2,1,0:T(8,128)(2,1)}, u32[]{:S(2)}) copy-start(bf16[1,512,1024]{2,1,0:T(8,128)(2,1)} %param.16) | copy-start | bytes 3145732
  (2 other events, 1.4 us)

commit v3 on v1

v3 whole, which is shorter than its diff:
```python
import jax
import jax.numpy as jnp
from jax import lax
from jax.experimental import pallas as pl
from jax.experimental.pallas import tpu as pltpu
from jax.sharding import PartitionSpec as P

SPAN = 256
EPS = 1e-05
F32 = jnp.float32
BF16 = jnp.bfloat16
MESH = pl.DeviceIdType.MESH
VMEM_ASK = 48 * 1024 * 1024

HC = 128
NS = 128
WR = 528
AUX = 128
HEAD = 64
SIDE = 4
AXIS = "seq"


def dot_nn(a, b):
    return lax.dot_general(a, b, (((1,), (0,)), ((), ())), preferred_element_type=F32)


def dot_nt(a, b):
    return lax.dot_general(a, b, (((1,), (1,)), ((), ())), preferred_element_type=F32)


def dot_tn(a, b):
    return lax.dot_general(a, b, (((0,), (0,)), ((), ())), preferred_element_type=F32)


def three(x):
    hi = x.astype(BF16)
    rest = x - hi.astype(F32)
    mid = rest.astype(BF16)
    low = (rest - mid.astype(F32)).astype(BF16)
    return hi, mid, low


def exact_left(ones, x):
    hi, mid, low = three(x)
    return dot_nn(ones, hi) + dot_nn(ones, mid) + dot_nn(ones, low)


def exact_right(x, ones):
    hi, mid, low = three(x)
    return dot_nn(hi, ones) + dot_nn(mid, ones) + dot_nn(low, ones)


def iota(shape, dim):
    return lax.broadcasted_iota(jnp.int32, shape, dim)


def sigmoid(x):
    return 1.0 / (1.0 + jnp.exp(-x))


def softplus(x):
    return jnp.maximum(x, 0.0) + jnp.log1p(jnp.exp(-jnp.abs(x)))


def conv_rows(vbuf, con, mask):
    z = vbuf[pl.ds(8, SPAN), :] * con[3:4, :] + con[4:5, :]
    for k in (1, 2, 3):
        z = z + vbuf[pl.ds(8 - k, SPAN), :] * con[3 - k : 4 - k, :] * mask[:, k - 1 : k]
    return z


def block_terms(dt, vec, mask, docr):
    step = softplus(dt + vec[0])
    log_decay = -step * vec[1]
    rows, cols = iota((SPAN, SPAN), 0), iota((SPAN, SPAN), 1)
    lower = rows >= cols
    running = exact_left(lower.astype(F32).astype(BF16), log_decay)
    turned = running.T
    allowed = lower & (mask[:, 8:9] == docr)
    decays = []
    for h in (0, 1):
        gaps = running[:, h * HEAD : h * HEAD + 1] - turned[h * HEAD : h * HEAD + 1, :]
        decays.append(jnp.exp(jnp.where(allowed, gaps, -1e30)))
    reach = jnp.exp(running) * mask[:, 6:7]
    total = running[SPAN - 1 :, :]
    tail = jnp.exp(total - running) * mask[:, 7:8]
    carry = jnp.exp(total) * mask[SPAN - 1 :, 6:7]
    return step, log_decay, decays, reach, tail, carry


def layer_constants(con):
    return con[5:6, :HC], con[5:6, HC : 2 * HC], con[5:6, 2 * HC : 3 * HC], con[6:7, :HC]


def pre_gain_of(con):
    return jnp.concatenate([con[k : k + 1, 3 * HC : 4 * HC] for k in range(8)], axis=1)


def head_ones():
    return (iota((16, HC), 0) == iota((16, HC), 1) // HEAD).astype(F32).astype(BF16)


def head_firsts():
    return (iota((HC, 16), 0) == iota((HC, 16), 1) * HEAD).astype(F32).astype(BF16)


def lanes_of(columns, rows):
    lane = iota((rows, AUX), 1)
    out = jnp.zeros((rows, AUX), F32)
    for k, column in enumerate(columns):
        out = jnp.where(lane == k, column.astype(F32), out)
    return out.astype(BF16)


def fwd_step(i, n_ref, wt_ref, wo_ref, con_ref, mask_ref, docr_ref, kept, part, vbuf, state):
    vh_ref, gate_ref, dt_ref, mix_ref, scan_ref, st_ref = kept

    @pl.when(i == 0)
    def _():
        vbuf[0:8, :] = jnp.zeros((8, 3 * HC), F32)
        state[...] = jnp.zeros_like(state)

    width = wo_ref.shape[2]
    chunk = wt_ref.shape[3]
    mask = mask_ref[...]
    con = con_ref[0]
    vec = layer_constants(con)
    conv = con[:, : 3 * HC]
    proj = dot_nt(n_ref[:, 0:chunk], wt_ref[0, 0])
    for k in range(1, wt_ref.shape[1]):
        proj = proj + dot_nt(n_ref[:, k * chunk : (k + 1) * chunk], wt_ref[0, k])
    gate = proj[:, :HC]
    v = proj[:, HC : 4 * HC].astype(BF16).astype(F32)
    dt = dot_nn(proj[:, 4 * HC :].astype(BF16), head_ones())
    vbuf[8:, :] = v
    z = conv_rows(vbuf, conv, mask)
    vh_ref[0] = vbuf[...]
    vbuf[0:8, :] = v[SPAN - 8 :, :]
    act = z * sigmoid(z)
    xc = act[:, :HC]
    b16 = act[:, HC : 2 * HC].astype(BF16)
    c16 = act[:, 2 * HC :].astype(BF16)
    step, _, decays, reach, tail, carry = block_terms(dt, vec, mask, docr_ref[0:1, :])
    xs = xc * step
    xs16 = xs.astype(BF16)
    scores = dot_nt(c16, b16)
    within = [dot_nn((scores * d).astype(BF16), xs16) for d in decays]
    first = iota((SPAN, HC), 1) < HEAD
    st = state[...]
    st_ref[0] = st
    scan = jnp.where(first, within[0], within[1]) + dot_nn(c16, st.astype(BF16)) * reach
    state[...] = st * carry + dot_tn(b16, (xs * tail).astype(BF16))
    mixed = (scan + xc * vec[2]).astype(BF16)
    g = mixed.astype(F32) * (gate * sigmoid(gate))
    place = pl.ds(pl.multiple_of(i * SPAN, SPAN), SPAN)
    part[place, :width] = dot_nn((g * vec[3]).astype(BF16), wo_ref[0]).astype(BF16)
    part[place, width:] = lanes_of(three(jnp.sum(g * g, axis=1, keepdims=True)), SPAN)
    gate_ref[...] = gate
    dt_ref[...] = dt
    mix_ref[...] = mixed
    scan_ref[...] = scan


def bwd_step(
    i, c_ref, n_ref, wt_ref, wo_ref, con_ref, mask_ref, docr_ref, kept,
    part, gin, gout, small, dzbuf, dstate,
):
    vh_ref, gate_ref, dt_ref, mix_ref, scan_ref, st_ref = kept

    @pl.when(i == 0)
    def _():
        dzbuf[SPAN:, :] = jnp.zeros((8, 3 * HC), F32)
        dstate[...] = jnp.zeros_like(dstate)
        gin[...] = jnp.zeros_like(gin)
        gout[...] = jnp.zeros_like(gout)
        small[...] = jnp.zeros_like(small)

    width = wo_ref.shape[2]
    chunk = wt_ref.shape[3]
    mask = mask_ref[...]
    con = con_ref[0]
    vec = layer_constants(con)
    conv = con[:, : 3 * HC]
    cot = c_ref[:, :width]
    aux = c_ref[:, width:].astype(F32)
    r = aux[:, 0:1] + aux[:, 1:2] + aux[:, 2:3]
    pull = aux[:, 3:4] + aux[:, 4:5]
    gate = gate_ref[...]
    sg = sigmoid(gate)
    silu = gate * sg
    mixed = mix_ref[...].astype(F32)
    g = mixed * silu
    gain = vec[3]
    dy = dot_nt(cot, wo_ref[0])
    gr = g * r
    gout[...] += dot_tn((gr * gain).astype(BF16), cot)
    d_gain = jnp.sum(dy * gr, axis=0, keepdims=True)
    dg = dy * (r * gain) - g * pull
    dm16 = (dg * silu).astype(BF16)
    dm = dm16.astype(F32)
    dgate = dg * mixed * (sg * (1.0 + gate * (1.0 - sg)))

    vbuf = vh_ref.at[0]
    z = conv_rows(vbuf, conv, mask)
    sz = sigmoid(z)
    act = z * sz
    xc = act[:, :HC]
    b16 = act[:, HC : 2 * HC].astype(BF16)
    c16 = act[:, 2 * HC :].astype(BF16)
    dt = dt_ref[...]
    step, log_decay, decays, reach, tail, carry = block_terms(dt, vec, mask, docr_ref[0:1, :])
    xs16 = (xc * step).astype(BF16)
    xs = xs16.astype(F32)
    scores = dot_nt(c16, b16)
    first = iota((SPAN, HC), 1) < HEAD
    zero16 = jnp.zeros((SPAN, HC), BF16)
    dscores = jnp.zeros((SPAN, SPAN), F32)
    dxs = []
    for h in (0, 1):
        own = jnp.where(first, dm16, zero16) if h == 0 else jnp.where(first, zero16, dm16)
        dp = dot_nt(own, xs16)
        dscores = dscores + dp * decays[h]
        dxs.append(dot_tn((scores * decays[h]).astype(BF16), dm16))
    ds16 = dscores.astype(BF16)
    st = st_ref[0]
    dst = dstate[...]
    dst16 = dst.astype(BF16)
    dcs16 = (dm * reach).astype(BF16)
    dc = dot_nn(ds16, b16) + dot_nt(dcs16, st.astype(BF16))
    db = dot_tn(ds16, c16) + dot_nt((xs * tail).astype(BF16), dst16)
    dxs_tail = dot_nn(b16, dst16) * tail
    dxs_all = jnp.where(first, dxs[0], dxs[1]) + dxs_tail
    dstate[...] = dst * carry + dot_tn(c16, dcs16)

    d_total = jnp.sum(xs * dxs_tail, axis=0, keepdims=True) + carry * jnp.sum(
        dst * st, axis=0, keepdims=True
    )
    flow = dm * scan_ref[...] - xs * dxs_all
    rows, cols = iota((SPAN, SPAN), 0), iota((SPAN, SPAN), 1)
    upper = (cols >= rows).astype(F32).astype(BF16)
    flow = exact_left(upper, flow) + d_total
    same_head = ((iota((HC, HC), 0) < HEAD) == (iota((HC, HC), 1) < HEAD)).astype(F32).astype(BF16)
    d_log = exact_right(flow, same_head)
    d_step = exact_right(dxs_all * xc, same_head) - d_log * vec[1]
    d_alog = jnp.sum(d_log * log_decay, axis=0, keepdims=True)
    d_dt = d_step * sigmoid(dt + vec[0])
    d_skip = jnp.sum(dm * xc, axis=0, keepdims=True)
    d_xc = dm * vec[2] + dxs_all * step

    dact = sz * (1.0 + z * (1.0 - sz))
    dzbuf[:SPAN, 0:HC] = d_xc * dact[:, :HC]
    dzbuf[:SPAN, HC : 2 * HC] = db * dact[:, HC : 2 * HC]
    dzbuf[:SPAN, 2 * HC :] = dc * dact[:, 2 * HC :]
    dz = dzbuf[:SPAN, :]
    dv = dz * conv[3:4, :]
    small[3:4, : 3 * HC] += jnp.sum(dz * vbuf[pl.ds(8, SPAN), :], axis=0, keepdims=True)
    small[4:5, : 3 * HC] += jnp.sum(dz, axis=0, keepdims=True)
    for k in (1, 2, 3):
        dv = dv + dzbuf[pl.ds(k, SPAN), :] * conv[3 - k : 4 - k, :] * mask[:, 2 + k : 3 + k]
        small[3 - k : 4 - k, : 3 * HC] += jnp.sum(
            dz * vbuf[pl.ds(8 - k, SPAN), :] * mask[:, k - 1 : k], axis=0, keepdims=True
        )
    dzbuf[SPAN:, :] = dz[:8, :]
    small[5:6, 0:HC] += d_gain
    small[5:6, HC : 2 * HC] += d_skip
    small[6:7, 0:HC] += jnp.sum(d_dt, axis=0, keepdims=True)
    small[6:7, HC : 2 * HC] += d_alog

    gp = jnp.concatenate([dgate.astype(BF16), dv.astype(BF16)], axis=1)
    gdt = dot_nn(d_dt.astype(BF16), head_firsts()).astype(BF16)
    wide = 4 * HC
    place = pl.ds(pl.multiple_of((pl.num_programs(0) - 1 - i) * SPAN, SPAN), SPAN)
    for k in range(wt_ref.shape[1]):
        cols_k = slice(k * chunk, (k + 1) * chunk)
        part[place, cols_k] = (
            dot_nn(gp, wt_ref[0, k, :wide]) + dot_nn(gdt, wt_ref[0, k, wide:])
        ).astype(BF16)
        gin[k, :wide] += dot_tn(gp, n_ref[:, cols_k])
        gin[k, wide:] += dot_tn(gdt, n_ref[:, cols_k])


def place_of(half, f, s):
    f, s = lax.rem(f, SIDE), lax.rem(s, SIDE)
    return s * SIDE + f if half == 0 else f * SIDE + s


def ring_places():
    me = lax.axis_index(AXIS)
    return me % SIDE, me // SIDE


def ring_neighbours():
    x, y = ring_places()
    steps = ((1, 0), (3, 0), (0, 1), (0, 3))
    return [{AXIS: place_of(0, x + dx, y + dy)} for dx, dy in steps]


def plane_neighbours():
    z = lax.axis_index("wshard")
    return [{"wshard": lax.rem(z + 1, SIDE)}, {"wshard": lax.rem(z + 3, SIDE)}]


def plane_across():
    return {"wshard": lax.rem(lax.axis_index("wshard") + 2, SIDE)}


def other_core():
    return {"section": 1 - lax.axis_index("section")}


def greet(targets):
    barrier = pltpu.get_barrier_semaphore()
    for target in targets:
        pl.semaphore_signal(barrier, inc=1, device_id=target, device_id_type=MESH)


def greeted(count):
    pl.semaphore_wait(pltpu.get_barrier_semaphore(), count)


def run(*parts):
    live = list(parts)
    while live:
        for part in list(live):
            try:
                next(part)
            except StopIteration:
                live.remove(part)


class Sender:
    def __init__(self, send, recv):
        self.send, self.recv, self.used, self.copies, self.free = send, recv, 0, {}, set()

    def make(self, name, source, target, to):
        copy = pltpu.make_async_remote_copy(
            src_ref=source, dst_ref=target, send_sem=self.send.at[self.used],
            recv_sem=self.recv.at[self.used], device_id=to, device_id_type=MESH,
        )
        self.used += 1
        self.copies[name] = copy
        return copy

    def go(self, name, source, target, to):
        self.make(name, source, target, to).start()
        self.free.add(name)

    def arrived(self, name):
        self.copies[name].wait_recv()

    def sent(self):
        for name in self.copies:
            if name in self.free:
                self.copies[name].wait_send()


def rows_at(ref, start, size):
    return ref.at[pl.ds(pl.multiple_of(start, 16), size)]


def spread_steps(x_ref, o_ref, out, own):
    x, y = ring_places()
    rows = x_ref.shape[0]
    half_rows, quarter = rows // 2, rows // 4
    mine = pltpu.make_async_copy(x_ref, rows_at(o_ref, place_of(0, x, y) * rows, rows), own)
    mine.start()
    firsts = ((x, y), (y, x))

    def go(name, half, block, offset, size, to, source=None):
        place = rows_at(o_ref, block * rows + half * half_rows + offset, size)
        out.go((half, name), place if source is None else source, place, {AXIS: to})

    def across(half, d):
        f, s = firsts[half]
        block = place_of(half, f + d, s)
        source = x_ref.at[pl.ds(half * half_rows, half_rows)] if d == 0 else None
        go(("t1", d), half, block, 0, half_rows, place_of(half, f, s + 1), source)
        go(("t2", d), half, block, 0, half_rows, place_of(half, f, s + 3), source)

    def onward(half, d):
        f, s = firsts[half]
        out.arrived((half, ("t1", d)))
        go(("u1", d), half, place_of(half, f + d, s + 3), 0, quarter, place_of(half, f, s + 1))
        out.arrived((half, ("t2", d)))
        go(("u2", d), half, place_of(half, f + d, s + 1), quarter, quarter, place_of(half, f, s + 3))

    for half in (0, 1):
        f, s = firsts[half]
        source = x_ref.at[pl.ds(half * half_rows, half_rows)]
        block = place_of(half, f, s)
        go("s1", half, block, 0, half_rows, place_of(half, f + 1, s), source)
        go("s2", half, block, 0, half_rows, place_of(half, f + 3, s), source)
    for half in (0, 1):
        across(half, 0)
    yield
    for half in (0, 1):
        f, s = firsts[half]
        out.arrived((half, "s1"))
        go("s3", half, place_of(half, f + 3, s), 0, quarter, place_of(half, f + 1, s))
        out.arrived((half, "s2"))
        go("s4", half, place_of(half, f + 1, s), quarter, quarter, place_of(half, f + 3, s))
    for half in (0, 1):
        across(half, 3)
        across(half, 1)
    yield
    for half in (0, 1):
        onward(half, 0)
    for half in (0, 1):
        out.arrived((half, "s3"))
        out.arrived((half, "s4"))
        across(half, 2)
    yield
    for d in (3, 1, 2):
        for half in (0, 1):
            onward(half, d)
        yield
    for half in (0, 1):
        for d in range(SIDE):
            out.arrived((half, ("u1", d)))
            out.arrived((half, ("u2", d)))
    mine.wait()


def collect_scratch(rows, cols):
    half_rows, quarter = rows // 2, rows // 4
    return [
        pltpu.VMEM((2, SIDE, 2, quarter, cols), BF16),
        pltpu.VMEM((2, SIDE, 2, half_rows, cols), BF16),
        pltpu.VMEM((2, SIDE, 2, half_rows, cols), BF16),
        pltpu.VMEM((2, SIDE, half_rows, cols), F32),
        pltpu.VMEM((2, 2, quarter, cols), BF16),
        pltpu.VMEM((2, 2, half_rows, cols), BF16),
        pltpu.VMEM((2, 3, half_rows, cols), BF16),
        pltpu.VMEM((rows, cols), F32),
    ]


def collect_steps(x_ref, buffers, out):
    far, near, stage, reduced, far2, near2, stage2, o_ref = buffers
    x, y = ring_places()
    rows = o_ref.shape[0]
    half_rows, quarter = rows // 2, rows // 4
    firsts = ((x, y), (y, x))
    order = (2, 1, 3, 0)

    def go(name, half, source, target, to):
        out.go((half, name), source, target, {AXIS: to})

    def start_of(half, f, s):
        return pl.multiple_of(place_of(half, f, s) * rows + half * half_rows, 16)

    for d in order:
        for half in (0, 1):
            f, s = firsts[half]
            start = start_of(half, f + d, s + 2)
            go(("a1", d), half, rows_at(x_ref, start, quarter), far.at[half, d, 0],
               place_of(half, f, s + 1))
            go(("a2", d), half, rows_at(x_ref, start + quarter, quarter), far.at[half, d, 1],
               place_of(half, f, s + 3))
    yield
    for d in order:
        for half in (0, 1):
            f, s = firsts[half]
            for side, step in enumerate((1, 3)):
                start = start_of(half, f + d, s + step)
                plain, through = quarter * (1 - side), quarter * side
                stage[half, d, side, pl.ds(plain, quarter)] = x_ref[
                    pl.ds(pl.multiple_of(start + plain, 16), quarter), :
                ]
                out.arrived((half, (("a1", "a2")[side], d)))
                stage[half, d, side, pl.ds(through, quarter)] = (
                    x_ref[pl.ds(pl.multiple_of(start + through, 16), quarter), :].astype(F32)
                    + far[half, d, side].astype(F32)
                ).astype(BF16)
                go((("b1", "b2")[side], d), half, stage.at[half, d, side], near.at[half, d, side],
                   place_of(half, f, s + step))
        if d in (1, 0):
            yield

    def reduce_second(half, d):
        f, s = firsts[half]
        out.arrived((half, ("b1", d)))
        out.arrived((half, ("b2", d)))
        reduced[half, d] = (
            x_ref[pl.ds(start_of(half, f + d, s), half_rows), :].astype(F32)
            + near[half, d, 0].astype(F32) + near[half, d, 1].astype(F32)
        )

    for half in (0, 1):
        f, s = firsts[half]
        reduce_second(half, 2)
        stage2[half, 2] = reduced[half, 2].astype(BF16)
        go("c1", half, stage2.at[half, 2, pl.ds(0, quarter)], far2.at[half, 0],
           place_of(half, f + 1, s))
        go("c2", half, stage2.at[half, 2, pl.ds(quarter, quarter)], far2.at[half, 1],
           place_of(half, f + 3, s))
    yield
    for d, side in ((1, 0), (3, 1)):
        for half in (0, 1):
            f, s = firsts[half]
            reduce_second(half, d)
            plain, through = quarter * (1 - side), quarter * side
            out.arrived((half, ("c1", "c2")[side]))
            stage2[half, side, pl.ds(plain, quarter)] = reduced[
                half, d, pl.ds(plain, quarter)
            ].astype(BF16)
            stage2[half, side, pl.ds(through, quarter)] = (
                reduced[half, d, pl.ds(through, quarter)] + far2[half, side].astype(F32)
            ).astype(BF16)
            go(("d1", "d2")[side], half, stage2.at[half, side], near2.at[half, side],
               place_of(half, f + d, s))
    yield
    for half in (0, 1):
        reduce_second(half, 0)
    for half in (0, 1):
        out.arrived((half, "d1"))
        out.arrived((half, "d2"))
        o_ref[pl.ds(half * half_rows, half_rows), :] = (
            reduced[half, 0] + near2[half, 0].astype(F32) + near2[half, 1].astype(F32)
        )


def half_of(rows):
    return rows // 32 * 16


def fold_scratch():
    scratch = [pltpu.VMEM((8, 4 * HC), F32)] * 3 + [pltpu.VMEM((3, 8, 4 * HC), F32)]
    for rows, cols in ((WR, 256), (HC // SIDE, 1024)):
        scratch += [pltpu.VMEM((SIDE, rows, cols), BF16)] * 3
        scratch += [pltpu.VMEM((2, rows - half_of(rows), cols), BF16)]
        scratch += [pltpu.VMEM((2, rows, cols), BF16)]
    return scratch


def fold_steps(layer, gin, gout, fin_ref, fout_ref, buffers, out):
    z = lax.axis_index("wshard")
    up, down = plane_neighbours()
    owner = lax.axis_index("section") == layer
    ours_in, land_in, total_in, far_in, near_in = buffers[4:9]
    ours_out, land_out, total_out, far_out, near_out = buffers[9:14]
    ours_in[...] = gin[...].astype(BF16)
    piece = HC // SIDE
    for k in range(SIDE):
        ours_out[k] = gout[k * piece : (k + 1) * piece, :].astype(BF16)
    arrays = (
        (ours_in, land_in, total_in, far_in, near_in, fin_ref),
        (ours_out, land_out, total_out, far_out, near_out, fout_ref),
    )

    def at(d):
        return lax.rem(z + d, SIDE)

    swaps, legs = {}, {}
    parts = []
    for ours in (ours_in, ours_out):
        half = half_of(ours.shape[1])
        parts.append((pl.ds(0, half), pl.ds(half, ours.shape[1] - half)))
    for d in (2, 1, 3, 0):
        for k, (ours, land, *_) in enumerate(arrays):
            swaps[k, d] = out.make(("swap", k, d), ours.at[at(d)], land.at[at(d)], other_core())
    for k, (_, _, total, far, near, _) in enumerate(arrays):
        for side, to in enumerate((up, down)):
            some = parts[k][side]
            legs[k, "far", side] = out.make(
                ("far", k, side), total.at[at(2), some], far.at[side, pl.ds(0, some.size)], to
            )
        legs[k, "near", 0] = out.make(("near", k, 0), total.at[at(1)], near.at[0], up)
        legs[k, "near", 1] = out.make(("near", k, 1), total.at[at(3)], near.at[1], down)

    @pl.when(jnp.logical_not(owner))
    def _():
        for copy in swaps.values():
            copy.start()

    yield

    def add_cores(d):
        for k, (ours, land, total, *_) in enumerate(arrays):
            swaps[k, d].wait_recv()
            total[at(d)] = (ours[at(d)].astype(F32) + land[at(d)].astype(F32)).astype(BF16)

    @pl.when(owner)
    def _():
        add_cores(2)
        for k in (0, 1):
            legs[k, "far", 0].start()
            legs[k, "far", 1].start()

    yield
    for side, d in ((0, 1), (1, 3)):
        @pl.when(owner)
        def _():
            add_cores(d)
            for k, (_, _, total, far, _, _) in enumerate(arrays):
                legs[k, "far", side].wait_recv()
                some = parts[k][side]
                total[at(d), some] = (
                    total[at(d), some].astype(F32) + far[side, pl.ds(0, some.size)].astype(F32)
                ).astype(BF16)
                legs[k, "near", side].start()

        yield

    @pl.when(owner)
    def _():
        add_cores(0)
        for k, (_, _, total, _, near, done) in enumerate(arrays):
            legs[k, "near", 0].wait_recv()
            legs[k, "near", 1].wait_recv()
            done[...] = (
                total[at(0)].astype(F32) + near[0].astype(F32) + near[1].astype(F32)
            ).astype(BF16)
        for leg in legs.values():
            leg.wait_send()

    @pl.when(jnp.logical_not(owner))
    def _():
        for copy in swaps.values():
            copy.wait_send()


def fold_small(layer, small, done_ref, buffers, out):
    owner = lax.axis_index("section") == layer
    land, total, _, planes = buffers[:4]
    up, down = plane_neighbours()
    swap = out.make("small", small, land, other_core())
    legs = [
        out.make(("small", k), total, planes.at[k], to)
        for k, to in enumerate((up, down, plane_across()))
    ]

    @pl.when(jnp.logical_not(owner))
    def _():
        swap.start()

    @pl.when(owner)
    def _():
        swap.wait_recv()
        total[...] = small[...] + land[...]
        for leg in legs:
            leg.start()

    yield

    @pl.when(owner)
    def _():
        for leg in legs:
            leg.wait_recv()
        done_ref[...] = total[...] + planes[0] + planes[1] + planes[2]
        for leg in legs:
            leg.wait_send()

    @pl.when(jnp.logical_not(owner))
    def _():
        swap.wait_send()


def norm_rows(u):
    return u * lax.rsqrt(jnp.mean(u * u, axis=1, keepdims=True) + EPS)


def payload_into(ref, c, branch, r, inner):
    width = c.shape[1]
    low = c.astype(BF16)
    pull = r * r * jnp.sum(low.astype(F32) * branch, axis=1, keepdims=True) / inner
    ref[:, :width] = low
    ref[:, width:] = lanes_of(list(three(r)) + list(three(pull))[:2], c.shape[0])


def forward_kernel(
    layer, inner, n_ref, wt_ref, wo_ref, con_ref, cons_ref, mask_ref, docr_ref, u_ref, cot_ref,
    vh_ref, gate_ref, dt_ref, mix_ref, scan_ref, st_ref, h_ref, branch_ref, r_ref, next_ref,
    vbuf, state, part, own_rows, landing, send, recv, send2, recv2, own, *buffers,
):
    i = pl.program_id(0)
    last = pl.num_programs(0) - 1

    @pl.when(i == 0)
    def _():
        greet(ring_neighbours())

    kept = (vh_ref, gate_ref, dt_ref, mix_ref, scan_ref, st_ref)
    fwd_step(i, n_ref, wt_ref, wo_ref, con_ref, mask_ref, docr_ref, kept, part, vbuf, state)

    @pl.when(i == last)
    def _():
        greeted(4)
        out = Sender(send, recv)
        run(collect_steps(part, buffers, out))
        width = u_ref.shape[1]
        total = buffers[-1]
        square = total[:, width : width + 1] + total[:, width + 1 : width + 2]
        square = square + total[:, width + 2 : width + 3]
        r = lax.rsqrt(square / inner + EPS)
        branch = total[:, :width] * r
        h = u_ref[...] + branch
        h_ref[...] = h
        branch_ref[...] = branch
        r_ref[...] = jnp.broadcast_to(r, r_ref.shape)
        if layer == 0:
            own_rows[...] = (norm_rows(h) * pre_gain_of(cons_ref[1])).astype(BF16)
        else:
            payload_into(own_rows, cot_ref[...], branch, r, inner)
        more = Sender(send2, recv2)
        run(spread_steps(own_rows, landing, more, own.at[0]))
        copy = pltpu.make_async_copy(landing, next_ref, own.at[1])
        copy.start()
        out.sent()
        more.sent()
        copy.wait()


def whole(shape):
    return pl.BlockSpec(shape, lambda i: (0,) * len(shape))


def of_layer(a, layer):
    rest = (0,) * (a.ndim - 1)
    return pl.BlockSpec((1,) + a.shape[1:], lambda i: (layer,) + rest)


def sems(count):
    return [pltpu.SemaphoreType.DMA((count,)), pltpu.SemaphoreType.DMA((count,))]


def forward_layer(layer, inner, n, wt, wo, cons, mask, docr, u, cot):
    length, width = n.shape
    blocks = length // SPAN
    mine = u.shape[0]
    wide = width + AUX
    out_cols = width if layer == 0 else wide

    def rows(cols):
        return pl.BlockSpec((SPAN, cols), lambda i: (i, 0))

    def shape(dims, dtype=F32):
        return jax.ShapeDtypeStruct(dims, dtype)

    return pl.pallas_call(
        lambda *refs: forward_kernel(layer, inner, *refs),
        grid=(blocks,),
        in_specs=[
            rows(width), of_layer(wt, layer), of_layer(wo, layer), of_layer(cons, layer),
            whole(cons.shape), rows(mask.shape[1]), pl.BlockSpec((8, SPAN), lambda i: (0, i)),
            whole(u.shape), whole(cot.shape),
        ],
        out_specs=[
            pl.BlockSpec((1, SPAN + 8, 3 * HC), lambda i: (i, 0, 0)),
            rows(HC), rows(HC), rows(HC), rows(HC),
            pl.BlockSpec((1, NS, HC), lambda i: (i, 0, 0)),
            whole(u.shape), whole(u.shape), whole((mine, HC)), pl.BlockSpec(memory_space=pl.ANY),
        ],
        out_shape=[
            shape((blocks, SPAN + 8, 3 * HC)), shape((length, HC)), shape((length, HC)),
            shape((length, HC), BF16), shape((length, HC)), shape((blocks, NS, HC)),
            shape(u.shape), shape(u.shape), shape((mine, HC)), shape((length, out_cols), BF16),
        ],
        scratch_shapes=[
            pltpu.VMEM((SPAN + 8, 3 * HC), F32), pltpu.VMEM((NS, HC), F32),
            pltpu.VMEM((length, wide), BF16), pltpu.VMEM((mine, out_cols), BF16),
            pltpu.VMEM((length, out_cols), BF16), *sems(40), *sems(40),
            pltpu.SemaphoreType.DMA((2,)), *collect_scratch(mine, wide),
        ],
        compiler_params=pltpu.CompilerParams(
            vmem_limit_bytes=VMEM_ASK, collective_id=1 + layer, has_side_effects=True
        ),
        name="forward_layer",
    )(n, wt, wo, cons, cons, mask, docr, u, cot)


def backward_kernel(
    layer, inner, c_ref, n_ref, wt_ref, wo_ref, con_ref, mask_ref, docr_ref,
    vh_ref, gate_ref, dt_ref, mix_ref, scan_ref, st_ref, u_ref, cot_ref, branch_ref, r_ref,
    cotout_ref, fin_ref, fout_ref, fsmall_ref, next_ref,
    dzbuf, dstate, part, gin, gout, small, own_rows, landing,
    send, recv, send2, recv2, send3, recv3, own, *buffers,
):
    i = pl.program_id(0)
    last = pl.num_programs(0) - 1
    targets = ring_neighbours() + plane_neighbours() + [plane_across(), other_core()]

    @pl.when(i == 0)
    def _():
        greet(targets)

    kept = (vh_ref, gate_ref, dt_ref, mix_ref, scan_ref, st_ref)
    bwd_step(
        i, c_ref, n_ref, wt_ref, wo_ref, con_ref, mask_ref, docr_ref, kept,
        part, gin, gout, small, dzbuf, dstate,
    )

    @pl.when(i == last)
    def _():
        greeted(len(targets))
        collecting, folding = buffers[:8], buffers[8:]
        out, folds, more = Sender(send, recv), Sender(send2, recv2), Sender(send3, recv3)
        run(
            collect_steps(part, collecting, out),
            fold_steps(layer, gin, gout, fin_ref, fout_ref, folding, folds),
        )
        g = collecting[-1][...]
        u = u_ref[...]
        gain = pre_gain_of(con_ref[0])
        width = u.shape[1]
        ri = lax.rsqrt(jnp.mean(u * u, axis=1, keepdims=True) + EPS)
        gg = g * gain
        dot = jnp.sum(gg * u, axis=1, keepdims=True) / width
        c = cot_ref[...] + gg * ri - u * (ri * ri * ri * dot)
        cotout_ref[...] = c
        d_pre = jnp.sum(g * u * ri, axis=0, keepdims=True)
        for k in range(8):
            small[k : k + 1, 3 * HC :] = d_pre[:, k * HC : (k + 1) * HC]
        ending = fold_small(layer, small, fsmall_ref, folding, folds)
        if layer == 1:
            payload_into(own_rows, c, branch_ref[...], r_ref[:, 0:1], inner)
            run(spread_steps(own_rows, landing, more, own.at[0]), ending)
            copy = pltpu.make_async_copy(landing, next_ref, own.at[1])
            copy.start()
            out.sent()
            more.sent()
            copy.wait()
        else:
            run(ending)
            next_ref[...] = jnp.zeros_like(next_ref)
            out.sent()


def backward_layer(layer, inner, c, n, wt, wo, cons, mask, docr, kept, u, cot, branch, r):
    length, width = n.shape
    blocks = length // SPAN
    last = blocks - 1
    mine = u.shape[0]
    wide = width + AUX

    def rows(cols):
        return pl.BlockSpec((SPAN, cols), lambda i: (last - i, 0))

    def stack(a):
        return pl.BlockSpec((1,) + a.shape[1:], lambda i: (last - i, 0, 0))

    def shape(dims, dtype=F32):
        return jax.ShapeDtypeStruct(dims, dtype)

    more = (length, wide) if layer == 1 else (16, HC)
    return pl.pallas_call(
        lambda *refs: backward_kernel(layer, inner, *refs),
        grid=(blocks,),
        in_specs=[
            rows(wide), rows(width), of_layer(wt, layer), of_layer(wo, layer),
            of_layer(cons, layer), rows(mask.shape[1]),
            pl.BlockSpec((8, SPAN), lambda i: (0, last - i)),
            stack(kept[0]), rows(HC), rows(HC), rows(HC), rows(HC), stack(kept[5]),
            whole(u.shape), whole(u.shape), whole(u.shape), whole(r.shape),
        ],
        out_specs=[
            whole(u.shape), whole((WR, 256)), whole((HC // SIDE, width)), whole((8, 4 * HC)),
            pl.BlockSpec(memory_space=pl.ANY) if layer == 1 else whole(more),
        ],
        out_shape=[
            shape(u.shape), shape((WR, 256), BF16), shape((HC // SIDE, width), BF16),
            shape((8, 4 * HC)), shape(more, BF16),
        ],
        scratch_shapes=[
            pltpu.VMEM((SPAN + 8, 3 * HC), F32), pltpu.VMEM((NS, HC), F32),
            pltpu.VMEM((length, width), BF16), pltpu.VMEM((SIDE, WR, 256), F32),
            pltpu.VMEM((HC, width), F32), pltpu.VMEM((8, 4 * HC), F32),
            pltpu.VMEM((mine, wide), BF16), pltpu.VMEM(more, BF16),
            *sems(40), *sems(24), *sems(40), pltpu.SemaphoreType.DMA((2,)),
            *collect_scratch(mine, width), *fold_scratch(),
        ],
        compiler_params=pltpu.CompilerParams(
            vmem_limit_bytes=VMEM_ASK, collective_id=3 + layer, has_side_effects=True
        ),
        name="backward_layer",
    )(c, n, wt, wo, cons, mask, docr, *kept, u, cot, branch, r)


def prepare_kernel(
    doc_ref, cw_ref, cb_ref, dtb_ref, alog_ref, skip_ref, pre_ref, gain_ref,
    con_ref, mask_ref, docr_ref,
):
    q = lax.axis_index(AXIS)
    part = lax.axis_index("section")
    inner = gain_ref.shape[1]
    own = pl.ds(pl.multiple_of(q * HC, HC), HC)
    con_ref[...] = jnp.zeros_like(con_ref)
    con_ref[0:4, :HC] = cw_ref[0, :, own]
    con_ref[0:4, HC : 3 * HC] = cw_ref[0, :, inner:]
    con_ref[4:5, :HC] = cb_ref[:, own]
    con_ref[4:5, HC : 3 * HC] = cb_ref[:, inner:]

    def lanes(ref):
        value = ref[...]
        lane = iota(value.shape, 1)
        two = [
            jnp.sum(jnp.where(lane == 2 * q + h, value, 0.0), axis=1, keepdims=True) for h in (0, 1)
        ]
        return jnp.where(iota((1, HC), 1) < HEAD, two[0], two[1])

    con_ref[5:6, :HC] = lanes(dtb_ref)
    con_ref[5:6, HC : 2 * HC] = jnp.exp(lanes(alog_ref))
    con_ref[5:6, 2 * HC : 3 * HC] = lanes(skip_ref)
    con_ref[6:7, :HC] = gain_ref[:, own]
    for k in range(8):
        con_ref[k : k + 1, 3 * HC :] = pre_ref[:, k * HC : (k + 1) * HC]

    doc = doc_ref[part].astype(F32)
    length = doc.shape[1]
    doc8 = jnp.broadcast_to(doc, (8, length))
    docr_ref[...] = doc8
    at = iota((8, length), 1)
    rows = []
    for k in (1, 2, 3):
        rows.append((pltpu.roll(doc8, k, 1) == doc8) & (at >= k))
    for k in (1, 2, 3):
        rows.append((pltpu.roll(doc8, length - k, 1) == doc8) & (at < length - k))
    before, final = doc8, doc8
    for b in range(length // SPAN):
        inside = (at >= b * SPAN) & (at < (b + 1) * SPAN)
        start = max(b * SPAN - 1, 0)
        end = (b + 1) * SPAN - 1
        before = jnp.where(inside, doc[:, start : start + 1], before)
        final = jnp.where(inside, doc[:, end : end + 1], final)
    rows += [before == doc8, final == doc8]
    sub = iota((8, length), 0)
    first = jnp.zeros((8, length), F32)
    for k, row in enumerate(rows):
        first = jnp.where((sub == k) & row, 1.0, first)
    both = jnp.concatenate([first, doc8, jnp.zeros((HC - 16, length), F32)])
    mask_ref[...] = both.T


def prepare(doc_ids, *params):
    length = doc_ids.shape[2]
    vmem = pl.BlockSpec(memory_space=pltpu.VMEM)
    return pl.pallas_call(
        prepare_kernel,
        in_specs=[vmem] * (1 + len(params)),
        out_specs=[vmem] * 3,
        out_shape=[
            jax.ShapeDtypeStruct((8, 4 * HC), F32), jax.ShapeDtypeStruct((length, HC), F32),
            jax.ShapeDtypeStruct((8, length), F32),
        ],
        compiler_params=pltpu.CompilerParams(vmem_limit_bytes=VMEM_ASK),
        name="prepare",
    )(doc_ids, *params)


def weights_steps(w_ref, wo_ref, wall_ref, woall_ref, own_w, dts, out, own):
    x, y = ring_places()
    q = lax.axis_index(AXIS)
    part, z = lax.axis_index("section"), lax.axis_index("wshard")
    up, down = plane_neighbours()
    half, half_wo = 256, HC // 2

    def at(d):
        return lax.rem(z + d, SIDE)

    mine = pltpu.make_async_copy(own_w, wall_ref.at[part, z], own.at[4])
    mine.start()
    out.go("up", own_w, wall_ref.at[part, z], up)
    out.go("down", own_w, wall_ref.at[part, z], down)
    role = at(SIDE - y)
    woown = woall_ref.at[part]
    wo_mine = wo_ref.at[0, pl.ds(pl.multiple_of(x * HC, HC), HC)]
    first, second = woown.at[pl.ds(0, half_wo)], woown.at[pl.ds(half_wo, half_wo)]
    rows_mine = pltpu.make_async_copy(wo_mine, woown, own.at[5])
    rows_up = out.make("wo_up", wo_mine, woown, up)
    rows_down = out.make("wo_down", wo_mine, woown, down)
    on_up = out.make("wo_on_up", first, first, up)
    on_down = out.make("wo_on_down", second, second, down)

    @pl.when(role == 0)
    def _():
        rows_mine.start()
        rows_up.start()
        rows_down.start()

    yield
    out.arrived("up")
    before, after = wall_ref.at[part, at(3)], wall_ref.at[part, at(1)]
    out.go("on_up", before.at[pl.ds(0, half)], before.at[pl.ds(0, half)], up)
    out.arrived("down")
    out.go("on_down", after.at[pl.ds(half, WR - half)], after.at[pl.ds(half, WR - half)], down)
    mine.wait()
    for k, d in enumerate((0, 3, 1)):
        out.go(("swap", k), wall_ref.at[part, at(d)], wall_ref.at[part, at(d)], other_core())

    yield

    @pl.when(role == 1)
    def _():
        rows_up.wait_recv()
        on_up.start()

    @pl.when(role == 3)
    def _():
        rows_down.wait_recv()
        on_down.start()

    @pl.when(role == 0)
    def _():
        rows_mine.wait()

    @pl.when(role == 2)
    def _():
        on_up.wait_recv()
        on_down.wait_recv()

    out.go("swap_wo", woown, woown, other_core())
    yield
    out.arrived("on_up")
    out.arrived("on_down")
    out.go(("swap", 3), wall_ref.at[part, at(2)], wall_ref.at[part, at(2)], other_core())
    yield
    for k in range(SIDE):
        out.arrived(("swap", k))
    out.arrived("swap_wo")

    @pl.when(role == 0)
    def _():
        rows_up.wait_send()
        rows_down.wait_send()

    @pl.when(role == 1)
    def _():
        on_up.wait_send()

    @pl.when(role == 3)
    def _():
        on_down.wait_send()


def opening_kernel(
    x_ref, og_ref, cons_ref, w_ref, wo_ref, o_ref, u_ref, cot_ref, wall_ref, woall_ref,
    own_rows, own_w, dts, send, recv, send2, recv2, own,
):
    targets = ring_neighbours() + plane_neighbours() + [other_core()]
    greet(targets)
    q = lax.axis_index(AXIS)
    part = lax.axis_index("section")
    inner = (w_ref.shape[0] - 2 * NS) // 2 // HC * HC
    pieces = [
        (pl.ds(pl.multiple_of(q * HC, HC), HC), own_w.at[pl.ds(0, HC)]),
        (pl.ds(pl.multiple_of(inner + q * HC, HC), HC), own_w.at[pl.ds(HC, HC)]),
        (pl.ds(2 * inner, 2 * NS), own_w.at[pl.ds(2 * HC, 2 * NS)]),
        (pl.ds(2 * inner + 2 * NS, dts.shape[0]), dts),
    ]
    copies = [
        pltpu.make_async_copy(w_ref.at[rows], target, own.at[k])
        for k, (rows, target) in enumerate(pieces)
    ]
    for copy in copies:
        copy.start()
    u = x_ref[part, 0].astype(F32)
    u_ref[...] = u
    cot_ref[...] = og_ref[part, 0].astype(F32)
    own_rows[...] = (norm_rows(u) * pre_gain_of(cons_ref[0])).astype(BF16)
    for copy in copies:
        copy.wait()
    heads = dts.shape[0]
    pick = (iota((16, heads), 1) == 2 * q + iota((16, heads), 0)) & (iota((16, heads), 0) < 2)
    own_w[4 * HC :, :] = dot_nn(pick.astype(F32).astype(BF16), dts[...]).astype(BF16)
    greeted(len(targets))
    out, planes = Sender(send, recv), Sender(send2, recv2)
    run(
        weights_steps(w_ref, wo_ref, wall_ref, woall_ref, own_w, dts, planes, own),
        spread_steps(own_rows, o_ref, out, own.at[6]),
    )
    out.sent()
    planes.sent()


def opening(block_input, out_grad, cons, w, wo, heads):
    vmem, hbm = pl.BlockSpec(memory_space=pltpu.VMEM), pl.BlockSpec(memory_space=pl.ANY)
    rows, width = block_input.shape[2:]
    count = lax.axis_size(AXIS)

    def shape(dims, dtype=F32):
        return jax.ShapeDtypeStruct(dims, dtype)

    return pl.pallas_call(
        opening_kernel,
        in_specs=[vmem, vmem, vmem, hbm, hbm],
        out_specs=[vmem] * 5,
        out_shape=[
            shape((count * rows, width), BF16), shape((rows, width)), shape((rows, width)),
            shape((2, SIDE, WR, w.shape[1]), BF16), shape((2, HC, width), BF16),
        ],
        scratch_shapes=[
            pltpu.VMEM((rows, width), BF16), pltpu.VMEM((WR, w.shape[1]), BF16),
            pltpu.VMEM((heads, w.shape[1]), BF16), *sems(40), *sems(16),
            pltpu.SemaphoreType.DMA((7,)),
        ],
        compiler_params=pltpu.CompilerParams(
            collective_id=5, has_side_effects=True, vmem_limit_bytes=VMEM_ASK
        ),
        name="opening",
    )(block_input, out_grad, cons, w, wo)


END_ROWS = 448


def closing_kernel(
    fin0, fout0, fs0, fin1, fout1, fs1, o_ref,
    mixed_in, mixed_out, came, block, landing, send, recv, send2, recv2, own,
):
    me = lax.axis_index(AXIS)
    count = lax.axis_size(AXIS)
    x, y = ring_places()
    z = lax.axis_index("wshard")
    part = lax.axis_index("section")
    others = [{AXIS: lax.rem(me + d, count)} for d in range(1, count)]
    turned = {AXIS: place_of(0, x, z), "wshard": y}

    greet(others)

    @pl.when(z != y)
    def _():
        pl.semaphore_signal(
            pltpu.get_barrier_semaphore(), inc=1, device_id=turned, device_id_type=MESH
        )

    zero = part == 0
    mixed_in[...] = jnp.where(zero, fin0[...], fin1[...])
    mixed_out[...] = jnp.where(zero, fout0[...], fout1[...])
    small = jnp.where(zero, fs0[...], fs1[...])
    greeted(len(others) + (z != y).astype(jnp.int32))
    out, more = Sender(send, recv), Sender(send2, recv2)
    def bc(j):
        return rows_at(mixed_in, 2 * HC + j * 16, 16)

    for d in range(1, count):
        to = lax.rem(me + d, count)
        out.go(d, bc(to), landing.at[d], {AXIS: to})
    turn = out.make("turn", mixed_out, came, turned)

    @pl.when(z != y)
    def _():
        turn.start()

    block[0 : 2 * HC, :] = mixed_in[0 : 2 * HC, :]
    block[2 * HC + 16 : 2 * HC + 32, :] = mixed_in[4 * HC :, :]
    chunks = jnp.concatenate([small[:, :256], small[:, 256:]])
    hi, mid, _ = three(chunks)
    block[END_ROWS - 32 : END_ROWS - 16, :] = hi
    block[END_ROWS - 16 :, :] = mid
    total = mixed_in[pl.ds(pl.multiple_of(2 * HC + me * 16, 16), 16), :].astype(F32)
    for d in range(1, count):
        out.arrived(d)
        total = total + landing[d].astype(F32)
    block[2 * HC : 2 * HC + 16, :] = total.astype(BF16)

    @pl.when(z != y)
    def _():
        turn.wait_recv()

    @pl.when(z == y)
    def _():
        came[...] = mixed_out[...]

    at = 2 * HC + 32
    for c in range(4):
        block[at + 32 * c : at + 32 * (c + 1), :] = came[:, c * 256 : (c + 1) * 256]
    run(spread_steps(block, o_ref, more, own))
    out.sent()
    more.sent()

    @pl.when(z != y)
    def _():
        turn.wait_send()


def closing(*sums):
    vmem = pl.BlockSpec(memory_space=pltpu.VMEM)
    count = lax.axis_size(AXIS)
    width = sums[1].shape[1]
    return pl.pallas_call(
        closing_kernel,
        in_specs=[vmem] * 6,
        out_specs=vmem,
        out_shape=jax.ShapeDtypeStruct((count * END_ROWS, 256), BF16),
        scratch_shapes=[
            pltpu.VMEM((WR, 256), BF16), pltpu.VMEM((HC // SIDE, width), BF16),
            pltpu.VMEM((HC // SIDE, width), BF16), pltpu.VMEM((END_ROWS, 256), BF16),
            pltpu.VMEM((count, 16, 256), BF16), *sems(17), *sems(40), pltpu.SemaphoreType.DMA,
        ],
        compiler_params=pltpu.CompilerParams(
            collective_id=6, has_side_effects=True, vmem_limit_bytes=VMEM_ASK
        ),
        name="closing",
    )(*sums)


def assemble_kernel(
    inner, all_ref, gin_ref, gout_ref, convw_ref, convb_ref, pre_ref, gain_ref, heads_ref
):
    count = all_ref.shape[0]
    lane = iota((1, HC), 1)
    bc = jnp.zeros((5, 2 * HC), F32)
    pre = jnp.zeros((8, HC), F32)
    per_head = [jnp.zeros((1, HC), F32)] * 3
    for j in range(count):
        own = slice(j * HC, (j + 1) * HC)
        gin_ref[own, :] = all_ref[j, 0:HC, :].astype(F32)
        gin_ref[inner + j * HC : inner + (j + 1) * HC, :] = all_ref[j, HC : 2 * HC, :].astype(F32)
        at = 2 * inner + j * 16
        gin_ref[at : at + 16, :] = all_ref[j, 256:272, :].astype(F32)
        at = 2 * inner + 2 * NS + 2 * j
        gin_ref[at : at + 2, :] = all_ref[j, 272:288, :].astype(F32)[0:2, :]
        big, piece = j % SIDE, j // SIDE
        at = big * HC + piece * 32
        for c in range(4):
            gout_ref[at : at + 32, c * 256 : (c + 1) * 256] = (
                all_ref[j, 288 + 32 * c : 320 + 32 * c, :].astype(F32)
            )
        small = all_ref[j, END_ROWS - 32 : END_ROWS - 16, :].astype(F32)
        small = small + all_ref[j, END_ROWS - 16 :, :].astype(F32)
        convw_ref[:, own] = small[0:4, :HC]
        convb_ref[:, own] = small[4:5, :HC]
        gain_ref[:, own] = small[5:6, :HC]
        bc = bc + jnp.concatenate([small[0:5, HC:], small[8:13, :HC]], axis=1)
        pre = pre + small[8:16, HC:]
        skip = small[5:6, HC:]
        for h in (0, 1):
            here = lane == 2 * j + h
            mine = (lane >= h * HEAD) & (lane < (h + 1) * HEAD)
            values = (
                small[6:7, h * HEAD : h * HEAD + 1],
                small[6:7, HC + h * HEAD : HC + h * HEAD + 1],
                jnp.sum(jnp.where(mine, skip, 0.0), axis=1, keepdims=True),
            )
            per_head = [jnp.where(here, v, p) for v, p in zip(values, per_head)]
    convw_ref[:, inner:] = bc[0:4]
    convb_ref[:, inner:] = bc[4:5]
    for k in range(8):
        pre_ref[:, k * HC : (k + 1) * HC] = pre[k : k + 1]
    heads_ref[...] = jnp.concatenate(per_head + [jnp.zeros((5, HC), F32)])


def assemble(everyone, inner, columns, width, channels):
    def shape(*dims):
        return jax.ShapeDtypeStruct(dims, F32)

    vmem = pl.BlockSpec(memory_space=pltpu.VMEM)
    return pl.pallas_call(
        lambda *refs: assemble_kernel(inner, *refs),
        in_specs=[vmem],
        out_specs=[vmem] * 7,
        out_shape=[
            shape(columns, 256), shape(512, width), shape(4, channels), shape(1, channels),
            shape(1, width), shape(1, inner), shape(8, HC),
        ],
        compiler_params=pltpu.CompilerParams(vmem_limit_bytes=VMEM_ASK),
        name="assemble",
    )(everyone)


def body(
    block_input, doc_ids, out_grad, in_proj, out_proj, conv_weight, conv_bias,
    dt_bias, a_log, skip_scale, pre_gain, norm_gain,
):
    part = lax.axis_index("section")
    inner = norm_gain.shape[1]
    width = block_input.shape[3]
    heads = dt_bias.shape[1]
    con, mask, docr = prepare(
        doc_ids, conv_weight, conv_bias, dt_bias, a_log, skip_scale, pre_gain, norm_gain
    )
    cons = lax.all_gather(con, "section", axis=0)
    n0, u0, cot, wt, wo = opening(
        block_input, out_grad, cons, jnp.swapaxes(in_proj[0], 0, 1), out_proj, heads
    )
    shared = (wt, wo, cons, mask, docr)
    *kept0, h0, branch0, r0, n1 = forward_layer(0, inner, n0, *shared, u0, cot)
    *kept1, h1, _, r1, c1 = forward_layer(1, inner, n1, *shared, h0, cot)
    g1, *sums1, c0 = backward_layer(1, inner, c1, n1, *shared, kept1, h0, cot, branch0, r0)
    g0, *sums0, _ = backward_layer(0, inner, c0, n0, *shared, kept0, u0, g1, branch0, r0)

    def by_layer(first, second):
        mine = jnp.where(part == 0, first, second)
        other = lax.ppermute(jnp.where(part == 0, second, first), "section", [(0, 1), (1, 0)])
        pair = jnp.where(part == 0, jnp.stack([mine, other]), jnp.stack([other, mine]))
        return pair[None, :, None]

    hidden = by_layer(h0, h1)
    input_grads = by_layer(g0, g1)
    everyone = closing(*sums0, *sums1).reshape(-1, END_ROWS, 256)
    gin, gout, convw, convb, pre, gain, per_head = assemble(
        everyone, inner, in_proj.shape[2], width, conv_weight.shape[2]
    )
    return (
        hidden, input_grads, jnp.swapaxes(gin, 0, 1)[None], gout[None], convw[None], convb,
        per_head[0:1, :heads], per_head[1:2, :heads], per_head[2:3, :heads], pre, gain,
    )


def solution(mesh):
    specs = (
        P(None, "wshard", "seq", None),
        P(None, "wshard", None),
        P(None, "wshard", "seq", None),
        P("section", "wshard", None),
        P("section", "wshard", None),
        P("section", None, None),
        P("section", None),
        P("section", None),
        P("section", None),
        P("section", None),
        P("section", None),
        P("section", None),
    )
    outs = (
        P("section", None, "wshard", "seq", None),
        P("section", None, "wshard", "seq", None),
        P("section", "wshard", None),
        P("section", "wshard", None),
        P("section", None, None),
    ) + (P("section", None),) * 6
    return jax.shard_map(body, mesh=mesh, in_specs=specs, out_specs=outs, check_vma=False)
```

time: 921 us -> 283 us (0.31)
  blocking collectives: 389 us -> 1.83 us
  Pallas kernels: 352 us -> 254 us
  local copies, waits for them, and re-layouts: 102 us -> 23.7 us
  other arithmetic: 40.8 us -> 1.76 us
  between operations: 15.2 us -> 0.82 us
  waiting for transfers between devices: 10.1 us -> 0.01 us
    psum x1 -> x0, blocking collectives: 345 us -> none  [body(): sums = lax.psum(mine, ('seq', 'wshard'))]
    pallas_call x12 -> x8, Pallas kernels: 352 us -> 254 us  [the longest x2 93 us: backward_layer(): pl.pallas_call(lambda *refs: backward_kernel(layer, inner, *refs), grid=(...]
    all_to_all x1 -> x0, blocking collectives: 41.6 us -> none  [sent_and_summed(): arrived = lax.all_to_all(x, axis, split_axis=0, concat_axis=0, tiled=True)]
    unnamed x152 -> x60, local copies, waits for them, and re-layouts: 50.7 us -> 23.2 us
    slice x32 -> x1, local copies, waits for them, and re-layouts: 20.5 us -> 0.52 us  [body(): per_head[2:3, :heads]]
    reduce_sum x10 -> x0, other arithmetic: 15.1 us -> none  [the longest x2 9.56 us: sent_and_summed(): return arrived.astype(F32).sum(axis=0)]
    convert_element_type x8 -> x0, local copies, waits for them, and re-layouts: 14.9 us -> none  [the longest x1 9.19 us: body(): own = jnp.moveaxis(own, 0, 1).astype(F32)]
    convert_element_type x12 -> x0, other arithmetic: 9.63 us -> none  [the longest x1 2.3 us: body(): own = jnp.moveaxis(own, 0, 1).astype(F32)]
  transfers between devices with their start and end apart: 8 -> 2, of which waited for: 3 -> 0; matrix products, arithmetic and copies ran while one was open for 3% -> 0% of each run, Pallas kernels for 9% -> 13%
where the time goes in v3:
time: 283 us
  Pallas kernels  254 us (90%)
  local copies, waits for them, and re-layouts  23.7 us (8%)
    pallas_call x2, Pallas kernels, backward_layer(): pl.pallas_call(lambda *refs: backward_kernel(layer, inner, *refs), grid=(...  93 us
    pallas_call x2, Pallas kernels, forward_layer(): pl.pallas_call(lambda *refs: forward_kernel(layer, inner, *refs), grid=(b...  89.4 us
    pallas_call x1, Pallas kernels, closing(): pl.pallas_call(closing_kernel, in_specs=[vmem] * 6, out_specs=vmem, out_s...  34 us
    pallas_call x1, Pallas kernels, opening(): pl.pallas_call(opening_kernel, in_specs=[vmem, vmem, vmem, hbm, hbm], out...  33.9 us
    unnamed x60, local copies, waits for them, and re-layouts  23.2 us
  transfers between devices with their start and end apart: 2, of which 0 were waited for; matrix products, arithmetic and copies ran while one was open for 0% of the time, Pallas kernels for 13%

profile of v3, /device:TPU:0, one launch (start us, length us, event | category | flops | bytes accessed | tf_op | source)
XLA Modules:
  0.0 282.7 jit_solution(2374872242673485476)
XLA Ops:
  0.7 0.0 copy-start.22
  0.7 0.8 copy-done.22
  1.4 0.7 copy-done.23
  2.1 0.7 copy-done.24
  2.8 0.7 copy-done.25
  3.5 0.7 copy-done.26
  4.2 0.7 copy-done.27
  4.9 0.7 copy-done.28
  5.5 0.7 copy-done.29
  6.2 0.3 prepare.1
  6.5 1.8 all-gather
  8.4 1.2 copy-done.3
  9.6 0.9 copy-done.20
  10.5 0.9 copy-done.21
  11.5 33.9 %opening.1 = (bf16[1024,1024]{1,0:T(8,128)(2,1)S(1)}, f32[64,1024]{1,0:T(8,128)S(1)}, f32[64,1024]{1,0:T(8,128)S(1)}, bf16[2,4,528,256]{3,2,1,0:T(8,128)(2,1)}, bf16[2,128,1024]{2,1,0:T(8,128)(2,1)S(1)}) custom-call(bf16[2,1,64,1024]{3,2,1,0:T(8,128)(2,1)S(1)} %copy-done.20, bf16[2,1,64,1024]{3,2,1,0:T(8,128)(2,1)S(1)} %copy-done.21, ...), custom_call_target="tpu_custom_call" | custom-call | tf_op jit(solution)/shard_map/opening/pallas_call | solution.py:1084
  45.4 0.0 copy-start
  45.4 1.3 copy-done
  46.8 44.6 %forward_layer.2 = (f32[4,264,384]{2,1,0:T(8,128)S(1)}, f32[1024,128]{1,0:T(8,128)S(1)}, f32[1024,128]{1,0:T(8,128)S(1)}, bf16[1024,128]{1,0:T(8,128)(2,1)S(1)},...) custom-call(bf16[1024,1024]{1,0:T(8,128)(2,1)} %copy-done, ...), custom_call_target="tpu_custom_call" | custom-call | tf_op jit(solution)/shard_map/forward_layer/pallas_call | solution.py:741
  91.4 0.0 copy-start.1
  91.4 1.1 copy-done.1
  92.6 0.8 copy-done.4
  93.3 0.7 copy-done.12
  94.0 44.8 %forward_layer.3 = (f32[4,264,384]{2,1,0:T(8,128)S(1)}, f32[1024,128]{1,0:T(8,128)S(1)}, f32[1024,128]{1,0:T(8,128)S(1)}, bf16[1024,128]{1,0:T(8,128)(2,1)S(1)},...) custom-call(bf16[1024,1024]{1,0:T(8,128)(2,1)} %get-tuple-element.62, ...), custom_call_target="tpu_custom_call" | custom-call | tf_op jit(solution)/shard_map/forward_layer/pallas_call | solution.py:741
  138.8 0.0 copy-start.2
  138.8 1.1 copy-done.2
  140.0 0.8 copy-done.6
  140.8 0.8 copy-done.8
  141.6 0.8 copy-done.10
  142.4 0.7 copy-done.14
  143.0 0.7 copy-done.16
  143.7 0.7 copy-done.18
  144.4 1.0 copy-done.7
  145.5 1.0 copy-done.9
  146.5 1.0 copy-done.11
  147.6 0.9 copy-done.15
  148.5 0.9 copy-done.17
  149.5 52.1 %backward_layer.2 = (f32[64,1024]{1,0:T(8,128)S(1)}, bf16[528,256]{1,0:T(8,128)(2,1)S(1)}, bf16[32,1024]{1,0:T(8,128)(2,1)S(1)}, f32[8,512]{1,0:T(8,128)S(1)}, bf16[1024,1152]{1,0:T(8,128)(2,1)}) custom-call(bf16[1024,1152]{1,0:T(8,128)(2,1)} %get-tuple-element.64.refs_0_, bf16[1024,1024]{1,0:T(8,128)(2,1)} %get-tuple-element.62.refs_0_.refs_1_, ...), custom_call_target="tpu_custom_call" | custom-call | tf_op jit(solution)/shard_map/backward_layer/pallas_call | solution.py:847
  201.6 40.9 %backward_layer.3 = (f32[64,1024]{1,0:T(8,128)S(1)}, bf16[528,256]{1,0:T(8,128)(2,1)S(1)}, bf16[32,1024]{1,0:T(8,128)(2,1)S(1)}, f32[8,512]{1,0:T(8,128)S(1)}, bf16[16,128]{1,0:T(8,128)(2,1)}) custom-call(bf16[1024,1152]{1,0:T(8,128)(2,1)} %get-tuple-element.73.refs_0_, bf16[1024,1024]{1,0:T(8,128)(2,1)} %copy-done, ...), custom_call_target="tpu_custom_call" | custom-call | tf_op jit(solution)/shard_map/backward_layer/pallas_call | solution.py:847
  242.5 0.1 collective-permute-start.1
  242.6 0.0 copy-done.19
  242.7 0.6 collective-permute-start
  243.3 34.0 %closing.1 = bf16[7168,256]{1,0:T(8,128)(2,1)S(1)} custom-call(bf16[528,256]{1,0:T(8,128)(2,1)S(1)} %get-tuple-element.82.fin0, bf16[32,1024]{1,0:T(8,128)(2,1)S(1)} %get-tuple-element.83.fout0, f32[8,512]{1,0:T(8,128)S(1)} %get-tuple-element.84.fs0, bf16[528,256]{1,0:T(8,128)(2,1)S(1)} %get-tuple-element.85.fin1, ...), custom_call_target="tpu_custom_call" | custom-call | tf_op jit(solution)/shard_map/closing/pallas_call | solution.py:1181
  277.3 3.2 %assemble.1 = (f32[4384,256]{1,0:T(8,128)}, f32[512,1024]{1,0:T(8,128)}, f32[4,2304]{1,0:T(4,128)}, f32[1,2304]{1,0:T(1,128)}, f32[1,1024]{1,0:T(1,128)}, /*index=5*/f32[1,2048]{1,0:T(1,128)}, f32[8,128]{1,0:T(8,128)S(1)}) custom-call(bf16[16,448,256]{2,1,0:T(8,128)(2,1)S(1)} %bitcast.16), custom_call_target="tpu_custom_call" | custom-call | tf_op jit(solution)/shard_map/assemble/pallas_call | solution.py:1249
  280.5 0.5 fusion
  281.0 0.0 collective-permute-done.1
  281.0 0.8 maximum_select_fusion.1
  281.8 0.0 collective-permute-done
  281.8 0.8 maximum_select_fusion
  (30 shorter events, 0.1 us)
Async XLA Ops:
  0.7 0.8 copy-start.22
  1.4 0.7 copy-start.23
  2.1 0.7 copy-start.24
  2.8 0.7 copy-start.25
  3.5 0.7 copy-start.26
  4.2 0.7 copy-start.27
  4.9 0.7 copy-start.28
  5.5 0.7 copy-start.29
  8.4 1.2 copy-start.3
  9.6 0.9 copy-start.20
  10.5 0.9 copy-start.21
  45.4 1.3 copy-start
  91.4 1.2 copy-start.1
  92.6 0.8 copy-start.4
  93.3 0.7 copy-start.12
  138.8 1.2 copy-start.2
  140.0 0.8 copy-start.6
  140.8 0.8 copy-start.8
  141.6 0.8 copy-start.10
  142.4 0.7 copy-start.14
  143.0 0.7 copy-start.16
  143.7 0.7 copy-start.18
  144.4 1.0 copy-start.7
  145.5 1.0 copy-start.9
  146.5 1.0 copy-start.11
  147.6 0.9 copy-start.15
  148.5 0.9 copy-start.17
  149.5 52.1 %copy-start.5 = (f32[1024,128]{1,0:T(8,128)S(1)}, f32[1024,128]{1,0:T(8,128)}, u32[]{:S(2)}) copy-start(f32[1024,128]{1,0:T(8,128)} %copy-done.4) | copy-start | bytes 1572868
  149.5 52.1 %copy-start.13 = (f32[4,128,128]{2,1,0:T(8,128)S(1)}, f32[4,128,128]{2,1,0:T(8,128)}, u32[]{:S(2)}) copy-start(f32[4,128,128]{2,1,0:T(8,128)} %copy-done.12) | copy-start | bytes 786436
  201.6 41.1 %copy-start.19 = (f32[64,1024]{1,0:T(8,128)S(1)}, f32[64,1024]{1,0:T(8,128)}, u32[]{:S(2)}) copy-start(f32[64,1024]{1,0:T(8,128)} %copy-done.18) | copy-start | bytes 786436
  242.5 38.4 %collective-permute-start.1 = (f32[64,1024]{1,0:T(8,128)S(1)}, f32[64,1024]{1,0:T(8,128)S(1)}, u32[]{:S(2)}, u32[]{:S(2)}) collective-permute-start(f32[64,1024]{1,0:T(8,128)S(1)} %get-tuple-element.96), channel_id=1, source_target_pairs={{0,64},{64,0},{1,65},{65,1},{2,66},{66,2},{3,67},{67,3},{4,68},{68... | collective-permute-start | bytes 786440 | tf_op jit(solution)/shard_map/ppermute | solution.py:1285
  242.7 39.1 %collective-permute-start = (f32[64,1024]{1,0:T(8,128)S(1)}, f32[64,1024]{1,0:T(8,128)S(1)}, u32[]{:S(2)}, u32[]{:S(2)}) collective-permute-start(f32[64,1024]{1,0:T(8,128)S(1)} %get-tuple-element.98), channel_id=1, source_target_pairs={{0,64},{64,0},{1,65},{65,1},{2,66},{66,2},{3,67},{67,3},{4,68},{68... | collective-permute-start | bytes 786440 | tf_op jit(solution)/shard_map/ppermute | solution.py:1285

commit v4 on v3

v4 whole, which is shorter than its diff:
```python
import jax
import jax.numpy as jnp
from jax import lax
from jax.experimental import pallas as pl
from jax.experimental.pallas import tpu as pltpu
from jax.sharding import PartitionSpec as P

SPAN = 256
EPS = 1e-05
F32 = jnp.float32
BF16 = jnp.bfloat16
MESH = pl.DeviceIdType.MESH
VMEM_ASK = 60 * 1024 * 1024

HC = 128
NS = 128
WR = 528
FR = 272
END_ROWS = 320
AUX = 128
HEAD = 64
SIDE = 4
AXIS = "seq"


def dot_nn(a, b):
    return lax.dot_general(a, b, (((1,), (0,)), ((), ())), preferred_element_type=F32)


def dot_nt(a, b):
    return lax.dot_general(a, b, (((1,), (1,)), ((), ())), preferred_element_type=F32)


def dot_tn(a, b):
    return lax.dot_general(a, b, (((0,), (0,)), ((), ())), preferred_element_type=F32)


def three(x):
    hi = x.astype(BF16)
    rest = x - hi.astype(F32)
    mid = rest.astype(BF16)
    low = (rest - mid.astype(F32)).astype(BF16)
    return hi, mid, low


def exact_left(ones, x):
    hi, mid, low = three(x)
    return dot_nn(ones, hi) + dot_nn(ones, mid) + dot_nn(ones, low)


def exact_right(x, ones):
    hi, mid, low = three(x)
    return dot_nn(hi, ones) + dot_nn(mid, ones) + dot_nn(low, ones)


def iota(shape, dim):
    return lax.broadcasted_iota(jnp.int32, shape, dim)


def sigmoid(x):
    return 1.0 / (1.0 + jnp.exp(-x))


def softplus(x):
    return jnp.maximum(x, 0.0) + jnp.log1p(jnp.exp(-jnp.abs(x)))


def conv_rows(vbuf, con, mask):
    z = vbuf[pl.ds(8, SPAN), :] * con[3:4, :] + con[4:5, :]
    for k in (1, 2, 3):
        z = z + vbuf[pl.ds(8 - k, SPAN), :] * con[3 - k : 4 - k, :] * mask[:, k - 1 : k]
    return z


def block_terms(dt, vec, mask, docr):
    step = softplus(dt + vec[0])
    log_decay = -step * vec[1]
    rows, cols = iota((SPAN, SPAN), 0), iota((SPAN, SPAN), 1)
    lower = rows >= cols
    running = exact_left(lower.astype(F32).astype(BF16), log_decay)
    turned = running.T
    allowed = lower & (mask[:, 8:9] == docr)
    decays = []
    for h in (0, 1):
        gaps = running[:, h * HEAD : h * HEAD + 1] - turned[h * HEAD : h * HEAD + 1, :]
        decays.append(jnp.exp(jnp.where(allowed, gaps, -1e30)))
    reach = jnp.exp(running) * mask[:, 6:7]
    total = running[SPAN - 1 :, :]
    tail = jnp.exp(total - running) * mask[:, 7:8]
    carry = jnp.exp(total) * mask[SPAN - 1 :, 6:7]
    return step, log_decay, decays, reach, tail, carry


def layer_constants(con):
    return con[5:6, :HC], con[5:6, HC : 2 * HC], con[5:6, 2 * HC : 3 * HC], con[6:7, :HC]


def pre_gain_of(con):
    return jnp.concatenate([con[k : k + 1, 3 * HC : 4 * HC] for k in range(8)], axis=1)


def head_ones():
    return (iota((16, HC), 0) == iota((16, HC), 1) // HEAD).astype(F32).astype(BF16)


def head_firsts():
    return (iota((HC, 16), 0) == iota((HC, 16), 1) * HEAD).astype(F32).astype(BF16)


def lanes_of(columns, rows):
    lane = iota((rows, AUX), 1)
    out = jnp.zeros((rows, AUX), F32)
    for k, column in enumerate(columns):
        out = jnp.where(lane == k, column.astype(F32), out)
    return out.astype(BF16)


def at_block(b):
    return pl.ds(pl.multiple_of(b * SPAN, SPAN), SPAN)


def fwd_step(layer, b, s):
    vh = s.vh.at[layer, b]
    rows = at_block(b)

    @pl.when(b == 0)
    def _():
        vh[0:8, :] = jnp.zeros((8, 3 * HC), F32)
        s.state[...] = jnp.zeros_like(s.state)

    @pl.when(b != 0)
    def _():
        vh[0:8, :] = s.vh[layer, jnp.maximum(b - 1, 0), SPAN:, :]

    width = s.wo.shape[2]
    chunk = s.wt.shape[3]
    mask = s.mask[rows, :]
    con = s.cons[layer]
    vec = layer_constants(con)
    conv = con[:, : 3 * HC]
    proj = dot_nt(s.n[layer, rows, 0:chunk], s.wt[layer, 0])
    for k in range(1, SIDE):
        proj = proj + dot_nt(s.n[layer, rows, k * chunk : (k + 1) * chunk], s.wt[layer, k])
    gate = proj[:, :HC]
    v = proj[:, HC : 4 * HC].astype(BF16).astype(F32)
    dt = dot_nn(proj[:, 4 * HC :].astype(BF16), head_ones())
    vh[8:, :] = v
    z = conv_rows(vh, conv, mask)
    act = z * sigmoid(z)
    xc = act[:, :HC]
    b16 = act[:, HC : 2 * HC].astype(BF16)
    c16 = act[:, 2 * HC :].astype(BF16)
    step, _, decays, reach, tail, carry = block_terms(dt, vec, mask, s.docr[b, 0:1, :])
    xs = xc * step
    xs16 = xs.astype(BF16)
    scores = dot_nt(c16, b16)
    within = [dot_nn((scores * d).astype(BF16), xs16) for d in decays]
    first = iota((SPAN, HC), 1) < HEAD
    st = s.state[...]
    s.st[layer, b] = st
    scan = jnp.where(first, within[0], within[1]) + dot_nn(c16, st.astype(BF16)) * reach
    s.state[...] = st * carry + dot_tn(b16, (xs * tail).astype(BF16))
    mixed = (scan + xc * vec[2]).astype(BF16)
    g = mixed.astype(F32) * (gate * sigmoid(gate))
    s.part[rows, :width] = dot_nn((g * vec[3]).astype(BF16), s.wo[layer]).astype(BF16)
    s.part[rows, width:] = lanes_of(three(jnp.sum(g * g, axis=1, keepdims=True)), SPAN)
    s.gate[layer, rows, :] = gate
    s.dt[layer, rows, :] = dt
    s.mix[layer, rows, :] = mixed
    s.scan[layer, rows, :] = scan


def bwd_step(layer, b, s):
    rows_b = at_block(b)
    vbuf = s.vh.at[layer, b]
    gin, gout, small, dzbuf, dstate = s.gin, s.gout, s.small, s.dz, s.state

    @pl.when(b == s.vh.shape[1] - 1)
    def _():
        dzbuf[SPAN:, :] = jnp.zeros((8, 3 * HC), F32)
        dstate[...] = jnp.zeros_like(dstate)
        gin[...] = jnp.zeros_like(gin)
        gout[...] = jnp.zeros_like(gout)
        small[...] = jnp.zeros_like(small)

    width = s.wo.shape[2]
    chunk = s.wt.shape[3]
    mask = s.mask[rows_b, :]
    con = s.cons[layer]
    vec = layer_constants(con)
    conv = con[:, : 3 * HC]
    cot = s.c[layer, rows_b, :width]
    aux = s.c[layer, rows_b, width:].astype(F32)
    r = aux[:, 0:1] + aux[:, 1:2] + aux[:, 2:3]
    pull = aux[:, 3:4] + aux[:, 4:5]
    gate = s.gate[layer, rows_b, :]
    sg = sigmoid(gate)
    silu = gate * sg
    mixed = s.mix[layer, rows_b, :].astype(F32)
    g = mixed * silu
    gain = vec[3]
    dy = dot_nt(cot, s.wo[layer])
    gr = g * r
    gout[...] += dot_tn((gr * gain).astype(BF16), cot)
    d_gain = jnp.sum(dy * gr, axis=0, keepdims=True)
    dg = dy * (r * gain) - g * pull
    dm16 = (dg * silu).astype(BF16)
    dm = dm16.astype(F32)
    dgate = dg * mixed * (sg * (1.0 + gate * (1.0 - sg)))

    z = conv_rows(vbuf, conv, mask)
    sz = sigmoid(z)
    act = z * sz
    xc = act[:, :HC]
    b16 = act[:, HC : 2 * HC].astype(BF16)
    c16 = act[:, 2 * HC :].astype(BF16)
    dt = s.dt[layer, rows_b, :]
    step, log_decay, decays, reach, tail, carry = block_terms(dt, vec, mask, s.docr[b, 0:1, :])
    xs16 = (xc * step).astype(BF16)
    xs = xs16.astype(F32)
    scores = dot_nt(c16, b16)
    first = iota((SPAN, HC), 1) < HEAD
    zero16 = jnp.zeros((SPAN, HC), BF16)
    dscores = jnp.zeros((SPAN, SPAN), F32)
    dxs = []
    for h in (0, 1):
        own = jnp.where(first, dm16, zero16) if h == 0 else jnp.where(first, zero16, dm16)
        dp = dot_nt(own, xs16)
        dscores = dscores + dp * decays[h]
        dxs.append(dot_tn((scores * decays[h]).astype(BF16), dm16))
    ds16 = dscores.astype(BF16)
    st = s.st[layer, b]
    dst = dstate[...]
    dst16 = dst.astype(BF16)
    dcs16 = (dm * reach).astype(BF16)
    dc = dot_nn(ds16, b16) + dot_nt(dcs16, st.astype(BF16))
    db = dot_tn(ds16, c16) + dot_nt((xs * tail).astype(BF16), dst16)
    dxs_tail = dot_nn(b16, dst16) * tail
    dxs_all = jnp.where(first, dxs[0], dxs[1]) + dxs_tail
    dstate[...] = dst * carry + dot_tn(c16, dcs16)

    d_total = jnp.sum(xs * dxs_tail, axis=0, keepdims=True) + carry * jnp.sum(
        dst * st, axis=0, keepdims=True
    )
    flow = dm * s.scan[layer, rows_b, :] - xs * dxs_all
    rows, cols = iota((SPAN, SPAN), 0), iota((SPAN, SPAN), 1)
    upper = (cols >= rows).astype(F32).astype(BF16)
    flow = exact_left(upper, flow) + d_total
    same_head = ((iota((HC, HC), 0) < HEAD) == (iota((HC, HC), 1) < HEAD)).astype(F32).astype(BF16)
    d_log = exact_right(flow, same_head)
    d_step = exact_right(dxs_all * xc, same_head) - d_log * vec[1]
    d_alog = jnp.sum(d_log * log_decay, axis=0, keepdims=True)
    d_dt = d_step * sigmoid(dt + vec[0])
    d_skip = jnp.sum(dm * xc, axis=0, keepdims=True)
    d_xc = dm * vec[2] + dxs_all * step

    dact = sz * (1.0 + z * (1.0 - sz))
    dzbuf[:SPAN, 0:HC] = d_xc * dact[:, :HC]
    dzbuf[:SPAN, HC : 2 * HC] = db * dact[:, HC : 2 * HC]
    dzbuf[:SPAN, 2 * HC :] = dc * dact[:, 2 * HC :]
    dz = dzbuf[:SPAN, :]
    dv = dz * conv[3:4, :]
    small[3:4, : 3 * HC] += jnp.sum(dz * vbuf[pl.ds(8, SPAN), :], axis=0, keepdims=True)
    small[4:5, : 3 * HC] += jnp.sum(dz, axis=0, keepdims=True)
    for k in (1, 2, 3):
        dv = dv + dzbuf[pl.ds(k, SPAN), :] * conv[3 - k : 4 - k, :] * mask[:, 2 + k : 3 + k]
        small[3 - k : 4 - k, : 3 * HC] += jnp.sum(
            dz * vbuf[pl.ds(8 - k, SPAN), :] * mask[:, k - 1 : k], axis=0, keepdims=True
        )
    dzbuf[SPAN:, :] = dz[:8, :]
    small[5:6, 0:HC] += d_gain
    small[5:6, HC : 2 * HC] += d_skip
    small[6:7, 0:HC] += jnp.sum(d_dt, axis=0, keepdims=True)
    small[6:7, HC : 2 * HC] += d_alog

    gp = jnp.concatenate([dgate.astype(BF16), dv.astype(BF16)], axis=1)
    gdt = dot_nn(d_dt.astype(BF16), head_firsts()).astype(BF16)
    wide = 4 * HC
    n = s.n[layer, rows_b, :]
    gin[:wide] += dot_nn(gp.T, n)
    gin[wide:] += dot_tn(gdt, n)
    for k in range(SIDE):
        cols_k = slice(k * chunk, (k + 1) * chunk)
        term = dot_nn(gp, s.wt[layer, k, :wide]) + dot_nn(gdt, s.wt[layer, k, wide:])
        s.part[rows_b, cols_k] = term.astype(BF16)
        d_pre = jnp.sum(term * n[:, cols_k].astype(F32), axis=0, keepdims=True)
        small[2 * k : 2 * k + 1, 3 * HC :] += d_pre[:, :HC]
        small[2 * k + 1 : 2 * k + 2, 3 * HC :] += d_pre[:, HC:]


def place_of(half, f, s):
    f, s = lax.rem(f, SIDE), lax.rem(s, SIDE)
    return s * SIDE + f if half == 0 else f * SIDE + s


def ring_places():
    me = lax.axis_index(AXIS)
    return me % SIDE, me // SIDE


def ring_neighbours():
    x, y = ring_places()
    steps = ((1, 0), (3, 0), (0, 1), (0, 3))
    return [{AXIS: place_of(0, x + dx, y + dy)} for dx, dy in steps]


def plane_neighbours():
    z = lax.axis_index("wshard")
    return [{"wshard": lax.rem(z + 1, SIDE)}, {"wshard": lax.rem(z + 3, SIDE)}]


def plane_across():
    return {"wshard": lax.rem(lax.axis_index("wshard") + 2, SIDE)}


def other_core():
    return {"section": 1 - lax.axis_index("section")}


def greet(targets):
    barrier = pltpu.get_barrier_semaphore()
    for target in targets:
        pl.semaphore_signal(barrier, inc=1, device_id=target, device_id_type=MESH)


def greeted(count):
    pl.semaphore_wait(pltpu.get_barrier_semaphore(), count)


def run(*parts, until=None):
    live = list(parts)
    while live if until is None else until in live:
        for part in list(live):
            try:
                next(part)
            except StopIteration:
                live.remove(part)
    return live


class Sender:
    def __init__(self, send, recv):
        self.send, self.recv, self.used, self.copies, self.free = send, recv, 0, {}, set()

    def make(self, name, source, target, to):
        copy = pltpu.make_async_remote_copy(
            src_ref=source, dst_ref=target, send_sem=self.send.at[self.used],
            recv_sem=self.recv.at[self.used], device_id=to, device_id_type=MESH,
        )
        self.used += 1
        self.copies[name] = copy
        return copy

    def go(self, name, source, target, to):
        self.make(name, source, target, to).start()
        self.free.add(name)

    def arrived(self, name):
        self.copies[name].wait_recv()

    def sent(self):
        for name in self.copies:
            if name in self.free:
                self.copies[name].wait_send()


def rows_at(ref, start, size):
    return ref.at[pl.ds(pl.multiple_of(start, 16), size)]


def spread_steps(x_ref, o_ref, out, own, tag=""):
    x, y = ring_places()
    rows = x_ref.shape[0]
    half_rows, quarter = rows // 2, rows // 4
    mine = pltpu.make_async_copy(x_ref, rows_at(o_ref, place_of(0, x, y) * rows, rows), own)
    mine.start()
    firsts = ((x, y), (y, x))

    def go(name, half, block, offset, size, to, source=None):
        place = rows_at(o_ref, block * rows + half * half_rows + offset, size)
        out.go((tag, half, name), place if source is None else source, place, {AXIS: to})

    def across(half, d):
        f, s = firsts[half]
        block = place_of(half, f + d, s)
        source = x_ref.at[pl.ds(half * half_rows, half_rows)] if d == 0 else None
        go(("t1", d), half, block, 0, half_rows, place_of(half, f, s + 1), source)
        go(("t2", d), half, block, 0, half_rows, place_of(half, f, s + 3), source)

    def onward(half, d):
        f, s = firsts[half]
        out.arrived((tag, half, ("t1", d)))
        go(("u1", d), half, place_of(half, f + d, s + 3), 0, quarter, place_of(half, f, s + 1))
        out.arrived((tag, half, ("t2", d)))
        go(("u2", d), half, place_of(half, f + d, s + 1), quarter, quarter, place_of(half, f, s + 3))

    for half in (0, 1):
        f, s = firsts[half]
        source = x_ref.at[pl.ds(half * half_rows, half_rows)]
        block = place_of(half, f, s)
        go("s1", half, block, 0, half_rows, place_of(half, f + 1, s), source)
        go("s2", half, block, 0, half_rows, place_of(half, f + 3, s), source)
    for half in (0, 1):
        across(half, 0)
    yield
    for half in (0, 1):
        f, s = firsts[half]
        out.arrived((tag, half, "s1"))
        go("s3", half, place_of(half, f + 3, s), 0, quarter, place_of(half, f + 1, s))
        out.arrived((tag, half, "s2"))
        go("s4", half, place_of(half, f + 1, s), quarter, quarter, place_of(half, f + 3, s))
    for half in (0, 1):
        across(half, 3)
        across(half, 1)
    yield
    for half in (0, 1):
        onward(half, 0)
    for half in (0, 1):
        out.arrived((tag, half, "s3"))
        out.arrived((tag, half, "s4"))
        across(half, 2)
    yield
    for d in (3, 1, 2):
        for half in (0, 1):
            onward(half, d)
        yield
    for half in (0, 1):
        for d in range(SIDE):
            out.arrived((tag, half, ("u1", d)))
            out.arrived((tag, half, ("u2", d)))
    mine.wait()


def collect_scratch(rows, cols):
    half_rows, quarter = rows // 2, rows // 4
    return [
        pltpu.VMEM((2, SIDE, 2, quarter, cols), BF16),
        pltpu.VMEM((2, SIDE, 2, half_rows, cols), BF16),
        pltpu.VMEM((2, SIDE, 2, half_rows, cols), BF16),
        pltpu.VMEM((2, SIDE, half_rows, cols), BF16),
        pltpu.VMEM((2, SIDE, half_rows, cols), BF16),
        pltpu.VMEM((rows, cols), F32),
    ]


def collect_steps(x_ref, buffers, out, wide):
    cols = pl.ds(0, wide)
    far, near, stage, stage2, last = [a.at[..., cols] for a in buffers[:5]]
    x_ref, o_ref = x_ref.at[:, cols], buffers[5].at[:, cols]
    x, y = ring_places()
    rows = o_ref.shape[0]
    half_rows, quarter = rows // 2, rows // 4
    firsts = ((x, y), (y, x))
    order = (2, 1, 3, 0)

    def go(name, half, source, target, to):
        out.go((half, name), source, target, {AXIS: to})

    def start_of(half, f, s):
        return pl.multiple_of(place_of(half, f, s) * rows + half * half_rows, 16)

    for d in order:
        for half in (0, 1):
            f, s = firsts[half]
            start = start_of(half, f + d, s + 2)
            go(("a1", d), half, rows_at(x_ref, start, quarter), far.at[half, d, 0],
               place_of(half, f, s + 1))
            go(("a2", d), half, rows_at(x_ref, start + quarter, quarter), far.at[half, d, 1],
               place_of(half, f, s + 3))
    yield
    for d in order:
        for half in (0, 1):
            f, s = firsts[half]
            for side, step in enumerate((1, 3)):
                start = start_of(half, f + d, s + step)
                plain, through = quarter * (1 - side), quarter * side
                stage[half, d, side, pl.ds(plain, quarter)] = x_ref[
                    pl.ds(pl.multiple_of(start + plain, 16), quarter), :
                ]
                out.arrived((half, (("a1", "a2")[side], d)))
                stage[half, d, side, pl.ds(through, quarter)] = (
                    x_ref[pl.ds(pl.multiple_of(start + through, 16), quarter), :].astype(F32)
                    + far[half, d, side].astype(F32)
                ).astype(BF16)
                go((("b1", "b2")[side], d), half, stage.at[half, d, side], near.at[half, d, side],
                   place_of(half, f, s + step))
        if d in (1, 0):
            yield

    def summed(half, d):
        f, s = firsts[half]
        out.arrived((half, ("b1", d)))
        out.arrived((half, ("b2", d)))
        return (
            x_ref[pl.ds(start_of(half, f + d, s), half_rows), :].astype(F32)
            + near[half, d, 0].astype(F32) + near[half, d, 1].astype(F32)
        )

    for d in order[:3]:
        for half in (0, 1):
            f, s = firsts[half]
            stage2[half, d] = summed(half, d).astype(BF16)
            go(("first", d), half, stage2.at[half, d], last.at[half, d], place_of(half, f + d, s))
        yield
    for half in (0, 1):
        o_ref[pl.ds(half * half_rows, half_rows), :] = summed(half, 0)
    yield
    for half in (0, 1):
        own = pl.ds(half * half_rows, half_rows)
        total = o_ref[own, :]
        for d in (1, 3, 2):
            out.arrived((half, ("first", d)))
            total = total + last[half, d].astype(F32)
        o_ref[own, :] = total


def half_of(rows):
    return rows // 32 * 16


def fold_scratch(count):
    scratch = [pltpu.VMEM((8, 4 * HC), F32)] * 2 + [pltpu.VMEM((3, 8, 4 * HC), F32)]
    for rows, cols in ((FR, 256), (HC // SIDE, 1024)):
        scratch += [pltpu.VMEM((SIDE, rows, cols), BF16)] * 3
        scratch += [pltpu.VMEM((2, rows - half_of(rows), cols), BF16)]
        scratch += [pltpu.VMEM((2, rows, cols), BF16)]
    scratch += [pltpu.VMEM((2 * NS, 1024), BF16), pltpu.VMEM((count, 16, 1024), BF16)]
    scratch += [pltpu.VMEM((SIDE, 16, 256), BF16)] * 3 + [pltpu.VMEM((3, 16, 256), BF16)]
    return scratch


def bc_steps(gin, buffers, out):
    me, count = lax.axis_index(AXIS), lax.axis_size(AXIS)
    terms, landing, mine = buffers[13], buffers[14], buffers[15]
    terms[...] = gin[2 * HC : 4 * HC, :].astype(BF16)
    for d in range(1, count):
        to = lax.rem(me + d, count)
        out.go(("bc", d), rows_at(terms, to * 16, 16), landing.at[d], {AXIS: to})
    yield
    yield
    total = terms[pl.ds(pl.multiple_of(me * 16, 16), 16), :].astype(F32)
    for d in range(1, count):
        out.arrived(("bc", d))
        total = total + landing[d].astype(F32)
    for k in range(SIDE):
        mine[k] = total[:, k * 256 : (k + 1) * 256].astype(BF16)
    yield


def fold_steps(layer, gin, gout, fin_ref, fout_ref, buffers, out):
    z = lax.axis_index("wshard")
    up, down = plane_neighbours()
    owner = lax.axis_index("section") == layer
    ours_in, land_in, total_in, far_in, near_in = buffers[3:8]
    ours_out, land_out, total_out, far_out, near_out = buffers[8:13]
    piece = HC // SIDE
    for k in range(SIDE):
        cols = slice(k * 256, (k + 1) * 256)
        ours_in[k, : 2 * HC] = gin[: 2 * HC, cols].astype(BF16)
        ours_in[k, 2 * HC :] = gin[4 * HC :, cols].astype(BF16)
        ours_out[k] = gout[k * piece : (k + 1) * piece, :].astype(BF16)
    arrays = (
        (ours_in, land_in, total_in, far_in, near_in, fin_ref),
        (ours_out, land_out, total_out, far_out, near_out, fout_ref),
    )

    def at(d):
        return lax.rem(z + d, SIDE)

    swaps, legs = {}, {}
    parts = []
    for ours in (ours_in, ours_out):
        half = half_of(ours.shape[1])
        parts.append((pl.ds(0, half), pl.ds(half, ours.shape[1] - half)))
    for d in (2, 1, 3, 0):
        for k, (ours, land, *_) in enumerate(arrays):
            swaps[k, d] = out.make(("swap", k, d), ours.at[at(d)], land.at[at(d)], other_core())
    for k, (_, _, total, far, near, _) in enumerate(arrays):
        for side, to in enumerate((up, down)):
            some = parts[k][side]
            legs[k, "far", side] = out.make(
                ("far", k, side), total.at[at(2), some], far.at[side, pl.ds(0, some.size)], to
            )
        legs[k, "near", 0] = out.make(("near", k, 0), total.at[at(1)], near.at[0], up)
        legs[k, "near", 1] = out.make(("near", k, 1), total.at[at(3)], near.at[1], down)

    @pl.when(jnp.logical_not(owner))
    def _():
        for copy in swaps.values():
            copy.start()

    yield

    def add_cores(d):
        for k, (ours, land, total, *_) in enumerate(arrays):
            swaps[k, d].wait_recv()
            total[at(d)] = (ours[at(d)].astype(F32) + land[at(d)].astype(F32)).astype(BF16)

    @pl.when(owner)
    def _():
        add_cores(2)
        for k in (0, 1):
            legs[k, "far", 0].start()
            legs[k, "far", 1].start()

    yield
    for side, d in ((0, 1), (1, 3)):
        @pl.when(owner)
        def _():
            add_cores(d)
            for k, (_, _, total, far, _, _) in enumerate(arrays):
                legs[k, "far", side].wait_recv()
                some = parts[k][side]
                total[at(d), some] = (
                    total[at(d), some].astype(F32) + far[side, pl.ds(0, some.size)].astype(F32)
                ).astype(BF16)
                legs[k, "near", side].start()

        yield

    @pl.when(owner)
    def _():
        add_cores(0)
        for k, (_, _, total, _, near, done) in enumerate(arrays):
            legs[k, "near", 0].wait_recv()
            legs[k, "near", 1].wait_recv()
            done[...] = (
                total[at(0)].astype(F32) + near[0].astype(F32) + near[1].astype(F32)
            ).astype(BF16)
        for leg in legs.values():
            leg.wait_send()

    @pl.when(jnp.logical_not(owner))
    def _():
        for copy in swaps.values():
            copy.wait_send()


def fold_small(layer, small, gains, done_ref, bc_ref, buffers, out):
    small[:, 3 * HC :] = small[:, 3 * HC :] / gains
    owner = lax.axis_index("section") == layer
    z = lax.axis_index("wshard")
    land, total, planes = buffers[:3]
    mine, land_bc, total_bc, planes_bc = buffers[15:19]
    up, down = plane_neighbours()
    swaps = [
        out.make("small", small, land, other_core()), out.make("bc", mine, land_bc, other_core()),
    ]
    legs = []
    for k, (d, to) in enumerate(((1, up), (3, down), (2, plane_across()))):
        legs.append(out.make(("small", k), total, planes.at[k], to))
        legs.append(out.make(
            ("bc", k), total_bc.at[lax.rem(z + d, SIDE)], planes_bc.at[k], to))

    @pl.when(jnp.logical_not(owner))
    def _():
        for swap in swaps:
            swap.start()

    @pl.when(owner)
    def _():
        for swap in swaps:
            swap.wait_recv()
        total[...] = small[...] + land[...]
        total_bc[...] = (mine[...].astype(F32) + land_bc[...].astype(F32)).astype(BF16)
        for leg in legs:
            leg.start()

    yield

    @pl.when(owner)
    def _():
        for leg in legs:
            leg.wait_recv()
        done_ref[...] = total[...] + planes[0] + planes[1] + planes[2]
        sum_bc = total_bc[z].astype(F32)
        for k in range(3):
            sum_bc = sum_bc + planes_bc[k].astype(F32)
        bc_ref[...] = sum_bc.astype(BF16)
        for leg in legs:
            leg.wait_send()

    @pl.when(jnp.logical_not(owner))
    def _():
        for swap in swaps:
            swap.wait_send()


def closing_steps(s, layer_sums, out, own):
    x, y = ring_places()
    z = lax.axis_index("wshard")
    first = lax.axis_index("section") == 0
    fin, bc, fout, small = [
        jnp.where(first, a[...], b[...]) for a, b in zip(layer_sums[0], layer_sums[1])
    ]
    s.turning[...] = fout
    turned = {AXIS: place_of(0, x, z), "wshard": y}
    turn = out.make("turn", s.turning, s.came, turned)

    @pl.when(z != y)
    def _():
        turn.start()

    s.block[0 : 2 * HC, :] = fin[: 2 * HC]
    s.block[2 * HC : 2 * HC + 16, :] = bc
    s.block[2 * HC + 16 : 2 * HC + 32, :] = fin[2 * HC :]
    hi, mid, _ = three(jnp.concatenate([small[:, :256], small[:, 256:]]))
    s.block[END_ROWS - 32 : END_ROWS - 16, :] = hi
    s.block[END_ROWS - 16 :, :] = mid
    main = spread_steps(s.block, s.gathered, out, own.at[2], "in")
    next(main)
    yield
    next(main)

    @pl.when(z != y)
    def _():
        turn.wait_recv()

    @pl.when(z == y)
    def _():
        s.came[...] = s.turning[...]

    for c in range(4):
        s.wide_rows[32 * c : 32 * (c + 1), :] = s.came[:, c * 256 : (c + 1) * 256]
    side = spread_steps(s.wide_rows, s.pieces, out, own.at[3], "out")
    live = [main, side]
    while live:
        for part in list(live):
            try:
                next(part)
            except StopIteration:
                live.remove(part)
        yield

    @pl.when(z != y)
    def _():
        turn.wait_send()


def norm_rows(u):
    return u * lax.rsqrt(jnp.mean(u * u, axis=1, keepdims=True) + EPS)


def payload_into(ref, c, branch, r, inner):
    width = c.shape[1]
    low = c.astype(BF16)
    pull = r * r * jnp.sum(low.astype(F32) * branch, axis=1, keepdims=True) / inner
    ref[:, :width] = low
    ref[:, width:] = lanes_of(list(three(r)) + list(three(pull))[:2], c.shape[0])


def constants_into(con, params):
    cw_ref, cb_ref, dtb_ref, alog_ref, skip_ref, pre_ref, gain_ref = params
    q = lax.axis_index(AXIS)
    inner = gain_ref.shape[1]
    own = pl.ds(pl.multiple_of(q * HC, HC), HC)
    con[...] = jnp.zeros_like(con)
    con[0:4, :HC] = cw_ref[0, :, own]
    con[0:4, HC : 3 * HC] = cw_ref[0, :, inner:]
    con[4:5, :HC] = cb_ref[:, own]
    con[4:5, HC : 3 * HC] = cb_ref[:, inner:]

    def lanes(ref):
        value = ref[...]
        lane = iota(value.shape, 1)
        two = [
            jnp.sum(jnp.where(lane == 2 * q + h, value, 0.0), axis=1, keepdims=True) for h in (0, 1)
        ]
        return jnp.where(iota((1, HC), 1) < HEAD, two[0], two[1])

    con[5:6, :HC] = lanes(dtb_ref)
    con[5:6, HC : 2 * HC] = jnp.exp(lanes(alog_ref))
    con[5:6, 2 * HC : 3 * HC] = lanes(skip_ref)
    con[6:7, :HC] = gain_ref[:, own]
    for k in range(8):
        con[k : k + 1, 3 * HC :] = pre_ref[:, k * HC : (k + 1) * HC]


def mask_steps(doc_ref, mask_ref, docr_ref):
    yield
    doc = doc_ref[lax.axis_index("section")].astype(F32)
    length = doc.shape[1]
    doc8 = jnp.broadcast_to(doc, (8, length))
    for b in range(length // SPAN):
        docr_ref[b] = doc8[:, b * SPAN : (b + 1) * SPAN]
    at = iota((8, length), 1)
    rows = []
    for k in (1, 2, 3):
        rows.append((pltpu.roll(doc8, k, 1) == doc8) & (at >= k))
    for k in (1, 2, 3):
        rows.append((pltpu.roll(doc8, length - k, 1) == doc8) & (at < length - k))
    before, final = doc8, doc8
    for b in range(length // SPAN):
        inside = (at >= b * SPAN) & (at < (b + 1) * SPAN)
        start = max(b * SPAN - 1, 0)
        end = (b + 1) * SPAN - 1
        before = jnp.where(inside, doc[:, start : start + 1], before)
        final = jnp.where(inside, doc[:, end : end + 1], final)
    rows += [before == doc8, final == doc8]
    sub = iota((8, length), 0)
    first = jnp.zeros((8, length), F32)
    for k, row in enumerate(rows):
        first = jnp.where((sub == k) & row, 1.0, first)
    both = jnp.concatenate([first, doc8, jnp.zeros((HC - 16, length), F32)])
    mask_ref[...] = both.T


def sems(count):
    return [pltpu.SemaphoreType.DMA((count,)), pltpu.SemaphoreType.DMA((count,))]


def weights_steps(layer, wo_ref, s, out, own):
    x, y = ring_places()
    z = lax.axis_index("wshard")
    holder = lax.axis_index("section") == layer

    def at(d):
        return lax.rem(z + d, SIDE)

    def to(d):
        return {"wshard": at(d)}

    hops = (2, 1, 3)
    mine = pltpu.make_async_copy(s.own_w, s.wt.at[layer, z], own.at[4])
    rows = {d: out.make(("w", d), s.own_w, s.wt.at[layer, z], to(d)) for d in hops}
    role = at(SIDE - y)
    target = s.wo.at[layer]
    source = wo_ref.at[0, pl.ds(pl.multiple_of(x * HC, HC), HC)]
    mine_wo = pltpu.make_async_copy(source, target, own.at[5])
    rows_wo = {d: out.make(("wo", d), source, target, to(d)) for d in hops}
    swaps = {}
    for d in range(SIDE):
        block = s.wt.at[layer, at(SIDE - d)]
        swaps[d] = out.make(("swap", d), block, block, other_core())
    swap_wo = out.make("swap_wo", target, target, other_core())

    @pl.when(holder)
    def _():
        mine.start()
        for copy in rows.values():
            copy.start()

    @pl.when(holder & (role == 0))
    def _():
        mine_wo.start()
        for copy in rows_wo.values():
            copy.start()

    yield

    @pl.when(holder)
    def _():
        mine.wait()
        swaps[0].start()

    yield
    for d in (1, 3, 2):
        @pl.when(holder)
        def _():
            rows[d].wait_recv()
            swaps[d].start()

        yield

    @pl.when(holder & (role == 0))
    def _():
        mine_wo.wait()

    for d in hops:
        @pl.when(holder & (role == d))
        def _():
            rows_wo[d].wait_recv()

    @pl.when(holder)
    def _():
        swap_wo.start()

    yield

    @pl.when(jnp.logical_not(holder))
    def _():
        for copy in swaps.values():
            copy.wait_recv()
        swap_wo.wait_recv()

    @pl.when(holder)
    def _():
        for copy in list(rows.values()) + list(swaps.values()) + [swap_wo]:
            copy.wait_send()

    @pl.when(holder & (role == 0))
    def _():
        for copy in rows_wo.values():
            copy.wait_send()


def hand_over(layer, rows, target, copy_sem, out, name):
    part = lax.axis_index("section")
    keep = pltpu.make_async_copy(rows, target.at[part], copy_sem)
    give = out.make(name, rows, target.at[part], other_core())

    @pl.when(part == layer)
    def _():
        keep.start()

    @pl.when(part != layer)
    def _():
        give.start()

    def finish():
        @pl.when(part == layer)
        def _():
            keep.wait()
            give.wait_recv()

        @pl.when(part != layer)
        def _():
            give.wait_send()

    return finish


class Scratch:
    def __init__(self, refs):
        self.__dict__.update(refs)


def scratch_shapes(count, rows, width, heads, params, doc_shape):
    length = count * rows
    blocks = length // SPAN
    wide = width + AUX
    half_rows, quarter = rows // 2, rows // 4
    shapes = {
        "n": ((2, length, width), BF16), "c": ((2, length, wide), BF16),
        "wt": ((2, SIDE, WR, 256), BF16), "wo": ((2, HC, width), BF16),
        "cons": ((2, 8, 4 * HC), F32), "mask": ((length, HC), F32),
        "docr": ((blocks, 8, SPAN), F32),
        "vh": ((2, blocks, SPAN + 8, 3 * HC), F32), "gate": ((2, length, HC), F32),
        "dt": ((2, length, HC), F32), "mix": ((2, length, HC), BF16),
        "scan": ((2, length, HC), F32), "st": ((2, blocks, NS, HC), F32),
        "state": ((NS, HC), F32), "dz": ((SPAN + 8, 3 * HC), F32),
        "part": ((length, wide), BF16), "gin": ((WR, width), F32), "gout": ((HC, width), F32),
        "small": ((8, 4 * HC), F32),
        "u": ((rows, width), F32), "h": ((2, rows, width), F32), "branch": ((rows, width), F32),
        "r": ((rows, HC), F32), "g": ((2, rows, width), F32),
        "own_n": ((rows, width), BF16), "own_c": ((rows, wide), BF16),
        "x_in": ((rows, width), BF16), "og_in": ((rows, width), BF16),
        "doc_in": (doc_shape, jnp.int32), "own_w": ((WR, 256), BF16), "dts": ((heads, 256), BF16),
        "turning": ((HC // SIDE, width), BF16), "came": ((HC // SIDE, width), BF16),
        "block": ((END_ROWS, 256), BF16), "wide_rows": ((HC, 256), BF16),
        "gathered": ((count * END_ROWS, 256), BF16), "pieces": ((count * HC, 256), BF16),
    }
    for k, p in enumerate(params):
        shapes["param%d" % k] = (p.shape, F32)
    for l in (0, 1):
        shapes["fin%d" % l] = ((FR, 256), BF16)
        shapes["bc%d" % l] = ((16, 256), BF16)
        shapes["fout%d" % l] = ((HC // SIDE, width), BF16)
        shapes["fsmall%d" % l] = ((8, 4 * HC), F32)
    return shapes


def layers_kernel(inner, names, x_ref, og_ref, w_ref, wo_ref, doc_ref, *refs):
    params, (hid_ref, ing_ref, next_ref, pieces_ref), refs = refs[:7], refs[7:11], refs[11:]
    s = Scratch(zip(names, refs))
    refs = refs[len(names) :]
    sem_pairs, (own, fetch), buffers = refs[:14], refs[14:16], refs[16:]
    collecting, folding = buffers[:6], buffers[6:]
    sems_of = [tuple(sem_pairs[2 * k : 2 * k + 2]) for k in range(7)]
    i = pl.program_id(0)
    blocks = s.vh.shape[1]
    phase, at = i // blocks, lax.rem(i, blocks)
    part, z = lax.axis_index("section"), lax.axis_index("wshard")
    q, count = lax.axis_index(AXIS), lax.axis_size(AXIS)
    x, y = ring_places()
    width = s.u.shape[1]
    wide = s.part.shape[1]
    handing = Sender(*sems_of[5])

    @pl.when(i == 0)
    def _():
        targets = [{AXIS: lax.rem(q + d, count)} for d in range(1, count)]
        targets += [{"wshard": lax.rem(z + d, SIDE)} for d in (1, 2, 3)] + [other_core()]
        greet(targets)

        @pl.when(z != y)
        def _():
            greet([{AXIS: place_of(0, x, z), "wshard": y}])

        held = [s.__dict__["param%d" % k] for k in range(7)]
        first = (w_ref.shape[0] - 2 * NS) // 2 // HC * HC
        pieces = list(zip(params, held))
        pieces += [(x_ref.at[part, 0], s.x_in)]
        pieces += [
            (w_ref.at[pl.ds(pl.multiple_of(q * HC, HC), HC)], s.own_w.at[pl.ds(0, HC)]),
            (w_ref.at[pl.ds(pl.multiple_of(first + q * HC, HC), HC)], s.own_w.at[pl.ds(HC, HC)]),
            (w_ref.at[pl.ds(2 * first, 2 * NS)], s.own_w.at[pl.ds(2 * HC, 2 * NS)]),
            (w_ref.at[pl.ds(2 * first + 2 * NS, s.dts.shape[0])], s.dts),
            (doc_ref, s.doc_in), (og_ref.at[part, 0], s.og_in),
        ]
        copies = [
            pltpu.make_async_copy(source, target, fetch.at[k])
            for k, (source, target) in enumerate(pieces)
        ]
        for copy in copies:
            copy.start()
        for copy in copies[:7]:
            copy.wait()
        constants_into(s.cons.at[part], held)
        copies[7].wait()
        u = s.x_in[...].astype(F32)
        s.u[...] = u
        normed = norm_rows(u)
        greeted(len(targets) + (z != y).astype(jnp.int32))
        out, planes = Sender(*sems_of[0]), Sender(*sems_of[1])
        planes.go("con", s.cons.at[part], s.cons.at[part], other_core())

        def prepare():
            for copy in copies[8:12]:
                copy.wait()
            heads = s.dts.shape[0]
            pick = (iota((16, heads), 1) == 2 * q + iota((16, heads), 0)) & (
                iota((16, heads), 0) < 2
            )
            pick = pick.astype(F32).astype(BF16)
            s.own_w[4 * HC :, :] = dot_nn(pick, s.dts[...]).astype(BF16)
            weights = weights_steps(0, wo_ref, s, planes, own)
            next(weights)
            yield
            for copy in copies[12:]:
                copy.wait()
            masks = mask_steps(s.doc_in, s.mask, s.docr)
            next(masks)
            yield
            yield from masks
            yield from weights

        planes.arrived("con")
        s.own_n[...] = (normed * pre_gain_of(s.cons[0])).astype(BF16)
        run(spread_steps(s.own_n, s.n.at[0], out, own.at[0]), prepare())
        out.sent()
        planes.sent()

    @pl.when(phase < 2)
    def _():
        fwd_step(phase, at, s)

    @pl.when(phase >= 2)
    def _():
        bwd_step(3 - phase, blocks - 1 - at, s)

    def normed_sums():
        total = collecting[-1]
        square = total[:, width : width + 1] + total[:, width + 1 : width + 2]
        square = square + total[:, width + 2 : width + 3]
        r = lax.rsqrt(square / inner + EPS)
        return total[:, :width] * r, r

    @pl.when(i == blocks - 1)
    def _():
        out, more, planes = Sender(*sems_of[2]), Sender(*sems_of[0]), Sender(*sems_of[6])
        weights = weights_steps(1, wo_ref, s, planes, own)
        collect = collect_steps(s.part, collecting, out, wide)
        live = run(collect, weights, until=collect)
        branch, r = normed_sums()
        h = s.u[...] + branch
        s.own_n[...] = (norm_rows(h) * pre_gain_of(s.cons[1])).astype(BF16)
        spread = spread_steps(s.own_n, s.n.at[1], more, own.at[0])
        next(spread)
        s.h[0] = h
        s.branch[...] = branch
        s.r[...] = jnp.broadcast_to(r, s.r.shape)
        run(spread, *live)
        out.sent()
        more.sent()
        planes.sent()

    @pl.when(i == 2 * blocks - 1)
    def _():
        out, more = Sender(*sems_of[2]), Sender(*sems_of[0])
        run(collect_steps(s.part, collecting, out, wide))
        branch, r = normed_sums()
        payload_into(s.own_c, s.og_in[...].astype(F32), branch, r, inner)
        spread = spread_steps(s.own_c, s.c.at[1], more, own.at[0])
        next(spread)
        s.h[1] = s.h[0] + branch
        run(spread)
        out.sent()
        more.sent()

    def input_gradient(layer, u, cot):
        g = collecting[-1][:, :width]
        ri = lax.rsqrt(jnp.mean(u * u, axis=1, keepdims=True) + EPS)
        gg = g * pre_gain_of(s.cons[layer])
        dot = jnp.sum(gg * u, axis=1, keepdims=True) / width
        return cot + gg * ri - u * (ri * ri * ri * dot)

    def sums_of(layer):
        return [s.__dict__[name + str(layer)] for name in ("fin", "bc", "fout", "fsmall")]

    def gradients(layer, out, folds):
        fin, bc, fout, fsmall = sums_of(layer)
        gains = s.cons[layer][:, 3 * HC :]
        fold = fold_steps(layer, s.gin, s.gout, fin, fout, folding, folds)
        sums = bc_steps(s.gin, folding, out)
        small = fold_small(layer, s.small, gains, fsmall, bc, folding, folds)
        return fold, sums, small

    @pl.when(i == 3 * blocks - 1)
    def _():
        out, folds, more = Sender(*sems_of[2]), Sender(*sems_of[3]), Sender(*sems_of[0])
        collect = collect_steps(s.part, collecting, out, width)
        fold, bc, small = gradients(1, out, folds)
        live = run(collect, fold, bc, until=collect)
        live = run(*live, until=bc) + [small]
        c = input_gradient(1, s.h[0], s.og_in[...].astype(F32))
        payload_into(s.own_c, c, s.branch[...], s.r[:, 0:1], inner)
        spread = spread_steps(s.own_c, s.c.at[0], more, own.at[0])
        next(spread)
        s.g[1] = c
        run(spread, *live)
        out.sent()
        more.sent()

    @pl.when(i == 4 * blocks - 1)
    def _():
        out, folds, more = Sender(*sems_of[2]), Sender(*sems_of[3]), Sender(*sems_of[4])
        finishers = [
            hand_over(0, s.h.at[0], hid_ref, own.at[6], handing, "h0"),
            hand_over(1, s.h.at[1], hid_ref, own.at[6], handing, "h1"),
            hand_over(1, s.g.at[1], ing_ref, own.at[7], handing, "g1"),
        ]
        collect = collect_steps(s.part, collecting, out, width)
        fold, bc, small = gradients(0, out, folds)
        live = run(collect, fold, bc, until=bc) + [small]
        live = run(*live, until=small)
        live = run(*live, until=fold)
        closing = closing_steps(s, (sums_of(0), sums_of(1)), more, own)
        if collect in live:
            live = run(closing, collect, until=collect)
        else:
            live = [closing]
        s.g[0] = input_gradient(0, s.u[...], s.g[1])
        finishers.append(hand_over(0, s.g.at[0], ing_ref, own.at[7], handing, "g0"))
        run(*live)
        copies = [
            pltpu.make_async_copy(s.gathered, next_ref, own.at[0]),
            pltpu.make_async_copy(s.pieces, pieces_ref, own.at[1]),
        ]
        for copy in copies:
            copy.start()
        out.sent()
        more.sent()
        for finish in finishers:
            finish()
        for copy in copies:
            copy.wait()


def layers(block_input, out_grad, w, wo, doc_ids, *params):
    hbm = pl.BlockSpec(memory_space=pl.ANY)
    rows, width = block_input.shape[2:]
    count = lax.axis_size(AXIS)
    inner = params[-1].shape[1]
    shapes = scratch_shapes(count, rows, width, params[2].shape[1], params, doc_ids.shape)

    def shape(dims, dtype=F32):
        return jax.ShapeDtypeStruct(dims, dtype)

    return pl.pallas_call(
        lambda *refs: layers_kernel(inner, list(shapes), *refs),
        grid=(4 * count * rows // SPAN,),
        in_specs=[hbm] * 12,
        out_specs=[hbm] * 4,
        out_shape=[
            shape((2, rows, width)), shape((2, rows, width)),
            shape((count * END_ROWS, 256), BF16), shape((count * HC, 256), BF16),
        ],
        scratch_shapes=[
            *[pltpu.VMEM(dims, dtype) for dims, dtype in shapes.values()],
            *sems(40), *sems(16), *sems(56), *sems(24), *sems(82), *sems(4), *sems(16),
            pltpu.SemaphoreType.DMA((8,)), pltpu.SemaphoreType.DMA((14,)),
            *collect_scratch(rows, width + AUX), *fold_scratch(count),
        ],
        compiler_params=pltpu.CompilerParams(
            collective_id=1, has_side_effects=True, vmem_limit_bytes=VMEM_ASK
        ),
        name="layers",
    )(block_input, out_grad, w, wo, doc_ids, *params)


def assemble_kernel(
    inner, all_ref, pieces_ref, gin_ref, gout_ref, convw_ref, convb_ref, pre_ref, gain_ref, heads_ref
):
    count = all_ref.shape[0]
    lane = iota((1, HC), 1)
    bc = jnp.zeros((5, 2 * HC), F32)
    pre = jnp.zeros((8, HC), F32)
    per_head = [jnp.zeros((1, HC), F32)] * 3
    for j in range(count):
        own = slice(j * HC, (j + 1) * HC)
        gin_ref[own, :] = all_ref[j, 0:HC, :].astype(F32)
        gin_ref[inner + j * HC : inner + (j + 1) * HC, :] = all_ref[j, HC : 2 * HC, :].astype(F32)
        at = 2 * inner + j * 16
        gin_ref[at : at + 16, :] = all_ref[j, 256:272, :].astype(F32)
        at = 2 * inner + 2 * NS + 2 * j
        gin_ref[at : at + 2, :] = all_ref[j, 272:288, :].astype(F32)[0:2, :]
        big, piece = j % SIDE, j // SIDE
        at = big * HC + piece * 32
        for c in range(4):
            gout_ref[at : at + 32, c * 256 : (c + 1) * 256] = (
                pieces_ref[j, 32 * c : 32 * (c + 1), :].astype(F32)
            )
        small = all_ref[j, END_ROWS - 32 : END_ROWS - 16, :].astype(F32)
        small = small + all_ref[j, END_ROWS - 16 :, :].astype(F32)
        convw_ref[:, own] = small[0:4, :HC]
        convb_ref[:, own] = small[4:5, :HC]
        gain_ref[:, own] = small[5:6, :HC]
        bc = bc + jnp.concatenate([small[0:5, HC:], small[8:13, :HC]], axis=1)
        pre = pre + small[8:16, HC:]
        skip = small[5:6, HC:]
        for h in (0, 1):
            here = lane == 2 * j + h
            mine = (lane >= h * HEAD) & (lane < (h + 1) * HEAD)
            values = (
                small[6:7, h * HEAD : h * HEAD + 1],
                small[6:7, HC + h * HEAD : HC + h * HEAD + 1],
                jnp.sum(jnp.where(mine, skip, 0.0), axis=1, keepdims=True),
            )
            per_head = [jnp.where(here, v, p) for v, p in zip(values, per_head)]
    convw_ref[:, inner:] = bc[0:4]
    convb_ref[:, inner:] = bc[4:5]
    for k in range(8):
        pre_ref[:, k * HC : (k + 1) * HC] = pre[k : k + 1]
    heads_ref[...] = jnp.concatenate(per_head + [jnp.zeros((5, HC), F32)])


def assemble(everyone, pieces, inner, columns, width, channels):
    def shape(*dims):
        return jax.ShapeDtypeStruct(dims, F32)

    vmem = pl.BlockSpec(memory_space=pltpu.VMEM)
    return pl.pallas_call(
        lambda *refs: assemble_kernel(inner, *refs),
        in_specs=[vmem] * 2,
        out_specs=[vmem] * 7,
        out_shape=[
            shape(columns, 256), shape(512, width), shape(4, channels), shape(1, channels),
            shape(1, width), shape(1, inner), shape(8, HC),
        ],
        compiler_params=pltpu.CompilerParams(vmem_limit_bytes=VMEM_ASK),
        name="assemble",
    )(everyone, pieces)


def body(
    block_input, doc_ids, out_grad, in_proj, out_proj, conv_weight, conv_bias,
    dt_bias, a_log, skip_scale, pre_gain, norm_gain,
):
    inner = norm_gain.shape[1]
    width = block_input.shape[3]
    heads = dt_bias.shape[1]
    hidden, input_grads, everyone, pieces = layers(
        block_input, out_grad, jnp.swapaxes(in_proj[0], 0, 1), out_proj, doc_ids,
        conv_weight, conv_bias, dt_bias, a_log, skip_scale, pre_gain, norm_gain,
    )
    everyone = everyone.reshape(-1, END_ROWS, 256)
    pieces = pieces.reshape(-1, HC, 256)
    gin, gout, convw, convb, pre, gain, per_head = assemble(
        everyone, pieces, inner, in_proj.shape[2], width, conv_weight.shape[2]
    )
    return (
        hidden[None, :, None], input_grads[None, :, None],
        jnp.swapaxes(gin, 0, 1)[None], gout[None], convw[None], convb,
        per_head[0:1, :heads], per_head[1:2, :heads], per_head[2:3, :heads], pre, gain,
    )


def solution(mesh):
    specs = (
        P(None, "wshard", "seq", None),
        P(None, "wshard", None),
        P(None, "wshard", "seq", None),
        P("section", "wshard", None),
        P("section", "wshard", None),
        P("section", None, None),
        P("section", None),
        P("section", None),
        P("section", None),
        P("section", None),
        P("section", None),
        P("section", None),
    )
    outs = (
        P("section", None, "wshard", "seq", None),
        P("section", None, "wshard", "seq", None),
        P("section", "wshard", None),
        P("section", "wshard", None),
        P("section", None, None),
    ) + (P("section", None),) * 6
    return jax.shard_map(body, mesh=mesh, in_specs=specs, out_specs=outs, check_vma=False)
```

time: 283 us -> 230 us (0.81)
  Pallas kernels: 254 us -> 226 us
  local copies, waits for them, and re-layouts: 23.7 us -> 2.91 us
    pallas_call x7 -> x1, Pallas kernels: 251 us -> 221 us  [layers(): pl.pallas_call(lambda *refs: layers_kernel(inner, list(shapes), *refs), g...]
    unnamed x60 -> x6, local copies, waits for them, and re-layouts: 23.2 us -> 1.59 us
  transfers between devices with their start and end apart: 2 -> 0, of which waited for: 0 -> 0; matrix products, arithmetic and copies ran while one was open for 0% -> 0% of each run, Pallas kernels for 13% -> 0%
where the time goes in v4:
time: 230 us
  Pallas kernels  226 us (98%)
  local copies, waits for them, and re-layouts  2.91 us (1%)
    pallas_call x1, Pallas kernels, layers(): pl.pallas_call(lambda *refs: layers_kernel(inner, list(shapes), *refs), g...  221 us
    pallas_call x1, Pallas kernels, assemble(): pl.pallas_call(lambda *refs: assemble_kernel(inner, *refs), in_specs=[vme...  5.22 us

profile of v4, /device:TPU:0, one launch (start us, length us, event | category | flops | bytes accessed | tf_op | source)
XLA Modules:
  0.0 229.7 jit_solution(13209117257763495302)
XLA Ops:
  0.6 220.9 %layers.1 = (f32[2,64,1024]{2,1,0:T(8,128)}, f32[2,64,1024]{2,1,0:T(8,128)}, bf16[5120,256]{1,0:T(8,128)(2,1)}, bf16[2048,256]{1,0:T(8,128)(2,1)}) custom-call(bf16[2,1,64,1024]{3,2,1,0:T(8,128)(2,1)} %refs_0_.1, bf16[2,1,64,1024]{3,2,1,0:T(8,128)(2,1)} %refs_1_.1, bf16[4384,256]{1,0:T(8,128)(2,1)} %bitcast.17, bf16[1,512,1024]{2,1,0:T(8,128)(2,1)} %refs_3_.1, ...), custom_call_target="tpu_custom_call" | custom-call | tf_op jit(solution)/shard_map/layers/pallas_call | solution.py:1170
  221.6 0.0 copy-start.1
  221.6 0.0 copy-start
  221.6 5.2 %assemble.1 = (f32[4384,256]{1,0:T(8,128)}, f32[512,1024]{1,0:T(8,128)}, f32[4,2304]{1,0:T(4,128)}, f32[1,2304]{1,0:T(1,128)}, f32[1,1024]{1,0:T(1,128)}, /*index=5*/f32[1,2048]{1,0:T(1,128)}, f32[8,128]{1,0:T(8,128)}) custom-call(bf16[16,320,256]{2,1,0:T(8,128)(2,1)} %bitcast.16, bf16[16,128,256]{2,1,0:T(8,128)(2,1)} %bitcast.18), custom_call_target="tpu_custom_call" | custom-call | tf_op jit(solution)/shard_map/assemble/pallas_call | solution.py:1243
  226.8 1.3 fusion
  228.2 0.0 copy-done.1
  228.2 0.8 copy.27
  229.0 0.0 copy-done
  229.0 0.8 copy.28
Async XLA Ops:
  221.6 6.6 %copy-start.1 = (f32[2,64,1024]{2,1,0:T(8,128)S(1)}, f32[2,64,1024]{2,1,0:T(8,128)}, u32[]{:S(2)}) copy-start(f32[2,64,1024]{2,1,0:T(8,128)} %get-tuple-element.22) | copy-start | bytes 1572868
  221.6 7.3 %copy-start = (f32[2,64,1024]{2,1,0:T(8,128)S(1)}, f32[2,64,1024]{2,1,0:T(8,128)}, u32[]{:S(2)}) copy-start(f32[2,64,1024]{2,1,0:T(8,128)} %get-tuple-element.23) | copy-start | bytes 1572868

commit v5 on v4

--- a/solution.py
+++ b/solution.py
@@ -88,7 +88,7 @@
     total = running[SPAN - 1 :, :]
     tail = jnp.exp(total - running) * mask[:, 7:8]
     carry = jnp.exp(total) * mask[SPAN - 1 :, 6:7]
-    return step, log_decay, decays, reach, tail, carry
+    return step, running, decays, reach, tail, carry
 
 
 def layer_constants(con):
@@ -146,11 +146,18 @@
     dt = dot_nn(proj[:, 4 * HC :].astype(BF16), head_ones())
     vh[8:, :] = v
     z = conv_rows(vh, conv, mask)
-    act = z * sigmoid(z)
+    sz = sigmoid(z)
+    act = z * sz
     xc = act[:, :HC]
     b16 = act[:, HC : 2 * HC].astype(BF16)
     c16 = act[:, 2 * HC :].astype(BF16)
-    step, _, decays, reach, tail, carry = block_terms(dt, vec, mask, s.docr[b, 0:1, :])
+    step, running, decays, reach, tail, carry = block_terms(dt, vec, mask, s.docr[b, 0:1, :])
+    s.act[layer, rows, :] = act
+    s.dact[layer, rows, :] = sz * (1.0 + z * (1.0 - sz))
+    s.step[layer, rows, :] = step
+    s.run[layer, rows, :] = running
+    for h in (0, 1):
+        s.decay[layer, b, h] = decays[h]
     xs = xc * step
     xs16 = xs.astype(BF16)
     scores = dot_nt(c16, b16)
@@ -208,14 +215,17 @@
     dm = dm16.astype(F32)
     dgate = dg * mixed * (sg * (1.0 + gate * (1.0 - sg)))
 
-    z = conv_rows(vbuf, conv, mask)
-    sz = sigmoid(z)
-    act = z * sz
+    act = s.act[layer, rows_b, :]
     xc = act[:, :HC]
     b16 = act[:, HC : 2 * HC].astype(BF16)
     c16 = act[:, 2 * HC :].astype(BF16)
-    dt = s.dt[layer, rows_b, :]
-    step, log_decay, decays, reach, tail, carry = block_terms(dt, vec, mask, s.docr[b, 0:1, :])
+    step, running = s.step[layer, rows_b, :], s.run[layer, rows_b, :]
+    log_decay = -step * vec[1]
+    decays = [s.decay[layer, b, h] for h in (0, 1)]
+    total = running[SPAN - 1 :, :]
+    reach = jnp.exp(running) * mask[:, 6:7]
+    tail = jnp.exp(total - running) * mask[:, 7:8]
+    carry = jnp.exp(total) * mask[SPAN - 1 :, 6:7]
     xs16 = (xc * step).astype(BF16)
     xs = xs16.astype(F32)
     scores = dot_nt(c16, b16)
@@ -250,11 +260,11 @@
     d_log = exact_right(flow, same_head)
     d_step = exact_right(dxs_all * xc, same_head) - d_log * vec[1]
     d_alog = jnp.sum(d_log * log_decay, axis=0, keepdims=True)
-    d_dt = d_step * sigmoid(dt + vec[0])
+    d_dt = d_step * sigmoid(s.dt[layer, rows_b, :] + vec[0])
     d_skip = jnp.sum(dm * xc, axis=0, keepdims=True)
     d_xc = dm * vec[2] + dxs_all * step
 
-    dact = sz * (1.0 + z * (1.0 - sz))
+    dact = s.dact[layer, rows_b, :]
     dzbuf[:SPAN, 0:HC] = d_xc * dact[:, :HC]
     dzbuf[:SPAN, HC : 2 * HC] = db * dact[:, HC : 2 * HC]
     dzbuf[:SPAN, 2 * HC :] = dc * dact[:, 2 * HC :]
@@ -939,7 +949,11 @@
         "dt": ((2, length, HC), F32), "mix": ((2, length, HC), BF16),
         "scan": ((2, length, HC), F32), "st": ((2, blocks, NS, HC), F32),
         "state": ((NS, HC), F32), "dz": ((SPAN + 8, 3 * HC), F32),
-        "part": ((length, wide), BF16), "gin": ((WR, width), F32), "gout": ((HC, width), F32),
+        "part": ((length, wide), BF16),
+        "act": ((2, length, 3 * HC), F32), "dact": ((2, length, 3 * HC), F32),
+        "step": ((2, length, HC), F32), "run": ((2, length, HC), F32),
+        "decay": ((2, blocks, 2, SPAN, SPAN), F32),
+        "gin": ((WR, width), F32), "gout": ((HC, width), F32),
         "small": ((8, 4 * HC), F32),
         "u": ((rows, width), F32), "h": ((2, rows, width), F32), "branch": ((rows, width), F32),
         "r": ((rows, HC), F32), "g": ((2, rows, width), F32),
@@ -1190,7 +1204,8 @@
 
 
 def assemble_kernel(
-    inner, all_ref, pieces_ref, gin_ref, gout_ref, convw_ref, convb_ref, pre_ref, gain_ref, heads_ref
+    inner, all_ref, pieces_ref, gin_ref, gout_ref, convw_ref, convb_ref, pre_ref, gain_ref,
+    step_ref, alog_ref, skip_ref,
 ):
     count = all_ref.shape[0]
     lane = iota((1, HC), 1)
@@ -1232,10 +1247,11 @@
     convb_ref[:, inner:] = bc[4:5]
     for k in range(8):
         pre_ref[:, k * HC : (k + 1) * HC] = pre[k : k + 1]
-    heads_ref[...] = jnp.concatenate(per_head + [jnp.zeros((5, HC), F32)])
-
-
-def assemble(everyone, pieces, inner, columns, width, channels):
+    for ref, value in zip((step_ref, alog_ref, skip_ref), per_head):
+        ref[...] = value[:, : ref.shape[1]]
+
+
+def assemble(everyone, pieces, inner, columns, width, channels, heads):
     def shape(*dims):
         return jax.ShapeDtypeStruct(dims, F32)
 
@@ -1243,10 +1259,10 @@
     return pl.pallas_call(
         lambda *refs: assemble_kernel(inner, *refs),
         in_specs=[vmem] * 2,
-        out_specs=[vmem] * 7,
+        out_specs=[vmem] * 9,
         out_shape=[
             shape(columns, 256), shape(512, width), shape(4, channels), shape(1, channels),
-            shape(1, width), shape(1, inner), shape(8, HC),
+            shape(1, width), shape(1, inner), *[shape(1, heads)] * 3,
         ],
         compiler_params=pltpu.CompilerParams(vmem_limit_bytes=VMEM_ASK),
         name="assemble",
@@ -1266,13 +1282,13 @@
     )
     everyone = everyone.reshape(-1, END_ROWS, 256)
     pieces = pieces.reshape(-1, HC, 256)
-    gin, gout, convw, convb, pre, gain, per_head = assemble(
-        everyone, pieces, inner, in_proj.shape[2], width, conv_weight.shape[2]
+    gin, gout, convw, convb, pre, gain, step, alog, skip = assemble(
+        everyone, pieces, inner, in_proj.shape[2], width, conv_weight.shape[2], heads
     )
     return (
         hidden[None, :, None], input_grads[None, :, None],
         jnp.swapaxes(gin, 0, 1)[None], gout[None], convw[None], convb,
-        per_head[0:1, :heads], per_head[1:2, :heads], per_head[2:3, :heads], pre, gain,
+        step, alog, skip, pre, gain,
     )
 
 

time: 230 us -> 223 us (0.970)
  Pallas kernels: 226 us -> 221 us
    pallas_call x1, Pallas kernels: 221 us -> 215 us  [layers(): pl.pallas_call(lambda *refs: layers_kernel(inner, list(shapes), *refs), g...]
where the time goes in v5:
time: 223 us
  Pallas kernels  221 us (99%)
    pallas_call x1, Pallas kernels, layers(): pl.pallas_call(lambda *refs: layers_kernel(inner, list(shapes), *refs), g...  215 us
    pallas_call x1, Pallas kernels, assemble(): pl.pallas_call(lambda *refs: assemble_kernel(inner, *refs), in_specs=[vme...  5.23 us

profile of v5, /device:TPU:0, one launch (start us, length us, event | category | flops | bytes accessed | tf_op | source)
XLA Modules:
  0.0 223.0 jit_solution(13901027872964757773)
XLA Ops:
  0.6 215.5 %layers.1 = (f32[2,64,1024]{2,1,0:T(8,128)}, f32[2,64,1024]{2,1,0:T(8,128)}, bf16[5120,256]{1,0:T(8,128)(2,1)}, bf16[2048,256]{1,0:T(8,128)(2,1)}) custom-call(bf16[2,1,64,1024]{3,2,1,0:T(8,128)(2,1)} %refs_0_.1, bf16[2,1,64,1024]{3,2,1,0:T(8,128)(2,1)} %refs_1_.1, bf16[4384,256]{1,0:T(8,128)(2,1)} %bitcast.17, bf16[1,512,1024]{2,1,0:T(8,128)(2,1)} %refs_3_.1, ...), custom_call_target="tpu_custom_call" | custom-call | tf_op jit(solution)/shard_map/layers/pallas_call | solution.py:1184
  216.1 0.0 copy-start.1
  216.1 0.0 copy-start
  216.1 5.2 %assemble.1 = (f32[4384,256]{1,0:T(8,128)}, f32[512,1024]{1,0:T(8,128)}, f32[4,2304]{1,0:T(4,128)}, f32[1,2304]{1,0:T(1,128)}, f32[1,1024]{1,0:T(1,128)}, /*inde...) custom-call(bf16[16,320,256]{2,1,0:T(8,128)(2,1)} %bitcast.16, bf16[16,128,256]{2,1,0:T(8,128)(2,1)} %bitcast.18), custom_call_target="tpu_custom_call" | custom-call | tf_op jit(solution)/shard_map/assemble/pallas_call | solution.py:1259
  221.4 0.0 copy-done.1
  221.4 0.8 copy.27
  222.2 0.0 copy-done
  222.2 0.8 copy.28
Async XLA Ops:
  216.1 5.2 %copy-start.1 = (f32[2,64,1024]{2,1,0:T(8,128)S(1)}, f32[2,64,1024]{2,1,0:T(8,128)}, u32[]{:S(2)}) copy-start(f32[2,64,1024]{2,1,0:T(8,128)} %get-tuple-element.24) | copy-start | bytes 1572868
  216.1 6.0 %copy-start = (f32[2,64,1024]{2,1,0:T(8,128)S(1)}, f32[2,64,1024]{2,1,0:T(8,128)}, u32[]{:S(2)}) copy-start(f32[2,64,1024]{2,1,0:T(8,128)} %get-tuple-element.25) | copy-start | bytes 1572868

commit v6 on v5

--- a/solution.py
+++ b/solution.py
@@ -1025,6 +1025,8 @@
         u = s.x_in[...].astype(F32)
         s.u[...] = u
         normed = norm_rows(u)
+        copies[12].wait()
+        run(mask_steps(s.doc_in, s.mask, s.docr))
         greeted(len(targets) + (z != y).astype(jnp.int32))
         out, planes = Sender(*sems_of[0]), Sender(*sems_of[1])
         planes.go("con", s.cons.at[part], s.cons.at[part], other_core())
@@ -1041,12 +1043,7 @@
             weights = weights_steps(0, wo_ref, s, planes, own)
             next(weights)
             yield
-            for copy in copies[12:]:
-                copy.wait()
-            masks = mask_steps(s.doc_in, s.mask, s.docr)
-            next(masks)
-            yield
-            yield from masks
+            copies[13].wait()
             yield from weights
 
         planes.arrived("con")

time: 223 us -> 224 us (level)
  no operation moved by 1% of the time
where the time goes in v6:
time: 224 us
  Pallas kernels  221 us (99%)
    pallas_call x1, Pallas kernels, layers(): pl.pallas_call(lambda *refs: layers_kernel(inner, list(shapes), *refs), g...  216 us
    pallas_call x1, Pallas kernels, assemble(): pl.pallas_call(lambda *refs: assemble_kernel(inner, *refs), in_specs=[vme...  5.23 us

profile of v6, /device:TPU:0, one launch (start us, length us, event | category | flops | bytes accessed | tf_op | source)
XLA Modules:
  0.0 223.6 jit_solution(3006560454315138154)
XLA Ops:
  0.6 216.1 %layers.1 = (f32[2,64,1024]{2,1,0:T(8,128)}, f32[2,64,1024]{2,1,0:T(8,128)}, bf16[5120,256]{1,0:T(8,128)(2,1)}, bf16[2048,256]{1,0:T(8,128)(2,1)}) custom-call(bf16[2,1,64,1024]{3,2,1,0:T(8,128)(2,1)} %refs_0_.1, bf16[2,1,64,1024]{3,2,1,0:T(8,128)(2,1)} %refs_1_.1, bf16[4384,256]{1,0:T(8,128)(2,1)} %bitcast.17, bf16[1,512,1024]{2,1,0:T(8,128)(2,1)} %refs_3_.1, ...), custom_call_target="tpu_custom_call" | custom-call | tf_op jit(solution)/shard_map/layers/pallas_call | solution.py:1181
  216.8 0.0 copy-start.1
  216.8 0.0 copy-start
  216.8 5.2 %assemble.1 = (f32[4384,256]{1,0:T(8,128)}, f32[512,1024]{1,0:T(8,128)}, f32[4,2304]{1,0:T(4,128)}, f32[1,2304]{1,0:T(1,128)}, f32[1,1024]{1,0:T(1,128)}, /*inde...) custom-call(bf16[16,320,256]{2,1,0:T(8,128)(2,1)} %bitcast.16, bf16[16,128,256]{2,1,0:T(8,128)(2,1)} %bitcast.18), custom_call_target="tpu_custom_call" | custom-call | tf_op jit(solution)/shard_map/assemble/pallas_call | solution.py:1256
  222.0 0.0 copy-done.1
  222.0 0.8 copy.27
  222.8 0.0 copy-done
  222.8 0.8 copy.28
Async XLA Ops:
  216.8 5.2 %copy-start.1 = (f32[2,64,1024]{2,1,0:T(8,128)S(1)}, f32[2,64,1024]{2,1,0:T(8,128)}, u32[]{:S(2)}) copy-start(f32[2,64,1024]{2,1,0:T(8,128)} %get-tuple-element.24) | copy-start | bytes 1572868
  216.8 6.0 %copy-start = (f32[2,64,1024]{2,1,0:T(8,128)S(1)}, f32[2,64,1024]{2,1,0:T(8,128)}, u32[]{:S(2)}) copy-start(f32[2,64,1024]{2,1,0:T(8,128)} %get-tuple-element.25) | copy-start | bytes 1572868
